TPU v7x, 32 devices: a whole 2x2x4 slice. The times are simulated.
32 devices in a mesh: dp: 4 (over x, core), context: 8 (over z, y).
Axes of the slice: x: 2, y: 2, z: 4, core: 2. Of those that a mesh axis runs over, the one named last changes fastest.
Arguments:
- inputs: bfloat16 [4, 4096, 1024], P('dp', 'context'), may hold values from -6 to 6
- step_size: float32 [4, 4096], P('dp', 'context'), may hold values from 0.25 to 4099
- decay_rate: float32 [256], replicated, may hold values from 4.8828125e-05 to 0.125
- frequency: float32 [256], replicated, may hold values from -0.5 to 0.5
- input_proj: bfloat16 [1024, 512], replicated, may hold values from -0.1875 to 0.1875
- output_proj: bfloat16 [1024, 512], replicated, may hold values from -0.25 to 0.25
- skip_gain: float32 [1024], replicated, may hold values from 0.25 to 1.75
- cotangent: bfloat16 [4, 4096, 1024], P('dp', 'context'), may hold values from -6 to 6
Outputs:
- outputs: bfloat16 [4, 4096, 1024], P('dp', 'context')
- input_grad: bfloat16 [4, 4096, 1024], P('dp', 'context')
- input_proj_grad: float32 [1024, 512], P('context')
- output_proj_grad: float32 [1024, 512], P('context')
All inputs are finite; a program needn't handle non-finite values.
Results may differ from a plain program's by a relative error of at most 0.0036.
Values sent between devices are 32-bit elements; how exact they have to be, the bound alone decides.
No kernel may reach another device: no remote copies, remote signals or barrier semaphores. Data moves between devices by JAX's collectives and lax.ppermute only.
A program may use at most 64 MiB of HBM per device.

v0:
```python
import jax
import jax.numpy as jnp
from jax import lax
from jax.sharding import PartitionSpec as P


def complex_combine(earlier_pair, later_pair):
    early_are, early_aim, early_bre, early_bim = earlier_pair
    later_are, later_aim, later_bre, later_bim = later_pair
    return (
        later_are * early_are - later_aim * early_aim,
        later_are * early_aim + later_aim * early_are,
        later_are * early_bre - later_aim * early_bim + later_bre,
        later_are * early_bim + later_aim * early_bre + later_bim,
    )


def on_device(
    inputs, step_size, decay_rate, frequency, input_proj, output_proj, skip_gain, cotangent
):
    batch_count, row_count, model_width = inputs.shape
    state_count = decay_rate.shape[0]
    damping = jnp.exp(-step_size[:, :, None] * decay_rate)
    phase_turn = step_size[:, :, None] * frequency
    lam_re = damping * jnp.cos(phase_turn)
    lam_im = damping * jnp.sin(phase_turn)
    norm_gain = jnp.sqrt(-jnp.expm1(-2.0 * decay_rate))
    pair_gain = jnp.concatenate([norm_gain, norm_gain])
    flat_in = inputs.reshape(batch_count * row_count, model_width)
    flat_cot = cotangent.reshape(batch_count * row_count, model_width)
    drive_term = (
        jnp.dot(flat_in, input_proj, preferred_element_type=jnp.float32).reshape(
            batch_count, row_count, 2 * state_count
        )
        * pair_gain
    )
    local_fwd = lax.associative_scan(
        complex_combine,
        (lam_re, lam_im, drive_term[..., :state_count], drive_term[..., state_count:]),
        axis=1,
    )
    fwd_summary = (
        local_fwd[0][:, -1],
        local_fwd[1][:, -1],
        local_fwd[2][:, -1],
        local_fwd[3][:, -1],
    )
    adjoint_drive = jnp.dot(flat_cot, output_proj, preferred_element_type=jnp.float32).reshape(
        batch_count, row_count, 2 * state_count
    )
    next_re = jnp.concatenate([lam_re[:, 1:], jnp.ones_like(lam_re[:, :1])], axis=1)
    next_im = jnp.concatenate([-lam_im[:, 1:], jnp.zeros_like(lam_im[:, :1])], axis=1)
    local_back = lax.associative_scan(
        complex_combine,
        (next_re, next_im, adjoint_drive[..., :state_count], adjoint_drive[..., state_count:]),
        axis=1,
        reverse=True,
    )
    first_re = lam_re[:, 0]
    first_im = -lam_im[:, 0]
    back_summary = (
        first_re * local_back[0][:, 0] - first_im * local_back[1][:, 0],
        first_re * local_back[1][:, 0] + first_im * local_back[0][:, 0],
        first_re * local_back[2][:, 0] - first_im * local_back[3][:, 0],
        first_re * local_back[3][:, 0] + first_im * local_back[2][:, 0],
    )
    stacked = jnp.stack(fwd_summary + back_summary)[None]
    everyone = lax.all_gather(stacked, "context", axis=0, tiled=True)
    device_count = lax.axis_size("context")
    position = lax.axis_index("context")
    fwd_incl = lax.associative_scan(
        complex_combine, tuple((everyone[:, slot_index] for slot_index in range(4))), axis=0
    )
    back_incl = lax.associative_scan(
        complex_combine,
        tuple((everyone[:, slot_index] for slot_index in range(4, 8))),
        axis=0,
        reverse=True,
    )
    lower = jnp.maximum(position - 1, 0)
    upper = jnp.minimum(position + 1, device_count - 1)
    has_lower = position > 0
    has_upper = position < device_count - 1
    carry_re = jnp.where(
        has_lower, lax.dynamic_index_in_dim(fwd_incl[2], lower, 0, keepdims=False), 0.0
    )
    carry_im = jnp.where(
        has_lower, lax.dynamic_index_in_dim(fwd_incl[3], lower, 0, keepdims=False), 0.0
    )
    inflow_re = jnp.where(
        has_upper, lax.dynamic_index_in_dim(back_incl[2], upper, 0, keepdims=False), 0.0
    )
    inflow_im = jnp.where(
        has_upper, lax.dynamic_index_in_dim(back_incl[3], upper, 0, keepdims=False), 0.0
    )
    state_re = local_fwd[2] + local_fwd[0] * carry_re[:, None] - local_fwd[1] * carry_im[:, None]
    state_im = local_fwd[3] + local_fwd[0] * carry_im[:, None] + local_fwd[1] * carry_re[:, None]
    back_re = (
        local_back[2] + local_back[0] * inflow_re[:, None] - local_back[1] * inflow_im[:, None]
    )
    back_im = (
        local_back[3] + local_back[0] * inflow_im[:, None] + local_back[1] * inflow_re[:, None]
    )
    last_contract = (((1,), (1,)), ((), ()))
    state_pairs = (
        jnp.concatenate([state_re, state_im], axis=-1)
        .astype(jnp.bfloat16)
        .reshape(batch_count * row_count, 2 * state_count)
    )
    mixed = lax.dot_general(
        state_pairs, output_proj, last_contract, preferred_element_type=jnp.float32
    ).reshape(batch_count, row_count, model_width)
    outputs = (mixed + skip_gain * inputs.astype(jnp.float32)).astype(jnp.bfloat16)
    adjoint_pairs = (
        (jnp.concatenate([back_re, back_im], axis=-1) * pair_gain)
        .astype(jnp.bfloat16)
        .reshape(batch_count * row_count, 2 * state_count)
    )
    back_in = lax.dot_general(
        adjoint_pairs, input_proj, last_contract, preferred_element_type=jnp.float32
    ).reshape(batch_count, row_count, model_width)
    input_grad = (back_in + skip_gain * cotangent.astype(jnp.float32)).astype(jnp.bfloat16)
    context_count = lax.axis_size("context")
    grad_scale = float(batch_count * row_count * lax.axis_size("dp") * context_count) ** (-0.5)
    token_contract = (((0,), (0,)), ((), ()))
    grad_in_part = lax.dot_general(
        flat_in, adjoint_pairs, token_contract, preferred_element_type=jnp.float32
    )
    grad_out_part = lax.dot_general(
        flat_cot, state_pairs, token_contract, preferred_element_type=jnp.float32
    )
    shares = lax.psum_scatter(
        jnp.concatenate([grad_in_part, grad_out_part], axis=1) * grad_scale,
        "context",
        scatter_dimension=0,
        tiled=True,
    )
    my_rows = lax.psum(shares, "dp")
    return (outputs, input_grad, my_rows[:, : 2 * state_count], my_rows[:, 2 * state_count :])


def solution(mesh):
    in_specs = (
        P("dp", "context", None),
        P("dp", "context"),
        P(),
        P(),
        P(),
        P(),
        P(),
        P("dp", "context", None),
    )
    out_specs = (
        P("dp", "context", None),
        P("dp", "context", None),
        P("context", None),
        P("context", None),
    )
    return jax.shard_map(
        on_device, mesh=mesh, in_specs=in_specs, out_specs=out_specs, check_vma=False
    )
```

profile of v0, /device:TPU:0, one launch (start us, length us, event | category | flops | bytes accessed | tf_op | source)
XLA Modules:
  0.0 499.2 jit_solution(15832531005890724060)
XLA Ops:
  8.7 2.7 fusion.8
  117.2 3.0 slice.1648
  121.6 3.0 slice.1651
  125.9 3.0 slice.1740
  197.1 2.2 pad.579
  214.0 2.3 pad.583
  233.2 2.6 pad.589
  237.4 2.6 pad.552
  272.2 2.2 multiply_add_fusion
  277.6 2.6 pad.626
  280.2 2.6 pad.625
  286.4 2.6 pad.661
  294.2 2.2 add.1295
  296.4 2.1 add.1293
  304.0 32.3 %all-gather = f32[64,1,256]{2,1,0:T(1,128)S(1)} all-gather(f32[8,1,256]{2,1,0:T(1,128)S(1)} %constant_dynamic-update-slice_fusion), channel_id=2, replica_groups=mesh['dp'=4,'context'=8] {'context'}, dimensions={0}, use_global_device_ids=true | all-gather | bytes 73728 | tf_op jit(solution)/shard_map/all_gather | solution.py:68
  336.9 4.9 rev.13
  341.8 4.7 rev.29
  346.5 4.8 rev.12
  351.3 4.7 rev.31
  362.2 2.5 maximum_multiply_fusion
  365.4 2.9 fusion
  368.3 85.9 %reduce-scatter.2.cloned.1.call-done = f32[128,1024]{0,1:T(8,128)} async-done(((f32[1024,1024]{0,1:T(8,128)}), f32[128,1024]{0,1:T(8,128)}) %reduce-scatter.2.cloned.1.call-update) | async-done | bytes 524304 | tf_op jit(solution)/shard_map/reduce_scatter | solution.py:132
  454.3 3.3 fusion.1
  457.6 32.1 %all-reduce.174.cloned.1.call-done = f32[128,1024]{0,1:T(8,128)} async-done(((f32[128,1024]{0,1:T(8,128)}), f32[128,1024]{0,1:T(8,128)}) %all-reduce.174.cloned.1.call-update) | async-done | bytes 524304 | tf_op jit(solution)/shard_map/psum | solution.py:138
  (909 shorter events, 268.3 us)
Async XLA Ops:
  7.2 21.0 %copy-start = (bf16[1024,512]{1,0:T(8,128)(2,1)S(1)}, bf16[1024,512]{1,0:T(8,128)(2,1)}, u32[]{:S(2)}) copy-start(bf16[1024,512]{1,0:T(8,128)(2,1)} %param.12) | copy-start | bytes 3145732
  7.2 447.1 %reduce-scatter.2.cloned.1.call-start = ((), (), s32[]{:S(2)}) async-start(), calls=%async_computation.1 | async-start | bytes 4718592 | tf_op jit(solution)/shard_map/reduce_scatter | solution.py:132
  55.4 51.1 %copy-start.43 = (bf16[1,512,1024]{2,1,0:T(8,128)(2,1)S(1)}, bf16[1,512,1024]{2,1,0:T(8,128)(2,1)}, u32[]{:S(2)}) copy-start(bf16[1,512,1024]{2,1,0:T(8,128)(2,1)} %param.15) | copy-start | bytes 3145732
  148.7 26.2 %copy-start.31 = (f32[1,255,256]{2,1,0:T(8,128)S(1)}, f32[1,255,256]{2,1,0:T(8,128)}, u32[]{:S(2)}) copy-start(f32[1,255,256]{2,1,0:T(8,128)} %slice.1643) | copy-start | bytes 783364
  150.0 26.4 %copy-start.32 = (f32[1,255,256]{2,1,0:T(8,128)S(1)}, f32[1,255,256]{2,1,0:T(8,128)}, u32[]{:S(2)}) copy-start(f32[1,255,256]{2,1,0:T(8,128)} %slice.1728) | copy-start | bytes 783364
  153.5 32.7 %copy-start.83 = (f32[1,7,256]{2,1,0:T(8,128)S(1)}, f32[1,7,256]{2,1,0:T(8,128)}, u32[]{:S(2)}) copy-start(f32[1,7,256]{2,1,0:T(8,128)} %slice.1520) | copy-start | bytes 21508
  153.6 32.7 %copy-start.84 = (f32[1,7,256]{2,1,0:T(8,128)S(1)}, f32[1,7,256]{2,1,0:T(8,128)}, u32[]{:S(2)}) copy-start(f32[1,7,256]{2,1,0:T(8,128)} %slice.1567) | copy-start | bytes 21508
  157.7 32.1 %copy-start.75 = (f32[1,15,256]{2,1,0:T(8,128)S(1)}, f32[1,15,256]{2,1,0:T(8,128)}, u32[]{:S(2)}) copy-start(f32[1,15,256]{2,1,0:T(8,128)} %slice.1573) | copy-start | bytes 46084
  157.7 32.1 %copy-start.76 = (f32[1,15,256]{2,1,0:T(8,128)S(1)}, f32[1,15,256]{2,1,0:T(8,128)}, u32[]{:S(2)}) copy-start(f32[1,15,256]{2,1,0:T(8,128)} %slice.1510) | copy-start | bytes 46084
  158.3 31.5 %copy-start.87 = (f32[1,15,256]{2,1,0:T(8,128)S(1)}, f32[1,15,256]{2,1,0:T(8,128)}, u32[]{:S(2)}) copy-start(f32[1,15,256]{2,1,0:T(8,128)} %slice.1581) | copy-start | bytes 46084
  158.3 31.5 %copy-start.88 = (f32[1,15,256]{2,1,0:T(8,128)S(1)}, f32[1,15,256]{2,1,0:T(8,128)}, u32[]{:S(2)}) copy-start(f32[1,15,256]{2,1,0:T(8,128)} %slice.1577) | copy-start | bytes 46084
  158.5 32.7 %copy-start.123 = (f32[1,1,256]{2,1,0:T(1,128)S(1)}, f32[1,1,256]{2,1,0:T(1,128)}, u32[]{:S(2)}) copy-start(f32[1,1,256]{2,1,0:T(1,128)} %slice.2020) | copy-start | bytes 3076
  158.5 32.8 %copy-start.122 = (f32[1,1,256]{2,1,0:T(1,128)S(1)}, f32[1,1,256]{2,1,0:T(1,128)}, u32[]{:S(2)}) copy-start(f32[1,1,256]{2,1,0:T(1,128)} %slice.1971) | copy-start | bytes 3076
  162.6 28.8 %copy-start.69 = (f32[1,31,256]{2,1,0:T(8,128)S(1)}, f32[1,31,256]{2,1,0:T(8,128)}, u32[]{:S(2)}) copy-start(f32[1,31,256]{2,1,0:T(8,128)} %slice.1500) | copy-start | bytes 95236
  162.6 28.8 %copy-start.70 = (f32[1,31,256]{2,1,0:T(8,128)S(1)}, f32[1,31,256]{2,1,0:T(8,128)}, u32[]{:S(2)}) copy-start(f32[1,31,256]{2,1,0:T(8,128)} %slice.1579) | copy-start | bytes 95236
  166.1 25.3 %copy-start.79 = (f32[1,31,256]{2,1,0:T(8,128)S(1)}, f32[1,31,256]{2,1,0:T(8,128)}, u32[]{:S(2)}) copy-start(f32[1,31,256]{2,1,0:T(8,128)} %slice.1583) | copy-start | bytes 95236
  166.1 25.4 %copy-start.80 = (f32[1,31,256]{2,1,0:T(8,128)S(1)}, f32[1,31,256]{2,1,0:T(8,128)}, u32[]{:S(2)}) copy-start(f32[1,31,256]{2,1,0:T(8,128)} %slice.1587) | copy-start | bytes 95236
  172.1 19.4 %copy-start.118 = (f32[1,1,256]{2,1,0:T(1,128)S(1)}, f32[1,1,256]{2,1,0:T(1,128)}, u32[]{:S(2)}) copy-start(f32[1,1,256]{2,1,0:T(1,128)} %slice.1935) | copy-start | bytes 3076
  336.9 19.9 %copy-start.10 = (f32[1,512,256]{2,1,0:T(8,128)S(1)}, f32[1,512,256]{2,1,0:T(8,128)}, u32[]{:S(2)}) copy-start(f32[1,512,256]{2,1,0:T(8,128)} %pad.590) | copy-start | bytes 1572868
  336.9 19.9 %copy-start.11 = (f32[1,512,256]{2,1,0:T(8,128)S(1)}, f32[1,512,256]{2,1,0:T(8,128)}, u32[]{:S(2)}) copy-start(f32[1,512,256]{2,1,0:T(8,128)} %pad.586) | copy-start | bytes 1572868
  336.9 19.9 %copy-start.12 = (f32[1,512,256]{2,1,0:T(8,128)S(1)}, f32[1,512,256]{2,1,0:T(8,128)}, u32[]{:S(2)}) copy-start(f32[1,512,256]{2,1,0:T(8,128)} %pad.588) | copy-start | bytes 1572868
  336.9 19.9 %copy-start.13 = (f32[1,512,256]{2,1,0:T(8,128)S(1)}, f32[1,512,256]{2,1,0:T(8,128)}, u32[]{:S(2)}) copy-start(f32[1,512,256]{2,1,0:T(8,128)} %pad.587) | copy-start | bytes 1572868
  364.7 89.6 %copy-start.22 = (bf16[512,256]{1,0:T(8,128)(2,1)S(1)}, bf16[512,256]{1,0:T(8,128)(2,1)}, u32[]{:S(2)}) copy-start(bf16[512,256]{1,0:T(8,128)(2,1)} %copy-done.21) | copy-start | bytes 786436
  364.7 124.9 %all-reduce.174.cloned.1.call-start = ((), (), s32[]{:S(2)}) async-start(), calls=%async_computation.2 | async-start | bytes 1048576 | tf_op jit(solution)/shard_map/psum | solution.py:138
  (115 other events, 837.1 us)
Sparse Core Ops, SparseCore 0:
  364.9 89.3 reduce-scatter.1
  456.7 32.8 all-reduce.173
where the time goes:
time: 504 us; the launch traced here: 499 us
  local copies, waits for them, and re-layouts  229 us (45%)
  waiting for transfers between devices  118 us (23%)
  other arithmetic  90.7 us (18%)
  blocking collectives  32.3 us (6%)
  between operations  17.1 us (3%)
  matrix products  11.5 us (2%)
    reduce_scatter x1, waiting for transfers between devices, on_device(): lax.psum_scatter(jnp.concatenate([grad_in_part, grad_out_part], axis=1) *...  85.9 us
    slice x122, local copies, waits for them, and re-layouts, on_device(): lax.associative_scan(complex_combine, (lam_re, lam_im, drive_term[..., :s...  74.7 us
    slice x132, local copies, waits for them, and re-layouts, on_device(): lax.associative_scan(complex_combine, (next_re, next_im, adjoint_drive[.....  73.8 us
    all_gather x1, blocking collectives, on_device(): everyone = lax.all_gather(stacked, 'context', axis=0, tiled=True)  32.3 us
    psum x1, waiting for transfers between devices, on_device(): my_rows = lax.psum(shares, 'dp')  32.1 us
    pad x64, local copies, waits for them, and re-layouts, on_device(): lax.associative_scan(complex_combine, (lam_re, lam_im, drive_term[..., :s...  30.5 us
    pad x64, local copies, waits for them, and re-layouts, on_device(): lax.associative_scan(complex_combine, (next_re, next_im, adjoint_drive[.....  22.5 us
    rev x4, local copies, waits for them, and re-layouts, on_device(): lax.associative_scan(complex_combine, (next_re, next_im, adjoint_drive[.....  19.1 us
  transfers between devices with their start and end apart: 2, of which 2 were waited for; matrix products, arithmetic and copies ran while one was open for 1% of the time, Pallas kernels for 0%

commit v1 on v0

v1 whole, which is shorter than its diff:
```python
import functools

import jax
import jax.numpy as jnp
from jax import lax
from jax.experimental import pallas as pl
from jax.experimental.pallas import tpu as pltpu
from jax.sharding import PartitionSpec as P

CHUNKS = 8
LANES = 128
VMEM_LIMIT = 24 * 1024 * 1024

TWO_OVER_PI = 0.6366197723675814
PIO2_HIGH = 1.5703125
PIO2_MID = 0.0004837512969970703
PIO2_LOW = 7.549789948768648e-08


def sin_cos(angle):
    quadrant_real = jnp.floor(angle * TWO_OVER_PI + 0.5)
    rest = angle - quadrant_real * PIO2_HIGH
    rest = rest - quadrant_real * PIO2_MID
    rest = rest - quadrant_real * PIO2_LOW
    square = rest * rest
    sine = rest + rest * square * (
        -1.6666654611e-1 + square * (8.3321608736e-3 + square * -1.9515295891e-4)
    )
    cosine = (
        1.0
        - 0.5 * square
        + square
        * square
        * (4.166664568298827e-2 + square * (-1.388731625493765e-3 + square * 2.443315711809948e-5))
    )
    quadrant = quadrant_real.astype(jnp.int32)
    swapped = (quadrant & 1) == 1
    sin_base = jnp.where(swapped, cosine, sine)
    cos_base = jnp.where(swapped, sine, cosine)
    sin_value = jnp.where((quadrant & 2) == 2, -sin_base, sin_base)
    cos_value = jnp.where(((quadrant + 1) & 2) == 2, -cos_base, cos_base)
    return sin_value, cos_value


def gain_of(decay):
    twice = 2.0 * decay
    series = 1.0 / 3628800.0
    for factorial in (362880.0, 40320.0, 5040.0, 720.0, 120.0, 24.0, 6.0, 2.0, 1.0):
        series = 1.0 / factorial - twice * series
    return jnp.sqrt(jnp.where(twice < 0.5, twice * series, 1.0 - jnp.exp(-twice)))


def local_scan_kernel(
    step_ref,
    decay_ref,
    frequency_ref,
    in_hbm,
    cot_hbm,
    in_proj_hbm,
    out_proj_hbm,
    fwd_re,
    fwd_im,
    fwd_are,
    fwd_aim,
    back_re,
    back_im,
    back_are,
    back_aim,
    chunk_ref,
    summary_ref,
    in_vmem,
    cot_vmem,
    in_proj_vmem,
    out_proj_vmem,
    lam_re,
    lam_im,
    drive,
    adjoint,
    sems,
):
    rows = in_vmem.shape[0]
    length = rows // CHUNKS
    states = decay_ref.shape[1]
    lanes = states // LANES
    loads = [
        pltpu.make_async_copy(source, target, sems.at[slot])
        for slot, (source, target) in enumerate(
            (
                (in_hbm, in_vmem),
                (in_proj_hbm, in_proj_vmem),
                (cot_hbm, cot_vmem),
                (out_proj_hbm, out_proj_vmem),
            )
        )
    ]
    for load in loads:
        load.start()
    decay = decay_ref[...]
    frequency = frequency_ref[...]
    gain = gain_of(decay)
    steps = step_ref[...]
    for place in range(length):
        here = jnp.broadcast_to(steps[:, place : place + 1], (CHUNKS, states))
        damping = jnp.exp(-here * decay)
        sine, cosine = sin_cos(here * frequency)
        lam_re[pl.ds(place * CHUNKS, CHUNKS), :] = damping * cosine
        lam_im[pl.ds(place * CHUNKS, CHUNKS), :] = damping * sine
    loads[0].wait()
    loads[1].wait()
    pair_gain = jnp.concatenate([gain, gain], axis=1)
    driven = (
        jnp.dot(in_vmem[...], in_proj_vmem[...], preferred_element_type=jnp.float32) * pair_gain
    )
    for lane in range(2 * lanes):
        drive[lane] = driven[:, lane * LANES : (lane + 1) * LANES]
    loads[2].wait()
    loads[3].wait()
    driven = jnp.dot(cot_vmem[...], out_proj_vmem[...], preferred_element_type=jnp.float32)
    for lane in range(2 * lanes):
        adjoint[lane] = driven[:, lane * LANES : (lane + 1) * LANES]

    def gather(ref, first, spread):
        return jnp.concatenate([ref[first + lane, spread, :] for lane in range(lanes)], axis=1)

    def scatter(ref, spread, value):
        for lane in range(lanes):
            ref[lane, spread, :] = value[:, lane * LANES : (lane + 1) * LANES]

    def body(place, carry):
        f_are, f_aim, f_re, f_im, b_are, b_aim, b_re, b_im = carry
        tile = pl.ds(pl.multiple_of(place * CHUNKS, CHUNKS), CHUNKS)
        spread = pl.ds(place, CHUNKS, stride=length)
        l_re, l_im = lam_re[tile, :], lam_im[tile, :]
        new_are = l_re * f_are - l_im * f_aim
        new_aim = l_re * f_aim + l_im * f_are
        new_re = l_re * f_re - l_im * f_im + gather(drive, 0, spread)
        new_im = l_re * f_im + l_im * f_re + gather(drive, lanes, spread)
        scatter(fwd_are, spread, new_are)
        scatter(fwd_aim, spread, new_aim)
        scatter(fwd_re, spread, new_re)
        scatter(fwd_im, spread, new_im)
        mirror = length - 1 - place
        tile = pl.ds(pl.multiple_of(mirror * CHUNKS, CHUNKS), CHUNKS)
        spread = pl.ds(mirror, CHUNKS, stride=length)
        l_re, l_im = lam_re[tile, :], lam_im[tile, :]
        a_re = b_re + gather(adjoint, 0, spread)
        a_im = b_im + gather(adjoint, lanes, spread)
        scatter(back_are, spread, b_are)
        scatter(back_aim, spread, b_aim)
        scatter(back_re, spread, a_re)
        scatter(back_im, spread, a_im)
        next_are = l_re * b_are + l_im * b_aim
        next_aim = l_re * b_aim - l_im * b_are
        next_re = l_re * a_re + l_im * a_im
        next_im = l_re * a_im - l_im * a_re
        return (new_are, new_aim, new_re, new_im, next_are, next_aim, next_re, next_im)

    zero = jnp.zeros((CHUNKS, states), jnp.float32)
    one = jnp.ones((CHUNKS, states), jnp.float32)
    totals = lax.fori_loop(
        0, length, body, (one, zero, zero, zero, one, zero, zero, zero), unroll=4
    )
    a_re, a_im, f_re, f_im, _, _, b_re, b_im = totals
    for slot, part in enumerate((a_re, a_im, f_re, f_im, b_re, b_im)):
        chunk_ref[slot] = part
    row = lambda part, chunk: part[chunk : chunk + 1, :]
    t_are, t_aim = row(a_re, 0), row(a_im, 0)
    t_re, t_im = row(f_re, 0), row(f_im, 0)
    for chunk in range(1, CHUNKS):
        l_re, l_im = row(a_re, chunk), row(a_im, chunk)
        t_are, t_aim = l_re * t_are - l_im * t_aim, l_re * t_aim + l_im * t_are
        t_re, t_im = (
            l_re * t_re - l_im * t_im + row(f_re, chunk),
            l_re * t_im + l_im * t_re + row(f_im, chunk),
        )
    u_re, u_im = row(b_re, CHUNKS - 1), row(b_im, CHUNKS - 1)
    for chunk in range(CHUNKS - 2, -1, -1):
        l_re, l_im = row(a_re, chunk), row(a_im, chunk)
        u_re, u_im = (
            l_re * u_re + l_im * u_im + row(b_re, chunk),
            l_re * u_im - l_im * u_re + row(b_im, chunk),
        )
    summary_ref[...] = jnp.concatenate(
        [t_are, t_aim, t_re, t_im, u_re, u_im, t_re, t_re], axis=0
    )


def local_scan(step_rows, decay, frequency, flat_in, flat_cot, input_proj, output_proj):
    rows = flat_in.shape[0]
    states = decay.shape[1]
    lanes = states // LANES
    plane = jax.ShapeDtypeStruct((lanes, rows, LANES), jnp.float32)
    vmem = pl.BlockSpec(memory_space=pltpu.VMEM)
    anywhere = pl.BlockSpec(memory_space=pl.ANY)
    return pl.pallas_call(
        local_scan_kernel,
        out_shape=[plane] * 8
        + [
            jax.ShapeDtypeStruct((6, CHUNKS, states), jnp.float32),
            jax.ShapeDtypeStruct((8, states), jnp.float32),
        ],
        in_specs=[vmem] * 3 + [anywhere] * 4,
        out_specs=[vmem] * 10,
        scratch_shapes=[
            pltpu.VMEM(flat_in.shape, flat_in.dtype),
            pltpu.VMEM(flat_cot.shape, flat_cot.dtype),
            pltpu.VMEM(input_proj.shape, input_proj.dtype),
            pltpu.VMEM(output_proj.shape, output_proj.dtype),
            pltpu.VMEM((rows, states), jnp.float32),
            pltpu.VMEM((rows, states), jnp.float32),
            pltpu.VMEM((2 * lanes, rows, LANES), jnp.float32),
            pltpu.VMEM((2 * lanes, rows, LANES), jnp.float32),
            pltpu.SemaphoreType.DMA((4,)),
        ],
        compiler_params=pltpu.CompilerParams(vmem_limit_bytes=VMEM_LIMIT),
        cost_estimate=pl.CostEstimate(
            flops=4 * rows * flat_in.shape[1] * 2 * states,
            bytes_accessed=4 * 2**20,
            transcendentals=rows * states,
        ),
        name="local_scan",
    )(step_rows, decay, frequency, flat_in, flat_cot, input_proj, output_proj)


def states_kernel(
    device_count,
    where_ref,
    decay_ref,
    chunk_ref,
    fwd_re,
    fwd_im,
    fwd_are,
    fwd_aim,
    back_re,
    back_im,
    back_are,
    back_aim,
    *rest,
):
    summaries = rest[:device_count]
    in_ref, cot_ref, state_ref, adjoint_ref, grad_ref, everyone = rest[device_count:]
    lanes, rows, _ = fwd_re.shape
    states = lanes * LANES
    length = rows // CHUNKS
    whole = lambda ref, part: jnp.concatenate([ref[lane, part, :] for lane in range(lanes)], axis=1)
    for slot, summary in enumerate(summaries):
        everyone[slot] = summary[...]
    me = where_ref[0]
    gain = gain_of(decay_ref[...])
    f_re = jnp.zeros((1, states), jnp.float32)
    f_im, b_re, b_im = f_re, f_re, f_re
    for device in range(device_count - 1):
        entry = everyone[me ^ device]
        l_re, l_im, d_re, d_im = entry[0:1], entry[1:2], entry[2:3], entry[3:4]
        before = device < me
        f_re, f_im = (
            jnp.where(before, l_re * f_re - l_im * f_im + d_re, f_re),
            jnp.where(before, l_re * f_im + l_im * f_re + d_im, f_im),
        )
    for device in range(device_count - 1, 0, -1):
        entry = everyone[me ^ device]
        l_re, l_im, d_re, d_im = entry[0:1], entry[1:2], entry[4:5], entry[5:6]
        after = device > me
        b_re, b_im = (
            jnp.where(after, l_re * b_re + l_im * b_im + d_re, b_re),
            jnp.where(after, l_re * b_im - l_im * b_re + d_im, b_im),
        )
    for chunk in range(CHUNKS):
        part = pl.ds(chunk * length, length)
        a_re, a_im = whole(fwd_are, part), whole(fwd_aim, part)
        state_ref[part, pl.ds(0, states)] = (whole(fwd_re, part) + a_re * f_re - a_im * f_im).astype(
            jnp.bfloat16
        )
        state_ref[part, pl.ds(states, states)] = (
            whole(fwd_im, part) + a_re * f_im + a_im * f_re
        ).astype(jnp.bfloat16)
        l_re, l_im = chunk_ref[0, chunk : chunk + 1, :], chunk_ref[1, chunk : chunk + 1, :]
        f_re, f_im = (
            l_re * f_re - l_im * f_im + chunk_ref[2, chunk : chunk + 1, :],
            l_re * f_im + l_im * f_re + chunk_ref[3, chunk : chunk + 1, :],
        )
    for chunk in range(CHUNKS - 1, -1, -1):
        part = pl.ds(chunk * length, length)
        a_re, a_im = whole(back_are, part), whole(back_aim, part)
        adjoint_ref[part, pl.ds(0, states)] = (
            (whole(back_re, part) + a_re * b_re - a_im * b_im) * gain
        ).astype(jnp.bfloat16)
        adjoint_ref[part, pl.ds(states, states)] = (
            (whole(back_im, part) + a_re * b_im + a_im * b_re) * gain
        ).astype(jnp.bfloat16)
        l_re, l_im = chunk_ref[0, chunk : chunk + 1, :], chunk_ref[1, chunk : chunk + 1, :]
        b_re, b_im = (
            l_re * b_re + l_im * b_im + chunk_ref[4, chunk : chunk + 1, :],
            l_re * b_im - l_im * b_re + chunk_ref[5, chunk : chunk + 1, :],
        )
    over_rows = (((0,), (0,)), ((), ()))

    @pl.when(where_ref[1] == 0)
    def _():
        grad_ref[...] = lax.dot_general(
            cot_ref[...], state_ref[...], over_rows, preferred_element_type=jnp.float32
        )

    @pl.when(where_ref[1] != 0)
    def _():
        grad_ref[...] = lax.dot_general(
            in_ref[...], adjoint_ref[...], over_rows, preferred_element_type=jnp.float32
        )


def global_states(where, decay, chunk_totals, planes, summaries, flat_in, flat_cot):
    rows, width = flat_in.shape
    states = decay.shape[1]
    vmem = pl.BlockSpec(memory_space=pltpu.VMEM)
    return pl.pallas_call(
        functools.partial(states_kernel, len(summaries)),
        out_shape=[
            jax.ShapeDtypeStruct((rows, 2 * states), jnp.bfloat16),
            jax.ShapeDtypeStruct((rows, 2 * states), jnp.bfloat16),
            jax.ShapeDtypeStruct((width, 2 * states), jnp.float32),
        ],
        in_specs=[pl.BlockSpec(memory_space=pltpu.SMEM)] + [vmem] * (12 + len(summaries)),
        out_specs=[vmem] * 3,
        scratch_shapes=[pltpu.VMEM((len(summaries), 8, states), jnp.float32)],
        compiler_params=pltpu.CompilerParams(vmem_limit_bytes=VMEM_LIMIT),
        cost_estimate=pl.CostEstimate(
            flops=2 * rows * width * 2 * states, bytes_accessed=9 * 2**20, transcendentals=0
        ),
        name="global_states",
    )(where, decay, chunk_totals, *planes, *summaries, flat_in, flat_cot)


def own_grad_kernel(where_ref, in_ref, cot_ref, state_ref, adjoint_ref, grad_ref):
    over_rows = (((0,), (0,)), ((), ()))

    @pl.when(where_ref[1] == 0)
    def _():
        grad_ref[...] = lax.dot_general(
            in_ref[...], adjoint_ref[...], over_rows, preferred_element_type=jnp.float32
        )

    @pl.when(where_ref[1] != 0)
    def _():
        grad_ref[...] = lax.dot_general(
            cot_ref[...], state_ref[...], over_rows, preferred_element_type=jnp.float32
        )


def own_grad(where, flat_in, flat_cot, state_pairs, adjoint_pairs):
    rows, width = flat_in.shape
    vmem = pl.BlockSpec(memory_space=pltpu.VMEM)
    return pl.pallas_call(
        own_grad_kernel,
        out_shape=jax.ShapeDtypeStruct((width, state_pairs.shape[1]), jnp.float32),
        in_specs=[pl.BlockSpec(memory_space=pltpu.SMEM)] + [vmem] * 4,
        out_specs=vmem,
        compiler_params=pltpu.CompilerParams(vmem_limit_bytes=VMEM_LIMIT),
        cost_estimate=pl.CostEstimate(
            flops=2 * rows * width * state_pairs.shape[1],
            bytes_accessed=5 * 2**20,
            transcendentals=0,
        ),
        name="own_grad",
    )(where, flat_in, flat_cot, state_pairs, adjoint_pairs)


def mix_kernel(pair_ref, proj_ref, gain_ref, skip_ref, out_ref):
    mixed = lax.dot_general(
        pair_ref[...],
        proj_ref[...],
        (((1,), (1,)), ((), ())),
        preferred_element_type=jnp.float32,
    )
    out_ref[...] = (mixed + gain_ref[...] * skip_ref[...].astype(jnp.float32)).astype(jnp.bfloat16)


def mix(pairs, proj, skip_gain, skipped):
    rows, width = skipped.shape
    vmem = pl.BlockSpec(memory_space=pltpu.VMEM)
    return pl.pallas_call(
        mix_kernel,
        out_shape=jax.ShapeDtypeStruct(skipped.shape, jnp.bfloat16),
        in_specs=[vmem] * 4,
        out_specs=vmem,
        compiler_params=pltpu.CompilerParams(vmem_limit_bytes=VMEM_LIMIT),
        cost_estimate=pl.CostEstimate(
            flops=2 * rows * width * pairs.shape[1], bytes_accessed=4 * 2**20, transcendentals=0
        ),
        name="mix",
    )(pairs, proj, skip_gain, skipped)


def on_device(
    inputs, step_size, decay_rate, frequency, input_proj, output_proj, skip_gain, cotangent
):
    batch_count, row_count, model_width = inputs.shape
    state_count = decay_rate.shape[0]
    dp_count, context_count = lax.axis_size("dp"), lax.axis_size("context")
    dp_bits, context_bits = dp_count.bit_length() - 1, context_count.bit_length() - 1
    dp_place, context_place = lax.axis_index("dp"), lax.axis_index("context")
    core = dp_place & 1

    def swap(array, axis, bit):
        count = dp_count if axis == "dp" else context_count
        return lax.ppermute(array, axis, [(place, place ^ (1 << bit)) for place in range(count)])

    flat_in = inputs.reshape(row_count, model_width)
    flat_cot = cotangent.reshape(row_count, model_width)
    decay = decay_rate.reshape(1, state_count)
    where = jnp.stack([context_place, core]).astype(jnp.int32)
    *planes, chunk_totals, summary = local_scan(
        step_size.reshape(CHUNKS, row_count // CHUNKS),
        decay,
        frequency.reshape(1, state_count),
        flat_in,
        flat_cot,
        input_proj,
        output_proj,
    )
    summaries = [summary]
    for bit in range(context_bits):
        summaries = summaries + [swap(entry, "context", bit) for entry in summaries]
    state_pairs, adjoint_pairs, lent = global_states(
        where, decay, chunk_totals, planes, summaries, flat_in, flat_cot
    )
    borrowed = swap(lent, "dp", 0)
    kept = own_grad(where, flat_in, flat_cot, state_pairs, adjoint_pairs)
    outputs = mix(state_pairs, output_proj, skip_gain.reshape(1, model_width), flat_in)
    input_grad = mix(adjoint_pairs, input_proj, skip_gain.reshape(1, model_width), flat_cot)

    piece = model_width // (context_count * dp_count // 2)
    bits = [("context", bit) for bit in reversed(range(context_bits))]
    bits += [("dp", bit) for bit in reversed(range(1, dp_bits))]
    half = state_count
    shape = [2] * len(bits) + [piece, half]
    parts = [
        (kept[:, cols : cols + half].reshape(shape), borrowed[:, cols : cols + half].reshape(shape))
        for cols in (0, half)
    ]

    def side(axis, bit, mine):
        place = dp_place if axis == "dp" else context_place
        own = (place >> bit) & 1
        return own if mine else 1 - own

    def halve(pair, left, axis, bit):
        at = left.index((axis, bit))
        pick = lambda array, mine: lax.dynamic_index_in_dim(
            array, side(axis, bit, mine), at, keepdims=False
        )
        away = swap(pick(pair[0], False) + pick(pair[1], False), axis, bit)
        return (pick(pair[0], True) + pick(pair[1], True), away)

    dp_order = [("dp", bit) for bit in range(1, dp_bits)]
    orders = [dp_order + [("context", 0)], [("context", 0)] + dp_order]
    left = [list(bits), list(bits)]
    for steps in zip(*orders):
        for stream, step in enumerate(steps):
            parts[stream] = halve(parts[stream], left[stream], *step)
            left[stream].remove(step)
    kept = jnp.concatenate([parts[0][0], parts[1][0]], axis=-1)
    borrowed = jnp.concatenate([parts[0][1], parts[1][1]], axis=-1)
    pair, rest = (kept, borrowed), left[0]
    for bit in range(1, context_bits):
        pair = halve(pair, rest, "context", bit)
        rest.remove(("context", bit))
    grad_scale = float(batch_count * row_count * dp_count * context_count) ** (-0.5)
    share = (pair[0] + pair[1]) * grad_scale
    for bit in range(1, dp_bits):
        other = swap(share, "dp", bit)
        own_first = side("dp", bit, True) == 0
        share = jnp.where(
            own_first, jnp.concatenate([share, other]), jnp.concatenate([other, share])
        )
    other = swap(share, "dp", 0)
    return (
        outputs.reshape(inputs.shape),
        input_grad.reshape(inputs.shape),
        jnp.where(core == 0, share, other),
        jnp.where(core == 0, other, share),
    )


def solution(mesh):
    in_specs = (
        P("dp", "context", None),
        P("dp", "context"),
        P(),
        P(),
        P(),
        P(),
        P(),
        P("dp", "context", None),
    )
    out_specs = (
        P("dp", "context", None),
        P("dp", "context", None),
        P("context", None),
        P("context", None),
    )
    return jax.shard_map(
        on_device, mesh=mesh, in_specs=in_specs, out_specs=out_specs, check_vma=False
    )
```

time: 504 us -> 115 us (0.23)
  local copies, waits for them, and re-layouts: 229 us -> 25.6 us
  other arithmetic: 90.7 us -> 10.2 us
  waiting for transfers between devices: 118 us -> 40.6 us
  blocking collectives: 32.3 us -> 0 us
  starting transfers between devices: 0.08 us -> 21.1 us
  between operations: 17.1 us -> 0.86 us
  Pallas kernels: 0 us -> 15.3 us
  matrix products: 11.5 us -> 0 us
    slice x267 -> x2, local copies, waits for them, and re-layouts: 150 us -> 1.81 us  [the longest x1 1.68 us: on_device(): borrowed[:, cols:cols + half].reshape(shape)]
    reduce_scatter x1 -> x0, waiting for transfers between devices: 85.9 us -> none  [on_device(): lax.psum_scatter(jnp.concatenate([grad_in_part, grad_out_part], axis=1) *...]
    pad x144 -> x0, local copies, waits for them, and re-layouts: 53.7 us -> none  [the longest x64 30.5 us: on_device(): lax.associative_scan(complex_combine, (lam_re, lam_im, drive_term[..., :s...]
    add x129 -> x6, other arithmetic: 49.2 us -> 4.66 us  [the longest x5 2.78 us: halve(): away = swap(pick(pair[0], False) + pick(pair[1], False), axis, bit)]
    ppermute x0 -> x16, waiting for transfers between devices: none -> 40.6 us  [swap(): lax.ppermute(array, axis, [(place, place ^ 1 << bit) for place in range(c...]
    all_gather x1 -> x0, blocking collectives: 32.3 us -> none  [on_device(): everyone = lax.all_gather(stacked, 'context', axis=0, tiled=True)]
    psum x1 -> x0, waiting for transfers between devices: 32.1 us -> none  [on_device(): my_rows = lax.psum(shares, 'dp')]
    concatenate x69 -> x0, other arithmetic: 26 us -> none  [the longest x30 16 us: on_device(): lax.associative_scan(complex_combine, (lam_re, lam_im, drive_term[..., :s...]
  transfers between devices with their start and end apart: 2 -> 16, of which waited for: 2 -> 11; matrix products, arithmetic and copies ran while one was open for 1% -> 2% of each run, Pallas kernels for 0% -> 4%
where the time goes in v1:
time: 115 us; the launch traced here: 114 us
  waiting for transfers between devices  40.6 us (35%)
  local copies, waits for them, and re-layouts  25.6 us (22%)
  starting transfers between devices  21.1 us (18%)
  Pallas kernels  15.3 us (13%)
  other arithmetic  10.2 us (9%)
    ppermute x16, waiting for transfers between devices, swap(): lax.ppermute(array, axis, [(place, place ^ 1 << bit) for place in range(c...  40.6 us
    unnamed x66, local copies, waits for them, and re-layouts  22.6 us
    ppermute x16, starting transfers between devices, swap(): lax.ppermute(array, axis, [(place, place ^ 1 << bit) for place in range(c...  21.1 us
    pallas_call x1, Pallas kernels, local_scan(): pl.pallas_call(local_scan_kernel, out_shape=[plane] * 8 + [jax.ShapeDtype...  7.38 us
    pallas_call x2, Pallas kernels, mix(): pl.pallas_call(mix_kernel, out_shape=jax.ShapeDtypeStruct(skipped.shape,...  3.45 us
    pallas_call x1, Pallas kernels, global_states(): pl.pallas_call(functools.partial(states_kernel, len(summaries)), out_shap...  3.15 us
    add x5, other arithmetic, halve(): away = swap(pick(pair[0], False) + pick(pair[1], False), axis, bit)  2.78 us
  transfers between devices with their start and end apart: 16, of which 11 were waited for; matrix products, arithmetic and copies ran while one was open for 2% of the time, Pallas kernels for 4%

profile of v1, /device:TPU:0, one launch (start us, length us, event | category | flops | bytes accessed | tf_op | source)
XLA Modules:
  0.0 113.6 jit_solution(5101635159350718532)
XLA Ops:
  8.8 7.4 %local_scan.1 = (f32[2,512,128]{2,1,0:T(8,128)S(1)}, f32[2,512,128]{2,1,0:T(8,128)S(1)}, f32[2,512,128]{2,1,0:T(8,128)S(1)}, f32[2,512,128]{2,1,0:T(8,128)S(1)},...) custom-call(f32[8,64]{1,0:T(8,128)S(1)} %reshape.64.step_ref, ...), custom_call_target="tpu_custom_call" | custom-call | flops 1073741824 | bytes 4194304 | tf_op jit(solution)/shard_map/local_scan/pallas_call | solution.py:195
  22.6 3.0 %collective-permute-start = (f32[8,256]{1,0:T(8,128)S(1)}, f32[8,256]{1,0:T(8,128)S(1)}, u32[]{:S(2)}, u32[]{:S(2)}) collective-permute-start(f32[8,256]{1,0:T(8,128)S(1)} %get-tuple-element.26.rest_0_), channel_id=1, source_target_pairs={{0,1},{1,0},{2,3},{3,2},{4,5},{5,4},{6,7},{7,6},{8,9},{9,8},{10,11... | collective-permute-start | bytes 24584 | tf_op jit(solution)/shard_map/ppermute | solution.py:405
  25.6 1.6 %collective-permute-start.1 = (f32[8,256]{1,0:T(8,128)S(1)}, f32[8,256]{1,0:T(8,128)S(1)}, u32[]{:S(2)}, u32[]{:S(2)}) collective-permute-start(f32[8,256]{1,0:T(8,128)S(1)} %get-tuple-element.26.rest_0_), channel_id=1, source_target_pairs={{0,2},{1,3},{2,0},{3,1},{4,6},{5,7},{6,4},{7,5},{8,10},{9,11},{10,... | collective-permute-start | bytes 24584 | tf_op jit(solution)/shard_map/ppermute | solution.py:405
  27.2 2.1 %collective-permute-start.2 = (f32[8,256]{1,0:T(8,128)S(1)}, f32[8,256]{1,0:T(8,128)S(1)}, u32[]{:S(2)}, u32[]{:S(2)}) collective-permute-start(f32[8,256]{1,0:T(8,128)S(1)} %collective-permute-done.rest_1_), channel_id=1, source_target_pairs={{0,2},{1,3},{2,0},{3,1},{4,6},{5,7},{6,4},{7,5},{8,10},{9,11},{10,... | collective-permute-start | bytes 24584 | tf_op jit(solution)/shard_map/ppermute | solution.py:405
  29.3 2.6 %collective-permute-start.3 = (f32[8,256]{1,0:T(8,128)S(1)}, f32[8,256]{1,0:T(8,128)S(1)}, u32[]{:S(2)}, u32[]{:S(2)}) collective-permute-start(f32[8,256]{1,0:T(8,128)S(1)} %get-tuple-element.26.rest_0_), channel_id=1, source_target_pairs={{0,4},{1,5},{2,6},{3,7},{4,0},{5,1},{6,2},{7,3},{8,12},{9,13},{10,... | collective-permute-start | bytes 24584 | tf_op jit(solution)/shard_map/ppermute | solution.py:405
  32.2 2.6 %collective-permute-start.5 = (f32[8,256]{1,0:T(8,128)S(1)}, f32[8,256]{1,0:T(8,128)S(1)}, u32[]{:S(2)}, u32[]{:S(2)}) collective-permute-start(f32[8,256]{1,0:T(8,128)S(1)} %collective-permute-done.1.rest_2_), channel_id=1, source_target_pairs={{0,4},{1,5},{2,6},{3,7},{4,0},{5,1},{6,2},{7,3},{8,12},{9,13},{10,... | collective-permute-start | bytes 24584 | tf_op jit(solution)/shard_map/ppermute | solution.py:405
  36.7 2.6 %collective-permute-done.6.rest_7_ = f32[8,256]{1,0:T(8,128)S(1)} collective-permute-done((f32[8,256]{1,0:T(8,128)S(1)}, f32[8,256]{1,0:T(8,128)S(1)}, u32[]{:S(2)}, u32[]{:S(2)}) %collective-permute-start.6) | collective-permute-done | bytes 8224 | tf_op jit(solution)/shard_map/ppermute | solution.py:405
  47.7 3.1 %global_states.1 = (bf16[512,512]{1,0:T(8,128)(2,1)S(1)}, bf16[512,512]{1,0:T(8,128)(2,1)S(1)}, f32[1024,512]{1,0:T(8,128)}) custom-call(s32[2]{0:T(128)S(1)} %pad_add_fusion.where_ref, f32[1,256]{1,0:T(1,128)S(1)} %bitcast.68, f32[6,8,256]{2,1,0:T(8,128)S(1)} %get-tuple-element.17.chunk_ref, f32[2,512,128]{2,1,0:T(8,128)S(1)} %copy-done.13, ...), custom_call_target="tpu_custom_call" | custom-call | flops 536870912 | bytes 9437184 | tf_op jit(solution)/shard_map/global_states/pallas_call | solution.py:315
  52.3 3.0 %collective-permute-done.7 = f32[1024,512]{1,0:T(8,128)} collective-permute-done((f32[1024,512]{1,0:T(8,128)}, f32[1024,512]{1,0:T(8,128)}, u32[]{:S(2)}, u32[]{:S(2)}) %collective-permute-start.7) | collective-permute-done | bytes 2097184 | tf_op jit(solution)/shard_map/ppermute | solution.py:405
  55.3 1.7 %fusion.14 = (f32[1024,256]{1,0:T(8,128)S(1)}, f32[1024,256]{1,0:T(8,128)S(1)}) fusion(f32[1024,512]{1,0:T(8,128)} %collective-permute-done.7), kind=kLoop, calls=%fused_computation.43 | loop fusion | bytes 4194304 | tf_op jit(solution)/shard_map/slice | solution.py:437
  57.3 1.6 %collective-permute-start.8 = (f32[2,2,2,64,256]{4,3,0,1,2:T(8,128)S(1)}, f32[2,2,2,64,256]{4,3,0,1,2:T(8,128)S(1)}, u32[]{:S(2)}, u32[]{:S(2)}) collective-permute-start(f32[2,2,2,64,256]{4,3,0,1,2:T(8,128)S(1)} %fusion.1), channel_id=1, source_target_pairs={{0,16},{8,24},{16,0},{24,8},{1,17},{9,25},{17,1},{25,9},{2,18},{10... | collective-permute-start | bytes 1572872 | tf_op jit(solution)/shard_map/ppermute | solution.py:405
  59.1 1.6 %collective-permute-start.9 = (f32[2,2,2,64,256]{4,3,0,1,2:T(8,128)S(1)}, f32[2,2,2,64,256]{4,3,0,1,2:T(8,128)S(1)}, u32[]{:S(2)}, u32[]{:S(2)}) collective-permute-start(f32[2,2,2,64,256]{4,3,0,1,2:T(8,128)S(1)} %fusion), channel_id=1, source_target_pairs={{0,1},{1,0},{2,3},{3,2},{4,5},{5,4},{6,7},{7,6},{8,9},{9,8},{10,11... | collective-permute-start | bytes 1572872 | tf_op jit(solution)/shard_map/ppermute | solution.py:405
  60.8 10.5 %collective-permute-done.8 = f32[2,2,2,64,256]{4,3,0,1,2:T(8,128)S(1)} collective-permute-done((f32[2,2,2,64,256]{4,3,0,1,2:T(8,128)S(1)}, f32[2,2,2,64,256]{4,3,0,1,2:T(8,128)S(1)}, u32[]{:S(2)}, u32[]{:S(2)}) %collective-permute-start.8) | collective-permute-done | bytes 524320 | tf_op jit(solution)/shard_map/ppermute | solution.py:405
  72.2 1.5 %collective-permute-start.10 = (f32[2,2,64,256]{3,2,0,1:T(8,128)}, f32[2,2,64,256]{3,2,0,1:T(8,128)S(1)}, u32[]{:S(2)}, u32[]{:S(2)}) collective-permute-start(f32[2,2,64,256]{3,2,0,1:T(8,128)} %get-tuple-element.48), channel_id=1, source_target_pairs={{0,1},{1,0},{2,3},{3,2},{4,5},{5,4},{6,7},{7,6},{8,9},{9,8},{10,11... | collective-permute-start | bytes 786440 | tf_op jit(solution)/shard_map/ppermute | solution.py:405
  76.0 3.9 %collective-permute-done.10 = f32[2,2,64,256]{3,2,0,1:T(8,128)S(1)} collective-permute-done((f32[2,2,64,256]{3,2,0,1:T(8,128)}, f32[2,2,64,256]{3,2,0,1:T(8,128)S(1)}, u32[]{:S(2)}, u32[]{:S(2)}) %collective-permute-start.10) | collective-permute-done | bytes 262176 | tf_op jit(solution)/shard_map/ppermute | solution.py:405
  79.9 2.2 %collective-permute-done.11 = f32[2,2,64,256]{3,2,0,1:T(8,128)} collective-permute-done((f32[2,2,64,256]{3,2,0,1:T(8,128)}, f32[2,2,64,256]{3,2,0,1:T(8,128)}, u32[]{:S(2)}, u32[]{:S(2)}) %collective-permute-start.11) | collective-permute-done | bytes 262176 | tf_op jit(solution)/shard_map/ppermute | solution.py:405
  83.1 1.9 %fusion.6 = (f32[2,1,64,512]{3,2,0,1:T(8,128)S(1)}, f32[2,64,512]{2,1,0:T(8,128)}) fusion(s32[]{:T(128)S(6)} %select_n.69, f32[2,2,64,256]{3,2,0,1:T(8,128)} %get-tuple-element.49, f32[2,2,64,256]{3,2,0,1:T(8,128)} %get-tuple-element.45, f32[2,2,64,512]{3,2,0,1:T(8,128)S(1)} %constant_dynamic-update-slice_fusion, s32[]{:T(128)S(6)} %select_n.71), kind=kLoop, calls=%fused_computation.14 | loop fusion | flops 262144 | bytes 1572872 | tf_op jit(solution)/shard_map/add | solution.py:452
  85.4 6.2 %collective-permute-done.12 = f32[2,64,512]{2,1,0:T(8,128)} collective-permute-done((f32[2,64,512]{2,1,0:T(8,128)}, f32[2,64,512]{2,1,0:T(8,128)}, u32[]{:S(2)}, u32[]{:S(2)}) %collective-permute-start.12) | collective-permute-done | bytes 262176 | tf_op jit(solution)/shard_map/ppermute | solution.py:405
  93.0 6.9 %collective-permute-done.13 = f32[64,512]{1,0:T(8,128)} collective-permute-done((f32[64,512]{1,0:T(8,128)S(1)}, f32[64,512]{1,0:T(8,128)}, u32[]{:S(2)}, u32[]{:S(2)}) %collective-permute-start.13) | collective-permute-done | bytes 131104 | tf_op jit(solution)/shard_map/ppermute | solution.py:405
  100.9 1.6 %collective-permute-start.14 = (f32[64,512]{1,0:T(8,128)S(1)}, f32[64,512]{1,0:T(8,128)}, u32[]{:S(2)}, u32[]{:S(2)}) collective-permute-start(f32[64,512]{1,0:T(8,128)S(1)} %fusion.12), channel_id=1, source_target_pairs={{0,16},{8,24},{16,0},{24,8},{1,17},{9,25},{17,1},{25,9},{2,18},{10... | collective-permute-start | bytes 393224 | tf_op jit(solution)/shard_map/ppermute | solution.py:405
  102.5 3.6 %collective-permute-done.14 = f32[64,512]{1,0:T(8,128)} collective-permute-done((f32[64,512]{1,0:T(8,128)S(1)}, f32[64,512]{1,0:T(8,128)}, u32[]{:S(2)}, u32[]{:S(2)}) %collective-permute-start.14) | collective-permute-done | bytes 131104 | tf_op jit(solution)/shard_map/ppermute | solution.py:405
  108.4 1.7 %mix.2 = bf16[512,1024]{1,0:T(8,128)(2,1)} custom-call(bf16[512,512]{1,0:T(8,128)(2,1)S(1)} %copy-done.11, bf16[1024,512]{1,0:T(8,128)(2,1)S(1)} %copy-done.5, f32[1,1024]{1,0:T(1,128)S(1)} %bitcast.65, bf16[512,1024]{1,0:T(8,128)(2,1)S(1)} %bitcast.60), custom_call_target="tpu_custom_call" | custom-call | flops 536870912 | bytes 4194304 | tf_op jit(solution)/shard_map/mix/pallas_call | solution.py:380
  110.1 1.7 %mix.3 = bf16[512,1024]{1,0:T(8,128)(2,1)} custom-call(bf16[512,512]{1,0:T(8,128)(2,1)S(1)} %copy-done.9, bf16[1024,512]{1,0:T(8,128)(2,1)S(1)} %copy-done.7, f32[1,1024]{1,0:T(1,128)S(1)} %bitcast.66, bf16[512,1024]{1,0:T(8,128)(2,1)S(1)} %bitcast.64), custom_call_target="tpu_custom_call" | custom-call | flops 536870912 | bytes 4194304 | tf_op jit(solution)/shard_map/mix/pallas_call | solution.py:380
  111.8 1.8 %broadcast_select_fusion = (f32[128,512]{1,0:T(8,128)}, f32[128,512]{1,0:T(8,128)}) fusion(f32[128,512]{1,0:T(8,128)} %collective-permute-done.15, f32[128,512]{1,0:T(8,128)S(1)} %maximum_select_fusion, pred[]{:T(512)S(6)} %eq.7), kind=kLoop, calls=%fused_computation.29 | loop fusion | flops 131072 | bytes 1048577 | tf_op jit(solution)/shard_map/jit(_where)/select_n | solution.py:480
  (98 shorter events, 36.4 us)
Async XLA Ops:
  8.8 30.5 %copy-start.1 = (bf16[1,512,1024]{2,1,0:T(8,128)(2,1)S(1)}, bf16[1,512,1024]{2,1,0:T(8,128)(2,1)}, u32[]{:S(2)}) copy-start(bf16[1,512,1024]{2,1,0:T(8,128)(2,1)} %param.8) | copy-start | bytes 3145732
  8.8 30.5 %copy-start.3 = (bf16[1,512,1024]{2,1,0:T(8,128)(2,1)S(1)}, bf16[1,512,1024]{2,1,0:T(8,128)(2,1)}, u32[]{:S(2)}) copy-start(bf16[1,512,1024]{2,1,0:T(8,128)(2,1)} %param.15) | copy-start | bytes 3145732
  8.8 30.5 %copy-start.30 = (f32[256]{0:T(256)S(1)}, f32[256]{0:T(256)}, u32[]{:S(2)}) copy-start(f32[256]{0:T(256)} %param.10) | copy-start | bytes 3076
  22.6 4.6 %collective-permute-start = (f32[8,256]{1,0:T(8,128)S(1)}, f32[8,256]{1,0:T(8,128)S(1)}, u32[]{:S(2)}, u32[]{:S(2)}) collective-permute-start(f32[8,256]{1,0:T(8,128)S(1)} %get-tuple-element.26.rest_0_), channel_id=1, source_target_pairs={{0,1},{1,0},{2,3},{3,2},{4,5},{5,4},{6,7},{7,6},{8,9},{9,8},{10,11... | collective-permute-start | bytes 24584 | tf_op jit(solution)/shard_map/ppermute | solution.py:405
  25.6 6.6 %collective-permute-start.1 = (f32[8,256]{1,0:T(8,128)S(1)}, f32[8,256]{1,0:T(8,128)S(1)}, u32[]{:S(2)}, u32[]{:S(2)}) collective-permute-start(f32[8,256]{1,0:T(8,128)S(1)} %get-tuple-element.26.rest_0_), channel_id=1, source_target_pairs={{0,2},{1,3},{2,0},{3,1},{4,6},{5,7},{6,4},{7,5},{8,10},{9,11},{10,... | collective-permute-start | bytes 24584 | tf_op jit(solution)/shard_map/ppermute | solution.py:405
  27.2 7.6 %collective-permute-start.2 = (f32[8,256]{1,0:T(8,128)S(1)}, f32[8,256]{1,0:T(8,128)S(1)}, u32[]{:S(2)}, u32[]{:S(2)}) collective-permute-start(f32[8,256]{1,0:T(8,128)S(1)} %collective-permute-done.rest_1_), channel_id=1, source_target_pairs={{0,2},{1,3},{2,0},{3,1},{4,6},{5,7},{6,4},{7,5},{8,10},{9,11},{10,... | collective-permute-start | bytes 24584 | tf_op jit(solution)/shard_map/ppermute | solution.py:405
  29.3 5.9 %collective-permute-start.3 = (f32[8,256]{1,0:T(8,128)S(1)}, f32[8,256]{1,0:T(8,128)S(1)}, u32[]{:S(2)}, u32[]{:S(2)}) collective-permute-start(f32[8,256]{1,0:T(8,128)S(1)} %get-tuple-element.26.rest_0_), channel_id=1, source_target_pairs={{0,4},{1,5},{2,6},{3,7},{4,0},{5,1},{6,2},{7,3},{8,12},{9,13},{10,... | collective-permute-start | bytes 24584 | tf_op jit(solution)/shard_map/ppermute | solution.py:405
  31.9 4.6 %collective-permute-start.4 = (f32[8,256]{1,0:T(8,128)S(1)}, f32[8,256]{1,0:T(8,128)S(1)}, u32[]{:S(2)}, u32[]{:S(2)}) collective-permute-start(f32[8,256]{1,0:T(8,128)S(1)} %collective-permute-done.rest_1_), channel_id=1, source_target_pairs={{0,4},{1,5},{2,6},{3,7},{4,0},{5,1},{6,2},{7,3},{8,12},{9,13},{10,... | collective-permute-start | bytes 24584 | tf_op jit(solution)/shard_map/ppermute | solution.py:405
  32.2 4.6 %collective-permute-start.5 = (f32[8,256]{1,0:T(8,128)S(1)}, f32[8,256]{1,0:T(8,128)S(1)}, u32[]{:S(2)}, u32[]{:S(2)}) collective-permute-start(f32[8,256]{1,0:T(8,128)S(1)} %collective-permute-done.1.rest_2_), channel_id=1, source_target_pairs={{0,4},{1,5},{2,6},{3,7},{4,0},{5,1},{6,2},{7,3},{8,12},{9,13},{10,... | collective-permute-start | bytes 24584 | tf_op jit(solution)/shard_map/ppermute | solution.py:405
  34.8 4.6 %collective-permute-start.6 = (f32[8,256]{1,0:T(8,128)S(1)}, f32[8,256]{1,0:T(8,128)S(1)}, u32[]{:S(2)}, u32[]{:S(2)}) collective-permute-start(f32[8,256]{1,0:T(8,128)S(1)} %collective-permute-done.2.rest_3_), channel_id=1, source_target_pairs={{0,4},{1,5},{2,6},{3,7},{4,0},{5,1},{6,2},{7,3},{8,12},{9,13},{10,... | collective-permute-start | bytes 24584 | tf_op jit(solution)/shard_map/ppermute | solution.py:405
  50.8 1.3 %copy-start.10 = (bf16[512,512]{1,0:T(8,128)(2,1)}, bf16[512,512]{1,0:T(8,128)(2,1)S(1)}, u32[]{:S(2)}) copy-start(bf16[512,512]{1,0:T(8,128)(2,1)S(1)} %get-tuple-element.27.pair_ref.state_ref) | copy-start | bytes 1572868
  50.8 4.5 %collective-permute-start.7 = (f32[1024,512]{1,0:T(8,128)}, f32[1024,512]{1,0:T(8,128)}, u32[]{:S(2)}, u32[]{:S(2)}) collective-permute-start(f32[1024,512]{1,0:T(8,128)} %get-tuple-element.29), channel_id=1, source_target_pairs={{0,8},{8,0},{16,24},{24,16},{1,9},{9,1},{17,25},{25,17},{2,10},{10... | collective-permute-start | bytes 6291464 | tf_op jit(solution)/shard_map/ppermute | solution.py:405
  57.3 14.0 %collective-permute-start.8 = (f32[2,2,2,64,256]{4,3,0,1,2:T(8,128)S(1)}, f32[2,2,2,64,256]{4,3,0,1,2:T(8,128)S(1)}, u32[]{:S(2)}, u32[]{:S(2)}) collective-permute-start(f32[2,2,2,64,256]{4,3,0,1,2:T(8,128)S(1)} %fusion.1), channel_id=1, source_target_pairs={{0,16},{8,24},{16,0},{24,8},{1,17},{9,25},{17,1},{25,9},{2,18},{10... | collective-permute-start | bytes 1572872 | tf_op jit(solution)/shard_map/ppermute | solution.py:405
  59.1 14.6 %collective-permute-start.9 = (f32[2,2,2,64,256]{4,3,0,1,2:T(8,128)S(1)}, f32[2,2,2,64,256]{4,3,0,1,2:T(8,128)S(1)}, u32[]{:S(2)}, u32[]{:S(2)}) collective-permute-start(f32[2,2,2,64,256]{4,3,0,1,2:T(8,128)S(1)} %fusion), channel_id=1, source_target_pairs={{0,1},{1,0},{2,3},{3,2},{4,5},{5,4},{6,7},{7,6},{8,9},{9,8},{10,11... | collective-permute-start | bytes 1572872 | tf_op jit(solution)/shard_map/ppermute | solution.py:405
  72.2 7.7 %collective-permute-start.10 = (f32[2,2,64,256]{3,2,0,1:T(8,128)}, f32[2,2,64,256]{3,2,0,1:T(8,128)S(1)}, u32[]{:S(2)}, u32[]{:S(2)}) collective-permute-start(f32[2,2,64,256]{3,2,0,1:T(8,128)} %get-tuple-element.48), channel_id=1, source_target_pairs={{0,1},{1,0},{2,3},{3,2},{4,5},{5,4},{6,7},{7,6},{8,9},{9,8},{10,11... | collective-permute-start | bytes 786440 | tf_op jit(solution)/shard_map/ppermute | solution.py:405
  74.5 32.6 %copy-start.5 = (bf16[1024,512]{1,0:T(8,128)(2,1)S(1)}, bf16[1024,512]{1,0:T(8,128)(2,1)}, u32[]{:S(2)}) copy-start(bf16[1024,512]{1,0:T(8,128)(2,1)} %proj_ref.2) | copy-start | bytes 3145732
  74.5 32.6 %copy-start.28 = (f32[1024]{0:T(1024)S(1)}, f32[1024]{0:T(1024)}, u32[]{:S(2)}) copy-start(f32[1024]{0:T(1024)} %param.14) | copy-start | bytes 12292
  74.6 7.6 %collective-permute-start.11 = (f32[2,2,64,256]{3,2,0,1:T(8,128)}, f32[2,2,64,256]{3,2,0,1:T(8,128)}, u32[]{:S(2)}, u32[]{:S(2)}) collective-permute-start(f32[2,2,64,256]{3,2,0,1:T(8,128)} %get-tuple-element.44), channel_id=1, source_target_pairs={{0,16},{8,24},{16,0},{24,8},{1,17},{9,25},{17,1},{25,9},{2,18},{10... | collective-permute-start | bytes 786440 | tf_op jit(solution)/shard_map/ppermute | solution.py:405
  85.0 6.7 %collective-permute-start.12 = (f32[2,64,512]{2,1,0:T(8,128)}, f32[2,64,512]{2,1,0:T(8,128)}, u32[]{:S(2)}, u32[]{:S(2)}) collective-permute-start(f32[2,64,512]{2,1,0:T(8,128)} %get-tuple-element.35), channel_id=1, source_target_pairs={{0,2},{1,3},{2,0},{3,1},{4,6},{5,7},{6,4},{7,5},{8,10},{9,11},{10,... | collective-permute-start | bytes 786440 | tf_op jit(solution)/shard_map/ppermute | solution.py:405
  92.6 7.3 %collective-permute-start.13 = (f32[64,512]{1,0:T(8,128)S(1)}, f32[64,512]{1,0:T(8,128)}, u32[]{:S(2)}, u32[]{:S(2)}) collective-permute-start(f32[64,512]{1,0:T(8,128)S(1)} %fusion.11), channel_id=1, source_target_pairs={{0,4},{1,5},{2,6},{3,7},{4,0},{5,1},{6,2},{7,3},{8,12},{9,13},{10,... | collective-permute-start | bytes 393224 | tf_op jit(solution)/shard_map/ppermute | solution.py:405
  100.9 5.1 %collective-permute-start.14 = (f32[64,512]{1,0:T(8,128)S(1)}, f32[64,512]{1,0:T(8,128)}, u32[]{:S(2)}, u32[]{:S(2)}) collective-permute-start(f32[64,512]{1,0:T(8,128)S(1)} %fusion.12), channel_id=1, source_target_pairs={{0,16},{8,24},{16,0},{24,8},{1,17},{9,25},{17,1},{25,9},{2,18},{10... | collective-permute-start | bytes 393224 | tf_op jit(solution)/shard_map/ppermute | solution.py:405
  107.1 4.7 %collective-permute-start.15 = (f32[128,512]{1,0:T(8,128)S(1)}, f32[128,512]{1,0:T(8,128)}, u32[]{:S(2)}, u32[]{:S(2)}) collective-permute-start(f32[128,512]{1,0:T(8,128)S(1)} %maximum_select_fusion), channel_id=1, source_target_pairs={{0,8},{8,0},{16,24},{24,16},{1,9},{9,1},{17,25},{25,17},{2,10},{10... | collective-permute-start | bytes 786440 | tf_op jit(solution)/shard_map/ppermute | solution.py:405
  107.2 2.9 %copy-start.7 = (bf16[1024,512]{1,0:T(8,128)(2,1)S(1)}, bf16[1024,512]{1,0:T(8,128)(2,1)}, u32[]{:S(2)}) copy-start(bf16[1024,512]{1,0:T(8,128)(2,1)} %proj_ref.3) | copy-start | bytes 3145732
  107.2 2.9 %copy-start.9 = (bf16[512,512]{1,0:T(8,128)(2,1)S(1)}, bf16[512,512]{1,0:T(8,128)(2,1)}, u32[]{:S(2)}) copy-start(bf16[512,512]{1,0:T(8,128)(2,1)} %copy-done.8) | copy-start | bytes 1572868
  (24 other events, 23.4 us)

commit v2 on v1

v2 whole, which is shorter than its diff:
```python
import functools

import jax
import jax.numpy as jnp
from jax import lax
from jax.experimental import pallas as pl
from jax.experimental.pallas import tpu as pltpu
from jax.sharding import PartitionSpec as P

CHUNKS = 8
LANES = 128
VMEM_LIMIT = 24 * 1024 * 1024
STREAMS = (((0, 1, "xyz"), (2, 3, "yxz")), ((1, 2, "xyz"), (3, 4, "yxz")))

TWO_OVER_PI = 0.6366197723675814
PIO2_HIGH = 1.5703125
PIO2_MID = 0.0004837512969970703
PIO2_LOW = 7.549789948768648e-08


def sin_cos(angle):
    quadrant_real = jnp.floor(angle * TWO_OVER_PI + 0.5)
    rest = angle - quadrant_real * PIO2_HIGH
    rest = rest - quadrant_real * PIO2_MID
    rest = rest - quadrant_real * PIO2_LOW
    square = rest * rest
    sine = rest + rest * square * (
        -1.6666654611e-1 + square * (8.3321608736e-3 + square * -1.9515295891e-4)
    )
    cosine = (
        1.0
        - 0.5 * square
        + square
        * square
        * (4.166664568298827e-2 + square * (-1.388731625493765e-3 + square * 2.443315711809948e-5))
    )
    quadrant = quadrant_real.astype(jnp.int32)
    swapped = (quadrant & 1) == 1
    sin_base = jnp.where(swapped, cosine, sine)
    cos_base = jnp.where(swapped, sine, cosine)
    sin_value = jnp.where((quadrant & 2) == 2, -sin_base, sin_base)
    cos_value = jnp.where(((quadrant + 1) & 2) == 2, -cos_base, cos_base)
    return sin_value, cos_value


def gain_of(decay):
    twice = 2.0 * decay
    series = 1.0 / 3628800.0
    for factorial in (362880.0, 40320.0, 5040.0, 720.0, 120.0, 24.0, 6.0, 2.0, 1.0):
        series = 1.0 / factorial - twice * series
    return jnp.sqrt(jnp.where(twice < 0.5, twice * series, 1.0 - jnp.exp(-twice)))


def places():
    return lax.axis_index("context"), lax.axis_index("dp")


def local_scan_kernel(
    step_hbm,
    decay_hbm,
    frequency_hbm,
    in_hbm,
    cot_hbm,
    in_proj_hbm,
    out_proj_hbm,
    fwd_re,
    fwd_im,
    fwd_are,
    fwd_aim,
    back_re,
    back_im,
    back_are,
    back_aim,
    chunk_ref,
    summary_ref,
    outside_ref,
    in_vmem,
    cot_vmem,
    in_proj_vmem,
    out_proj_vmem,
    decay_ref,
    step_ref,
    frequency_ref,
    lam_re,
    lam_im,
    drive,
    adjoint,
    sems,
):
    rows = in_vmem.shape[0]
    length = rows // CHUNKS
    states = decay_ref.shape[1]
    lanes = states // LANES
    copies = [
        pltpu.make_async_copy(source, target, sems.at[slot])
        for slot, (source, target) in enumerate(
            (
                (step_hbm, step_ref),
                (decay_hbm, decay_ref),
                (frequency_hbm, frequency_ref),
                (in_hbm, in_vmem),
                (in_proj_hbm, in_proj_vmem),
                (cot_hbm, cot_vmem),
                (out_proj_hbm, out_proj_vmem),
            )
        )
    ]
    for copy in copies:
        copy.start()
    for copy in copies[:3]:
        copy.wait()
    loads = copies[3:]
    decay = decay_ref[...]
    frequency = frequency_ref[...]
    gain = gain_of(decay)
    steps = jnp.concatenate(
        [step_ref[:, chunk * length : (chunk + 1) * length] for chunk in range(CHUNKS)], axis=0
    )
    for place in range(length):
        here = jnp.broadcast_to(steps[:, place : place + 1], (CHUNKS, states))
        damping = jnp.exp(-here * decay)
        sine, cosine = sin_cos(here * frequency)
        lam_re[pl.ds(place * CHUNKS, CHUNKS), :] = damping * cosine
        lam_im[pl.ds(place * CHUNKS, CHUNKS), :] = damping * sine
    loads[0].wait()
    loads[1].wait()
    pair_gain = jnp.concatenate([gain, gain], axis=1)
    driven = (
        jnp.dot(in_vmem[...], in_proj_vmem[...], preferred_element_type=jnp.float32) * pair_gain
    )
    for lane in range(2 * lanes):
        drive[lane] = driven[:, lane * LANES : (lane + 1) * LANES]
    loads[2].wait()
    loads[3].wait()
    driven = jnp.dot(cot_vmem[...], out_proj_vmem[...], preferred_element_type=jnp.float32)
    for lane in range(2 * lanes):
        adjoint[lane] = driven[:, lane * LANES : (lane + 1) * LANES]

    def gather(ref, first, spread):
        return jnp.concatenate([ref[first + lane, spread, :] for lane in range(lanes)], axis=1)

    def scatter(ref, spread, value):
        for lane in range(lanes):
            ref[lane, spread, :] = value[:, lane * LANES : (lane + 1) * LANES]

    def body(place, carry):
        f_are, f_aim, f_re, f_im, b_are, b_aim, b_re, b_im = carry
        tile = pl.ds(pl.multiple_of(place * CHUNKS, CHUNKS), CHUNKS)
        spread = pl.ds(place, CHUNKS, stride=length)
        l_re, l_im = lam_re[tile, :], lam_im[tile, :]
        new_are = l_re * f_are - l_im * f_aim
        new_aim = l_re * f_aim + l_im * f_are
        new_re = l_re * f_re - l_im * f_im + gather(drive, 0, spread)
        new_im = l_re * f_im + l_im * f_re + gather(drive, lanes, spread)
        scatter(fwd_are, spread, new_are)
        scatter(fwd_aim, spread, new_aim)
        scatter(fwd_re, spread, new_re)
        scatter(fwd_im, spread, new_im)
        mirror = length - 1 - place
        tile = pl.ds(pl.multiple_of(mirror * CHUNKS, CHUNKS), CHUNKS)
        spread = pl.ds(mirror, CHUNKS, stride=length)
        l_re, l_im = lam_re[tile, :], lam_im[tile, :]
        a_re = b_re + gather(adjoint, 0, spread)
        a_im = b_im + gather(adjoint, lanes, spread)
        scatter(back_are, spread, b_are)
        scatter(back_aim, spread, b_aim)
        scatter(back_re, spread, a_re)
        scatter(back_im, spread, a_im)
        next_are = l_re * b_are + l_im * b_aim
        next_aim = l_re * b_aim - l_im * b_are
        next_re = l_re * a_re + l_im * a_im
        next_im = l_re * a_im - l_im * a_re
        return (new_are, new_aim, new_re, new_im, next_are, next_aim, next_re, next_im)

    zero = jnp.zeros((CHUNKS, states), jnp.float32)
    one = jnp.ones((CHUNKS, states), jnp.float32)
    totals = lax.fori_loop(
        0, length, body, (one, zero, zero, zero, one, zero, zero, zero), unroll=4
    )
    a_re, a_im, f_re, f_im, _, _, b_re, b_im = totals
    for slot, part in enumerate((a_re, a_im, f_re, f_im, b_re, b_im)):
        chunk_ref[slot] = part
    row = lambda part, chunk: part[chunk : chunk + 1, :]
    t_are, t_aim = row(a_re, 0), row(a_im, 0)
    t_re, t_im = row(f_re, 0), row(f_im, 0)
    for chunk in range(1, CHUNKS):
        l_re, l_im = row(a_re, chunk), row(a_im, chunk)
        t_are, t_aim = l_re * t_are - l_im * t_aim, l_re * t_aim + l_im * t_are
        t_re, t_im = (
            l_re * t_re - l_im * t_im + row(f_re, chunk),
            l_re * t_im + l_im * t_re + row(f_im, chunk),
        )
    u_re, u_im = row(b_re, CHUNKS - 1), row(b_im, CHUNKS - 1)
    for chunk in range(CHUNKS - 2, -1, -1):
        l_re, l_im = row(a_re, chunk), row(a_im, chunk)
        u_re, u_im = (
            l_re * u_re + l_im * u_im + row(b_re, chunk),
            l_re * u_im - l_im * u_re + row(b_im, chunk),
        )
    summary_ref[...] = jnp.concatenate(
        [t_are, t_aim, t_re, t_im, u_re, u_im, t_are, t_aim], axis=0
    )
    one, zero = jnp.ones_like(t_are), jnp.zeros_like(t_are)
    outside_ref[...] = jnp.concatenate([one, zero, zero, zero] * 2, axis=0)


def held(shape, dtype=jnp.float32):
    return pltpu.VMEM(shape, dtype)


def call(kernel, name, out_shape, *args, inputs=None, outputs=None, scratch=(), flops=0):
    vmem = pl.BlockSpec(memory_space=pltpu.VMEM)
    return pl.pallas_call(
        kernel,
        out_shape=out_shape,
        in_specs=inputs or [vmem] * len(args),
        out_specs=outputs or jax.tree.map(lambda _: vmem, out_shape),
        scratch_shapes=scratch,
        compiler_params=pltpu.CompilerParams(vmem_limit_bytes=VMEM_LIMIT),
        cost_estimate=pl.CostEstimate(
            flops=flops, bytes_accessed=max(flops // 1000, 1024), transcendentals=0
        ),
        name=name,
    )(*args)


def local_scan(step_row, decay, frequency, flat_in, flat_cot, input_proj, output_proj):
    rows = flat_in.shape[0]
    states = decay.shape[1]
    lanes = states // LANES
    args = [
        pltpu.with_memory_space_constraint(array, pltpu.HBM)
        for array in (step_row, decay, frequency, flat_in, flat_cot, input_proj, output_proj)
    ]
    return call(
        local_scan_kernel,
        "local_scan",
        [held((lanes, rows, LANES))] * 8
        + [held((6, CHUNKS, states)), held((8, states)), held((8, states))]
        + [held(array.shape, array.dtype) for array in args[3:]]
        + [held(decay.shape)],
        *args,
        inputs=[pl.BlockSpec(memory_space=pltpu.HBM)] * 7,
        scratch=[
            pltpu.VMEM(step_row.shape, jnp.float32),
            pltpu.VMEM(frequency.shape, jnp.float32),
            pltpu.VMEM((rows, states), jnp.float32),
            pltpu.VMEM((rows, states), jnp.float32),
            pltpu.VMEM((2 * lanes, rows, LANES), jnp.float32),
            pltpu.VMEM((2 * lanes, rows, LANES), jnp.float32),
            pltpu.SemaphoreType.DMA((7,)),
        ],
        flops=4 * rows * flat_in.shape[1] * 2 * states,
    )


def times(a, b):
    return a[0] * b[0] - a[1] * b[1], a[0] * b[1] + a[1] * b[0]


def times_conj(a, b):
    return a[0] * b[0] + a[1] * b[1], a[0] * b[1] - a[1] * b[0]


def plus(a, b):
    return a[0] + b[0], a[1] + b[1]


def pick(upper, a, b):
    return tuple(jnp.where(upper, x, y) for x, y in zip(a, b))


def pairs_of(array):
    return [(array[row : row + 1], array[row + 1 : row + 2]) for row in range(0, 8, 2)]


def widen(bit, outside, other):
    upper = ((lax.axis_index("context") >> bit) & 1) == 1
    below, below_sum, above, above_sum = outside
    product, forward, backward, _ = other
    return (
        pick(upper, times(below, product), below),
        pick(upper, plus(times(below, forward), below_sum), below_sum),
        pick(upper, above, times(above, product)),
        pick(upper, above_sum, plus(times_conj(above, backward), above_sum)),
    )


def combine_kernel(bit, total_ref, outside_ref, other_ref, total_out, outside_out):
    other = pairs_of(other_ref[...])
    mine = pairs_of(total_ref[...])
    outside = widen(bit, pairs_of(outside_ref[...]), other)
    outside_out[...] = jnp.concatenate([part for pair in outside for part in pair], axis=0)
    upper = ((lax.axis_index("context") >> bit) & 1) == 1
    low = [pick(upper, theirs, ours) for theirs, ours in zip(other, mine)]
    high = [pick(upper, ours, theirs) for theirs, ours in zip(other, mine)]
    product = times(low[0], high[0])
    forward = plus(times(high[0], low[1]), high[1])
    backward = plus(times_conj(low[0], high[2]), low[2])
    total_out[...] = jnp.concatenate([*product, *forward, *backward, *product], axis=0)


def states_kernel(
    bit,
    decay_ref,
    chunk_ref,
    fwd_re,
    fwd_im,
    fwd_are,
    fwd_aim,
    back_re,
    back_im,
    back_are,
    back_aim,
    outside_ref,
    other_ref,
    in_ref,
    cot_ref,
    state_ref,
    adjoint_ref,
    grad_ref,
):
    lanes, rows, _ = fwd_re.shape
    states = lanes * LANES
    length = rows // CHUNKS
    whole = lambda ref, part: jnp.concatenate([ref[lane, part, :] for lane in range(lanes)], axis=1)
    dp_place = places()[1]
    gain = gain_of(decay_ref[...])
    outside = widen(bit, pairs_of(outside_ref[...]), pairs_of(other_ref[...]))
    (f_re, f_im), (b_re, b_im) = outside[1], outside[3]
    for chunk in range(CHUNKS):
        part = pl.ds(chunk * length, length)
        a_re, a_im = whole(fwd_are, part), whole(fwd_aim, part)
        state_ref[part, pl.ds(0, states)] = (whole(fwd_re, part) + a_re * f_re - a_im * f_im).astype(
            jnp.bfloat16
        )
        state_ref[part, pl.ds(states, states)] = (
            whole(fwd_im, part) + a_re * f_im + a_im * f_re
        ).astype(jnp.bfloat16)
        l_re, l_im = chunk_ref[0, chunk : chunk + 1, :], chunk_ref[1, chunk : chunk + 1, :]
        f_re, f_im = (
            l_re * f_re - l_im * f_im + chunk_ref[2, chunk : chunk + 1, :],
            l_re * f_im + l_im * f_re + chunk_ref[3, chunk : chunk + 1, :],
        )
    for chunk in range(CHUNKS - 1, -1, -1):
        part = pl.ds(chunk * length, length)
        a_re, a_im = whole(back_are, part), whole(back_aim, part)
        adjoint_ref[part, pl.ds(0, states)] = (
            (whole(back_re, part) + a_re * b_re - a_im * b_im) * gain
        ).astype(jnp.bfloat16)
        adjoint_ref[part, pl.ds(states, states)] = (
            (whole(back_im, part) + a_re * b_im + a_im * b_re) * gain
        ).astype(jnp.bfloat16)
        l_re, l_im = chunk_ref[0, chunk : chunk + 1, :], chunk_ref[1, chunk : chunk + 1, :]
        b_re, b_im = (
            l_re * b_re + l_im * b_im + chunk_ref[4, chunk : chunk + 1, :],
            l_re * b_im - l_im * b_re + chunk_ref[5, chunk : chunk + 1, :],
        )
    over_rows = (((0,), (0,)), ((), ()))

    @pl.when(dp_place & 1 == 0)
    def _():
        grad_ref[...] = lax.dot_general(
            cot_ref[...], state_ref[...], over_rows, preferred_element_type=jnp.float32
        )

    @pl.when(dp_place & 1 == 1)
    def _():
        grad_ref[...] = lax.dot_general(
            in_ref[...], adjoint_ref[...], over_rows, preferred_element_type=jnp.float32
        )


def global_states(bit, decay, chunk_totals, planes, outside, other, flat_in, flat_cot):
    rows, width = flat_in.shape
    states = decay.shape[1]
    return call(
        functools.partial(states_kernel, bit),
        "global_states",
        [
            held((rows, 2 * states), jnp.bfloat16),
            held((rows, 2 * states), jnp.bfloat16),
            held((width, 2 * states)),
        ],
        decay,
        chunk_totals,
        *planes,
        outside,
        other,
        flat_in,
        flat_cot,
        flops=2 * rows * width * 2 * states,
    )


def products_kernel(
    in_ref,
    cot_ref,
    state_ref,
    adjoint_ref,
    in_proj_ref,
    out_proj_ref,
    skip_ref,
    grad_ref,
    out_hbm,
    back_hbm,
    out_ref,
    back_ref,
    sems,
):
    over_rows = (((0,), (0,)), ((), ()))
    over_states = (((1,), (1,)), ((), ()))
    skip = skip_ref[...]
    stores = []
    for slot, (pairs, proj, skipped, target, result) in enumerate(
        (
            (state_ref, out_proj_ref, in_ref, out_ref, out_hbm),
            (adjoint_ref, in_proj_ref, cot_ref, back_ref, back_hbm),
        )
    ):
        mixed = lax.dot_general(
            pairs[...], proj[...], over_states, preferred_element_type=jnp.float32
        )
        target[...] = (mixed + skip * skipped[...].astype(jnp.float32)).astype(jnp.bfloat16)
        stores.append(pltpu.make_async_copy(target, result, sems.at[slot]))
        stores[-1].start()
    core = places()[1] & 1

    @pl.when(core == 0)
    def _():
        grad_ref[...] = lax.dot_general(
            in_ref[...], adjoint_ref[...], over_rows, preferred_element_type=jnp.float32
        )

    @pl.when(core == 1)
    def _():
        grad_ref[...] = lax.dot_general(
            cot_ref[...], state_ref[...], over_rows, preferred_element_type=jnp.float32
        )

    for store in stores:
        store.wait()


def products(flat_in, flat_cot, state_pairs, adjoint_pairs, input_proj, output_proj, skip_gain):
    rows, width = flat_in.shape
    vmem = pl.BlockSpec(memory_space=pltpu.VMEM)
    hbm = pl.BlockSpec(memory_space=pltpu.HBM)
    return call(
        products_kernel,
        "products",
        [
            held((width, state_pairs.shape[1])),
            jax.ShapeDtypeStruct(flat_in.shape, jnp.bfloat16),
            jax.ShapeDtypeStruct(flat_in.shape, jnp.bfloat16),
        ],
        flat_in,
        flat_cot,
        state_pairs,
        adjoint_pairs,
        input_proj,
        output_proj,
        skip_gain,
        outputs=[vmem, hbm, hbm],
        scratch=[
            pltpu.VMEM(flat_in.shape, jnp.bfloat16),
            pltpu.VMEM(flat_in.shape, jnp.bfloat16),
            pltpu.SemaphoreType.DMA((2,)),
        ],
        flops=6 * rows * width * state_pairs.shape[1],
    )


def own_bit(step):
    axis, bit = step
    return (lax.axis_index(axis) >> bit) & 1


def add_kernel(plans, scale, *refs):
    merged = plans[0][3] is None
    count = 1 if merged else len(plans)
    outs = refs[len(refs) - count :]
    at = 0
    for number, (layouts, columns, settled, sent) in enumerate(plans):
        out = outs[0] if merged else outs[number]
        sources = refs[at : at + len(layouts)]
        at += len(layouts)
        free = [step for step in layouts[-1] if step not in settled and step != sent]
        fixed = {step: own_bit(step) for step in settled}
        if sent is not None:
            fixed[sent] = 1 - own_bit(sent)
        for block in range(2 ** len(free)):
            values = dict(fixed)
            for place, step in enumerate(free):
                values[step] = (block >> (len(free) - 1 - place)) & 1
            total = None
            for source, layout in zip(sources, layouts):
                index = 0
                for step in layout:
                    index = index * 2 + values[step]
                wide = source.shape[2] != columns[1] - columns[0]
                part = source[index, :, columns[0] : columns[1]] if wide else source[index]
                total = part if total is None else total + part
            if merged:
                out[block, :, columns[0] : columns[1]] = total * scale
            else:
                out[block] = total


def gather_kernel(*refs):
    in_ref, out_ref = refs[-2:]
    dp_place = places()[1]
    for offset, share in enumerate(refs[:-2]):
        place = dp_place ^ offset

        @pl.when(place & 1 == 0)
        def _():
            in_ref[place >> 1] = share[0]

        @pl.when(place & 1 == 1)
        def _():
            out_ref[place >> 1] = share[0]


def on_device(
    inputs, step_size, decay_rate, frequency, input_proj, output_proj, skip_gain, cotangent
):
    batch_count, row_count, model_width = inputs.shape
    state_count = decay_rate.shape[0]
    dp_count, context_count = lax.axis_size("dp"), lax.axis_size("context")
    dp_bits, context_bits = dp_count.bit_length() - 1, context_count.bit_length() - 1

    def swap(array, step):
        axis, bit = step
        count = dp_count if axis == "dp" else context_count
        return lax.ppermute(array, axis, [(place, place ^ (1 << bit)) for place in range(count)])

    *planes, chunk_totals, total, outside, flat_in, flat_cot, in_proj, out_proj, decay = local_scan(
        step_size,
        decay_rate.reshape(1, state_count),
        frequency.reshape(1, state_count),
        inputs.reshape(row_count, model_width),
        cotangent.reshape(row_count, model_width),
        input_proj,
        output_proj,
    )
    for bit in range(context_bits - 1):
        other = swap(total, ("context", bit))
        total, outside = call(
            functools.partial(combine_kernel, bit),
            "combine",
            [held(total.shape), held(outside.shape)],
            total,
            outside,
            other,
        )
    last = context_bits - 1
    state_pairs, adjoint_pairs, lent = global_states(
        last, decay, chunk_totals, planes, outside, swap(total, ("context", last)), flat_in, flat_cot
    )
    borrowed = swap(lent, ("dp", 0))
    kept, outputs, input_grad = products(
        flat_in,
        flat_cot,
        state_pairs,
        adjoint_pairs,
        in_proj,
        out_proj,
        skip_gain.reshape(1, model_width),
    )

    extra_bits = [("dp", bit) for bit in range(1, dp_bits)]
    piece = model_width // (context_count * dp_count // 2)
    layout = [("context", bit) for bit in reversed(range(context_bits))] + extra_bits[::-1]
    blocks = (2 ** len(layout), piece, 2 * state_count)
    grad_scale = float(batch_count * row_count * dp_count * context_count) ** (-0.5)
    z_bits = [("context", bit) for bit in range(1, context_bits)]
    y_bits = [("context", 0)]
    by_name = {"x": extra_bits, "y": y_bits, "z": z_bits, "Z": z_bits[::-1]}
    groups = []
    for plan in STREAMS:
        groups.append([])
        for first, past, names in plan:
            groups[-1].append(
                {
                    "columns": (first * LANES, past * LANES),
                    "sources": [kept.reshape(blocks), borrowed.reshape(blocks)],
                    "layouts": [layout, layout],
                    "settled": [],
                    "order": [step for name in names for step in by_name[name]],
                }
            )
    streams = [stream for group in groups for stream in group]

    def add(streams, steps, scale=None):
        plans, args, shapes = [], [], []
        for stream, step in zip(streams, steps):
            plans.append((stream["layouts"], stream["columns"], list(stream["settled"]), step))
            args += stream["sources"]
            free = len(layout) - len(stream["settled"]) - (step is not None)
            width = stream["columns"][1] - stream["columns"][0]
            shapes.append(held((2**free, piece, width)))
        if scale is not None:
            shapes = [held((1, piece, 2 * state_count))]
        name = "halve" if scale is None else "share"
        return call(functools.partial(add_kernel, plans, scale), name, shapes, *args)

    for place in range(len(layout)):
        for group in groups:
            steps = [stream["order"][place] for stream in group]
            for stream, step, away in zip(group, steps, add(group, steps)):
                stream["settled"] = stream["settled"] + [step]
                left = [bit for bit in layout if bit not in stream["settled"]]
                stream["sources"] = stream["sources"] + [swap(away, step)]
                stream["layouts"] = stream["layouts"] + [left]
    shares = list(add(streams, [None] * len(streams), grad_scale))
    for bit in [*range(1, dp_bits), 0]:
        shares = shares + [swap(share, ("dp", bit)) for share in shares]
    order = [0]
    for bit in [*range(1, dp_bits), 0]:
        order = order + [offset ^ (1 << bit) for offset in order]
    by_offset = [shares[order.index(offset)] for offset in range(dp_count)]
    whole = jax.ShapeDtypeStruct((dp_count // 2, piece, 2 * state_count), jnp.float32)
    grads = call(gather_kernel, "gather", [whole, whole], *by_offset)
    grads = [grad.reshape(model_width // context_count, 2 * state_count) for grad in grads]
    return (outputs.reshape(inputs.shape), input_grad.reshape(inputs.shape), *grads)


def solution(mesh):
    in_specs = (
        P("dp", "context", None),
        P("dp", "context"),
        P(),
        P(),
        P(),
        P(),
        P(),
        P("dp", "context", None),
    )
    out_specs = (
        P("dp", "context", None),
        P("dp", "context", None),
        P("context", None),
        P("context", None),
    )
    return jax.shard_map(
        on_device, mesh=mesh, in_specs=in_specs, out_specs=out_specs, check_vma=False
    )
```

time: 115 us -> 71.6 us (0.62); the launches traced: 114 us -> 71.4 us
  local copies, waits for them, and re-layouts: 25.6 us -> 0.01 us
  other arithmetic: 10.2 us -> 0 us
  waiting for transfers between devices: 40.6 us -> 30.9 us
  starting transfers between devices: 21.1 us -> 27.2 us
  Pallas kernels: 15.3 us -> 12.6 us
    unnamed x66 -> x2, local copies, waits for them, and re-layouts: 22.6 us -> 0.01 us
    ppermute x16 -> x23, waiting for transfers between devices: 40.6 us -> 30.9 us  [swap(): lax.ppermute(array, axis, [(place, place ^ 1 << bit) for place in range(c...]
    ppermute x16 -> x23, starting transfers between devices: 21.1 us -> 27.2 us  [swap(): lax.ppermute(array, axis, [(place, place ^ 1 << bit) for place in range(c...]
    add x6 -> x0, other arithmetic: 4.66 us -> none  [the longest x5 2.78 us: halve(): away = swap(pick(pair[0], False) + pick(pair[1], False), axis, bit)]
    select_n x2 -> x0, other arithmetic: 2.8 us -> none  [the longest x1 1.79 us: on_device(): jnp.where(core == 0, other, share)]
    pallas_call x5 -> x15, Pallas kernels: 15.3 us -> 12.6 us  [call(): pl.pallas_call(kernel, out_shape=out_shape, in_specs=inputs or [vmem] * l...]
    slice x2 -> x0, local copies, waits for them, and re-layouts: 1.81 us -> none  [the longest x1 1.68 us: on_device(): borrowed[:, cols:cols + half].reshape(shape)]
    unnamed x1 -> x0, other arithmetic: 1.34 us -> none
  transfers between devices with their start and end apart: 16 -> 23, of which waited for: 11 -> 17; matrix products, arithmetic and copies ran while one was open for 2% -> 0% of each run, Pallas kernels for 4% -> 4%
where the time goes in v2:
time: 71.6 us; the launch traced here: 71.4 us
  waiting for transfers between devices  30.9 us (43%)
  starting transfers between devices  27.2 us (38%)
  Pallas kernels  12.6 us (18%)
  between operations  0.72 us (1%)
    ppermute x23, waiting for transfers between devices, swap(): lax.ppermute(array, axis, [(place, place ^ 1 << bit) for place in range(c...  30.9 us
    ppermute x23, starting transfers between devices, swap(): lax.ppermute(array, axis, [(place, place ^ 1 << bit) for place in range(c...  27.2 us
    pallas_call x15, Pallas kernels, call(): pl.pallas_call(kernel, out_shape=out_shape, in_specs=inputs or [vmem] * l...  12.6 us
  transfers between devices with their start and end apart: 23, of which 17 were waited for; matrix products, arithmetic and copies ran while one was open for 0% of the time, Pallas kernels for 4%

profile of v2, /device:TPU:0, one launch (start us, length us, event | category | flops | bytes accessed | tf_op | source)
XLA Modules:
  0.0 71.4 jit_solution(10995149775579732068)
XLA Ops:
  0.6 7.6 %local_scan.1 = (f32[2,512,128]{2,1,0:T(8,128)S(1)}, f32[2,512,128]{2,1,0:T(8,128)S(1)}, f32[2,512,128]{2,1,0:T(8,128)S(1)}, f32[2,512,128]{2,1,0:T(8,128)S(1)},...) custom-call(f32[1,512]{1,0:T(1,128)} %step_hbm.1, ...), custom_call_target="tpu_custom_call" | custom-call | flops 1073741824 | bytes 1073741 | tf_op jit(solution)/shard_map/local_scan/pallas_call | solution.py:213
  8.2 3.0 %collective-permute-start = (f32[8,256]{1,0:T(8,128)S(1)}, f32[8,256]{1,0:T(8,128)S(1)}, u32[]{:S(2)}, u32[]{:S(2)}) collective-permute-start(f32[8,256]{1,0:T(8,128)S(1)} %get-tuple-element.60.total_ref), channel_id=1, source_target_pairs={{0,1},{1,0},{2,3},{3,2},{4,5},{5,4},{6,7},{7,6},{8,9},{9,8},{10,11... | collective-permute-start | bytes 24584 | tf_op jit(solution)/shard_map/ppermute | solution.py:536
  11.3 1.6 %collective-permute-done.other_ref = f32[8,256]{1,0:T(8,128)S(1)} collective-permute-done((f32[8,256]{1,0:T(8,128)S(1)}, f32[8,256]{1,0:T(8,128)S(1)}, u32[]{:S(2)}, u32[]{:S(2)}) %collective-permute-start) | collective-permute-done | bytes 8224 | tf_op jit(solution)/shard_map/ppermute | solution.py:536
  12.9 2.1 %collective-permute-start.1 = (f32[8,256]{1,0:T(8,128)S(1)}, f32[8,256]{1,0:T(8,128)S(1)}, u32[]{:S(2)}, u32[]{:S(2)}) collective-permute-start(f32[8,256]{1,0:T(8,128)S(1)} %get-tuple-element.62.total_ref), channel_id=1, source_target_pairs={{0,2},{1,3},{2,0},{3,1},{4,6},{5,7},{6,4},{7,5},{8,10},{9,11},{10,... | collective-permute-start | bytes 24584 | tf_op jit(solution)/shard_map/ppermute | solution.py:536
  15.1 1.6 %collective-permute-done.1.other_ref = f32[8,256]{1,0:T(8,128)S(1)} collective-permute-done((f32[8,256]{1,0:T(8,128)S(1)}, f32[8,256]{1,0:T(8,128)S(1)}, u32[]{:S(2)}, u32[]{:S(2)}) %collective-permute-start.1) | collective-permute-done | bytes 8224 | tf_op jit(solution)/shard_map/ppermute | solution.py:536
  16.7 3.1 %collective-permute-start.2 = (f32[8,256]{1,0:T(8,128)S(1)}, f32[8,256]{1,0:T(8,128)S(1)}, u32[]{:S(2)}, u32[]{:S(2)}) collective-permute-start(f32[8,256]{1,0:T(8,128)S(1)} %get-tuple-element.65), channel_id=1, source_target_pairs={{0,4},{1,5},{2,6},{3,7},{4,0},{5,1},{6,2},{7,3},{8,12},{9,13},{10,... | collective-permute-start | bytes 24584 | tf_op jit(solution)/shard_map/ppermute | solution.py:536
  19.8 1.6 %collective-permute-done.2.other_ref = f32[8,256]{1,0:T(8,128)S(1)} collective-permute-done((f32[8,256]{1,0:T(8,128)S(1)}, f32[8,256]{1,0:T(8,128)S(1)}, u32[]{:S(2)}, u32[]{:S(2)}) %collective-permute-start.2) | collective-permute-done | bytes 8224 | tf_op jit(solution)/shard_map/ppermute | solution.py:536
  22.7 2.3 %products.1 = (f32[1024,512]{1,0:T(8,128)S(1)}, bf16[512,1024]{1,0:T(8,128)(2,1)}, bf16[512,1024]{1,0:T(8,128)(2,1)}) custom-call(bf16[512,1024]{1,0:T(8,128)(2,1)S(1)} %get-tuple-element.48.in_ref, bf16[512,1024]{1,0:T(8,128)(2,1)S(1)} %get-tuple-element.49.cot_ref, bf16[512,512]{1,0:T(8,128)(2,1)S(1)} %get-tuple-element.66.state_ref, ...), custom_call_target="tpu_custom_call" | custom-call | flops 1610612736 | bytes 1610612 | tf_op jit(solution)/shard_map/products/pallas_call | solution.py:213
  25.1 1.8 %collective-permute-done.3 = f32[1024,512]{1,0:T(8,128)S(1)} collective-permute-done((f32[1024,512]{1,0:T(8,128)S(1)}, f32[1024,512]{1,0:T(8,128)S(1)}, u32[]{:S(2)}, u32[]{:S(2)}) %collective-permute-start.3) | collective-permute-done | bytes 2097184 | tf_op jit(solution)/shard_map/ppermute | solution.py:536
  27.0 1.9 %collective-permute-start.12 = (f32[8,64,128]{2,1,0:T(8,128)S(1)}, f32[8,64,128]{2,1,0:T(8,128)S(1)}, u32[]{:S(2)}, u32[]{:S(2)}) collective-permute-start(f32[8,64,128]{2,1,0:T(8,128)S(1)} %get-tuple-element.82), channel_id=1, source_target_pairs={{0,16},{8,24},{16,0},{24,8},{1,17},{9,25},{17,1},{25,9},{2,18},{10... | collective-permute-start | bytes 786440 | tf_op jit(solution)/shard_map/ppermute | solution.py:536
  28.9 1.5 %collective-permute-start.13 = (f32[8,64,128]{2,1,0:T(8,128)S(1)}, f32[8,64,128]{2,1,0:T(8,128)S(1)}, u32[]{:S(2)}, u32[]{:S(2)}) collective-permute-start(f32[8,64,128]{2,1,0:T(8,128)S(1)} %get-tuple-element.83), channel_id=1, source_target_pairs={{0,1},{1,0},{2,3},{3,2},{4,5},{5,4},{6,7},{7,6},{8,9},{9,8},{10,11... | collective-permute-start | bytes 786440 | tf_op jit(solution)/shard_map/ppermute | solution.py:536
  31.3 4.9 %collective-permute-done.12.refs_2_.refs_14_ = f32[8,64,128]{2,1,0:T(8,128)S(1)} collective-permute-done((f32[8,64,128]{2,1,0:T(8,128)S(1)}, f32[8,64,128]{2,1,0:T(8,128)S(1)}, u32[]{:S(2)}, u32[]{:S(2)}) %collective-permute-start.12) | collective-permute-done | bytes 262176 | tf_op jit(solution)/shard_map/ppermute | solution.py:536
  36.2 1.9 %collective-permute-done.13.refs_5_.refs_6_.refs_7_.refs_20_ = f32[8,64,128]{2,1,0:T(8,128)S(1)} collective-permute-done((f32[8,64,128]{2,1,0:T(8,128)S(1)}, f32[8,64,128]{2,1,0:T(8,128)S(1)}, u32[]{:S(2)}, u32[]{:S(2)}) %collective-permute-start.13) | collective-permute-done | bytes 262176 | tf_op jit(solution)/shard_map/ppermute | solution.py:536
  38.2 1.6 %collective-permute-start.14 = (f32[4,64,128]{2,1,0:T(8,128)S(1)}, f32[4,64,128]{2,1,0:T(8,128)S(1)}, u32[]{:S(2)}, u32[]{:S(2)}) collective-permute-start(f32[4,64,128]{2,1,0:T(8,128)S(1)} %get-tuple-element.84), channel_id=1, source_target_pairs={{0,1},{1,0},{2,3},{3,2},{4,5},{5,4},{6,7},{7,6},{8,9},{9,8},{10,11... | collective-permute-start | bytes 393224 | tf_op jit(solution)/shard_map/ppermute | solution.py:536
  40.3 1.5 %collective-permute-done.4.refs_2_ = f32[8,64,128]{2,1,0:T(8,128)S(1)} collective-permute-done((f32[8,64,128]{2,1,0:T(8,128)S(1)}, f32[8,64,128]{2,1,0:T(8,128)S(1)}, u32[]{:S(2)}, u32[]{:S(2)}) %collective-permute-start.4) | collective-permute-done | bytes 262176 | tf_op jit(solution)/shard_map/ppermute | solution.py:536
  41.8 1.9 %collective-permute-done.5.refs_5_.refs_6_.refs_7_.refs_8_ = f32[8,64,128]{2,1,0:T(8,128)S(1)} collective-permute-done((f32[8,64,128]{2,1,0:T(8,128)S(1)}, f32[8,64,128]{2,1,0:T(8,128)S(1)}, u32[]{:S(2)}, u32[]{:S(2)}) %collective-permute-start.5) | collective-permute-done | bytes 262176 | tf_op jit(solution)/shard_map/ppermute | solution.py:536
  43.8 1.6 %collective-permute-start.6 = (f32[4,64,128]{2,1,0:T(8,128)S(1)}, f32[4,64,128]{2,1,0:T(8,128)S(1)}, u32[]{:S(2)}, u32[]{:S(2)}) collective-permute-start(f32[4,64,128]{2,1,0:T(8,128)S(1)} %get-tuple-element.76), channel_id=1, source_target_pairs={{0,1},{1,0},{2,3},{3,2},{4,5},{5,4},{6,7},{7,6},{8,9},{9,8},{10,11... | collective-permute-start | bytes 393224 | tf_op jit(solution)/shard_map/ppermute | solution.py:536
  46.4 1.7 %collective-permute-start.16 = (f32[2,64,128]{2,1,0:T(8,128)S(1)}, f32[2,64,128]{2,1,0:T(8,128)S(1)}, u32[]{:S(2)}, u32[]{:S(2)}) collective-permute-start(f32[2,64,128]{2,1,0:T(8,128)S(1)} %get-tuple-element.86), channel_id=1, source_target_pairs={{0,2},{1,3},{2,0},{3,1},{4,6},{5,7},{6,4},{7,5},{8,10},{9,11},{10,... | collective-permute-start | bytes 196616 | tf_op jit(solution)/shard_map/ppermute | solution.py:536
  50.4 1.6 %collective-permute-start.8 = (f32[2,64,128]{2,1,0:T(8,128)S(1)}, f32[2,64,128]{2,1,0:T(8,128)S(1)}, u32[]{:S(2)}, u32[]{:S(2)}) collective-permute-start(f32[2,64,128]{2,1,0:T(8,128)S(1)} %get-tuple-element.78), channel_id=1, source_target_pairs={{0,2},{1,3},{2,0},{3,1},{4,6},{5,7},{6,4},{7,5},{8,10},{9,11},{10,... | collective-permute-start | bytes 196616 | tf_op jit(solution)/shard_map/ppermute | solution.py:536
  52.5 2.8 %collective-permute-start.18 = (f32[1,64,128]{2,1,0:T(8,128)S(1)}, f32[1,64,128]{2,1,0:T(8,128)S(1)}, u32[]{:S(2)}, u32[]{:S(2)}) collective-permute-start(f32[1,64,128]{2,1,0:T(8,128)S(1)} %get-tuple-element.88), channel_id=1, source_target_pairs={{0,4},{1,5},{2,6},{3,7},{4,0},{5,1},{6,2},{7,3},{8,12},{9,13},{10,... | collective-permute-start | bytes 98312 | tf_op jit(solution)/shard_map/ppermute | solution.py:536
  56.5 2.4 %collective-permute-start.10 = (f32[1,64,128]{2,1,0:T(8,128)S(1)}, f32[1,64,128]{2,1,0:T(8,128)S(1)}, u32[]{:S(2)}, u32[]{:S(2)}) collective-permute-start(f32[1,64,128]{2,1,0:T(8,128)S(1)} %get-tuple-element.80), channel_id=1, source_target_pairs={{0,4},{1,5},{2,6},{3,7},{4,0},{5,1},{6,2},{7,3},{8,12},{9,13},{10,... | collective-permute-start | bytes 98312 | tf_op jit(solution)/shard_map/ppermute | solution.py:536
  60.1 1.6 %collective-permute-done.10.refs_5_ = f32[1,64,128]{2,1,0:T(8,128)S(1)} collective-permute-done((f32[1,64,128]{2,1,0:T(8,128)S(1)}, f32[1,64,128]{2,1,0:T(8,128)S(1)}, u32[]{:S(2)}, u32[]{:S(2)}) %collective-permute-start.10) | collective-permute-done | bytes 32800 | tf_op jit(solution)/shard_map/ppermute | solution.py:536
  61.8 2.4 %collective-permute-done.11.refs_11_ = f32[1,64,128]{2,1,0:T(8,128)S(1)} collective-permute-done((f32[1,64,128]{2,1,0:T(8,128)S(1)}, f32[1,64,128]{2,1,0:T(8,128)S(1)}, u32[]{:S(2)}, u32[]{:S(2)}) %collective-permute-start.11) | collective-permute-done | bytes 32800 | tf_op jit(solution)/shard_map/ppermute | solution.py:536
  64.4 4.8 %collective-permute-done.21.refs_2_ = f32[1,64,512]{2,1,0:T(8,128)S(1)} collective-permute-done((f32[1,64,512]{2,1,0:T(8,128)S(1)}, f32[1,64,512]{2,1,0:T(8,128)S(1)}, u32[]{:S(2)}, u32[]{:S(2)}) %collective-permute-start.21) | collective-permute-done | bytes 131104 | tf_op jit(solution)/shard_map/ppermute | solution.py:536
  (39 shorter events, 11.7 us)
Async XLA Ops:
  8.2 4.7 %collective-permute-start = (f32[8,256]{1,0:T(8,128)S(1)}, f32[8,256]{1,0:T(8,128)S(1)}, u32[]{:S(2)}, u32[]{:S(2)}) collective-permute-start(f32[8,256]{1,0:T(8,128)S(1)} %get-tuple-element.60.total_ref), channel_id=1, source_target_pairs={{0,1},{1,0},{2,3},{3,2},{4,5},{5,4},{6,7},{7,6},{8,9},{9,8},{10,11... | collective-permute-start | bytes 24584 | tf_op jit(solution)/shard_map/ppermute | solution.py:536
  12.9 3.8 %collective-permute-start.1 = (f32[8,256]{1,0:T(8,128)S(1)}, f32[8,256]{1,0:T(8,128)S(1)}, u32[]{:S(2)}, u32[]{:S(2)}) collective-permute-start(f32[8,256]{1,0:T(8,128)S(1)} %get-tuple-element.62.total_ref), channel_id=1, source_target_pairs={{0,2},{1,3},{2,0},{3,1},{4,6},{5,7},{6,4},{7,5},{8,10},{9,11},{10,... | collective-permute-start | bytes 24584 | tf_op jit(solution)/shard_map/ppermute | solution.py:536
  16.7 4.7 %collective-permute-start.2 = (f32[8,256]{1,0:T(8,128)S(1)}, f32[8,256]{1,0:T(8,128)S(1)}, u32[]{:S(2)}, u32[]{:S(2)}) collective-permute-start(f32[8,256]{1,0:T(8,128)S(1)} %get-tuple-element.65), channel_id=1, source_target_pairs={{0,4},{1,5},{2,6},{3,7},{4,0},{5,1},{6,2},{7,3},{8,12},{9,13},{10,... | collective-permute-start | bytes 24584 | tf_op jit(solution)/shard_map/ppermute | solution.py:536
  21.5 1.3 %copy-start = (f32[1024]{0:T(1024)S(1)}, f32[1024]{0:T(1024)}, u32[]{:S(2)}) copy-start(f32[1024]{0:T(1024)} %param.14) | copy-start | bytes 12292
  22.7 4.2 %collective-permute-start.3 = (f32[1024,512]{1,0:T(8,128)S(1)}, f32[1024,512]{1,0:T(8,128)S(1)}, u32[]{:S(2)}, u32[]{:S(2)}) collective-permute-start(f32[1024,512]{1,0:T(8,128)S(1)} %get-tuple-element.73), channel_id=1, source_target_pairs={{0,8},{8,0},{16,24},{24,16},{1,9},{9,1},{17,25},{25,17},{2,10},{10... | collective-permute-start | bytes 6291464 | tf_op jit(solution)/shard_map/ppermute | solution.py:536
  27.0 9.2 %collective-permute-start.12 = (f32[8,64,128]{2,1,0:T(8,128)S(1)}, f32[8,64,128]{2,1,0:T(8,128)S(1)}, u32[]{:S(2)}, u32[]{:S(2)}) collective-permute-start(f32[8,64,128]{2,1,0:T(8,128)S(1)} %get-tuple-element.82), channel_id=1, source_target_pairs={{0,16},{8,24},{16,0},{24,8},{1,17},{9,25},{17,1},{25,9},{2,18},{10... | collective-permute-start | bytes 786440 | tf_op jit(solution)/shard_map/ppermute | solution.py:536
  28.9 9.2 %collective-permute-start.13 = (f32[8,64,128]{2,1,0:T(8,128)S(1)}, f32[8,64,128]{2,1,0:T(8,128)S(1)}, u32[]{:S(2)}, u32[]{:S(2)}) collective-permute-start(f32[8,64,128]{2,1,0:T(8,128)S(1)} %get-tuple-element.83), channel_id=1, source_target_pairs={{0,1},{1,0},{2,3},{3,2},{4,5},{5,4},{6,7},{7,6},{8,9},{9,8},{10,11... | collective-permute-start | bytes 786440 | tf_op jit(solution)/shard_map/ppermute | solution.py:536
  30.5 11.3 %collective-permute-start.4 = (f32[8,64,128]{2,1,0:T(8,128)S(1)}, f32[8,64,128]{2,1,0:T(8,128)S(1)}, u32[]{:S(2)}, u32[]{:S(2)}) collective-permute-start(f32[8,64,128]{2,1,0:T(8,128)S(1)} %get-tuple-element.74), channel_id=1, source_target_pairs={{0,16},{8,24},{16,0},{24,8},{1,17},{9,25},{17,1},{25,9},{2,18},{10... | collective-permute-start | bytes 786440 | tf_op jit(solution)/shard_map/ppermute | solution.py:536
  31.1 12.6 %collective-permute-start.5 = (f32[8,64,128]{2,1,0:T(8,128)S(1)}, f32[8,64,128]{2,1,0:T(8,128)S(1)}, u32[]{:S(2)}, u32[]{:S(2)}) collective-permute-start(f32[8,64,128]{2,1,0:T(8,128)S(1)} %get-tuple-element.75), channel_id=1, source_target_pairs={{0,1},{1,0},{2,3},{3,2},{4,5},{5,4},{6,7},{7,6},{8,9},{9,8},{10,11... | collective-permute-start | bytes 786440 | tf_op jit(solution)/shard_map/ppermute | solution.py:536
  38.2 8.2 %collective-permute-start.14 = (f32[4,64,128]{2,1,0:T(8,128)S(1)}, f32[4,64,128]{2,1,0:T(8,128)S(1)}, u32[]{:S(2)}, u32[]{:S(2)}) collective-permute-start(f32[4,64,128]{2,1,0:T(8,128)S(1)} %get-tuple-element.84), channel_id=1, source_target_pairs={{0,1},{1,0},{2,3},{3,2},{4,5},{5,4},{6,7},{7,6},{8,9},{9,8},{10,11... | collective-permute-start | bytes 393224 | tf_op jit(solution)/shard_map/ppermute | solution.py:536
  39.7 6.7 %collective-permute-start.15 = (f32[4,64,128]{2,1,0:T(8,128)S(1)}, f32[4,64,128]{2,1,0:T(8,128)S(1)}, u32[]{:S(2)}, u32[]{:S(2)}) collective-permute-start(f32[4,64,128]{2,1,0:T(8,128)S(1)} %get-tuple-element.85), channel_id=1, source_target_pairs={{0,16},{8,24},{16,0},{24,8},{1,17},{9,25},{17,1},{25,9},{2,18},{10... | collective-permute-start | bytes 393224 | tf_op jit(solution)/shard_map/ppermute | solution.py:536
  43.8 5.0 %collective-permute-start.6 = (f32[4,64,128]{2,1,0:T(8,128)S(1)}, f32[4,64,128]{2,1,0:T(8,128)S(1)}, u32[]{:S(2)}, u32[]{:S(2)}) collective-permute-start(f32[4,64,128]{2,1,0:T(8,128)S(1)} %get-tuple-element.76), channel_id=1, source_target_pairs={{0,1},{1,0},{2,3},{3,2},{4,5},{5,4},{6,7},{7,6},{8,9},{9,8},{10,11... | collective-permute-start | bytes 393224 | tf_op jit(solution)/shard_map/ppermute | solution.py:536
  45.4 5.0 %collective-permute-start.7 = (f32[4,64,128]{2,1,0:T(8,128)S(1)}, f32[4,64,128]{2,1,0:T(8,128)S(1)}, u32[]{:S(2)}, u32[]{:S(2)}) collective-permute-start(f32[4,64,128]{2,1,0:T(8,128)S(1)} %get-tuple-element.77), channel_id=1, source_target_pairs={{0,16},{8,24},{16,0},{24,8},{1,17},{9,25},{17,1},{25,9},{2,18},{10... | collective-permute-start | bytes 393224 | tf_op jit(solution)/shard_map/ppermute | solution.py:536
  46.4 6.0 %collective-permute-start.16 = (f32[2,64,128]{2,1,0:T(8,128)S(1)}, f32[2,64,128]{2,1,0:T(8,128)S(1)}, u32[]{:S(2)}, u32[]{:S(2)}) collective-permute-start(f32[2,64,128]{2,1,0:T(8,128)S(1)} %get-tuple-element.86), channel_id=1, source_target_pairs={{0,2},{1,3},{2,0},{3,1},{4,6},{5,7},{6,4},{7,5},{8,10},{9,11},{10,... | collective-permute-start | bytes 196616 | tf_op jit(solution)/shard_map/ppermute | solution.py:536
  48.1 4.4 %collective-permute-start.17 = (f32[2,64,128]{2,1,0:T(8,128)S(1)}, f32[2,64,128]{2,1,0:T(8,128)S(1)}, u32[]{:S(2)}, u32[]{:S(2)}) collective-permute-start(f32[2,64,128]{2,1,0:T(8,128)S(1)} %get-tuple-element.87), channel_id=1, source_target_pairs={{0,2},{1,3},{2,0},{3,1},{4,6},{5,7},{6,4},{7,5},{8,10},{9,11},{10,... | collective-permute-start | bytes 196616 | tf_op jit(solution)/shard_map/ppermute | solution.py:536
  50.4 5.1 %collective-permute-start.8 = (f32[2,64,128]{2,1,0:T(8,128)S(1)}, f32[2,64,128]{2,1,0:T(8,128)S(1)}, u32[]{:S(2)}, u32[]{:S(2)}) collective-permute-start(f32[2,64,128]{2,1,0:T(8,128)S(1)} %get-tuple-element.78), channel_id=1, source_target_pairs={{0,2},{1,3},{2,0},{3,1},{4,6},{5,7},{6,4},{7,5},{8,10},{9,11},{10,... | collective-permute-start | bytes 196616 | tf_op jit(solution)/shard_map/ppermute | solution.py:536
  52.0 4.5 %collective-permute-start.9 = (f32[2,64,128]{2,1,0:T(8,128)S(1)}, f32[2,64,128]{2,1,0:T(8,128)S(1)}, u32[]{:S(2)}, u32[]{:S(2)}) collective-permute-start(f32[2,64,128]{2,1,0:T(8,128)S(1)} %get-tuple-element.79), channel_id=1, source_target_pairs={{0,2},{1,3},{2,0},{3,1},{4,6},{5,7},{6,4},{7,5},{8,10},{9,11},{10,... | collective-permute-start | bytes 196616 | tf_op jit(solution)/shard_map/ppermute | solution.py:536
  52.5 7.0 %collective-permute-start.18 = (f32[1,64,128]{2,1,0:T(8,128)S(1)}, f32[1,64,128]{2,1,0:T(8,128)S(1)}, u32[]{:S(2)}, u32[]{:S(2)}) collective-permute-start(f32[1,64,128]{2,1,0:T(8,128)S(1)} %get-tuple-element.88), channel_id=1, source_target_pairs={{0,4},{1,5},{2,6},{3,7},{4,0},{5,1},{6,2},{7,3},{8,12},{9,13},{10,... | collective-permute-start | bytes 98312 | tf_op jit(solution)/shard_map/ppermute | solution.py:536
  55.3 4.8 %collective-permute-start.19 = (f32[1,64,128]{2,1,0:T(8,128)S(1)}, f32[1,64,128]{2,1,0:T(8,128)S(1)}, u32[]{:S(2)}, u32[]{:S(2)}) collective-permute-start(f32[1,64,128]{2,1,0:T(8,128)S(1)} %get-tuple-element.89), channel_id=1, source_target_pairs={{0,4},{1,5},{2,6},{3,7},{4,0},{5,1},{6,2},{7,3},{8,12},{9,13},{10,... | collective-permute-start | bytes 98312 | tf_op jit(solution)/shard_map/ppermute | solution.py:536
  56.5 5.2 %collective-permute-start.10 = (f32[1,64,128]{2,1,0:T(8,128)S(1)}, f32[1,64,128]{2,1,0:T(8,128)S(1)}, u32[]{:S(2)}, u32[]{:S(2)}) collective-permute-start(f32[1,64,128]{2,1,0:T(8,128)S(1)} %get-tuple-element.80), channel_id=1, source_target_pairs={{0,4},{1,5},{2,6},{3,7},{4,0},{5,1},{6,2},{7,3},{8,12},{9,13},{10,... | collective-permute-start | bytes 98312 | tf_op jit(solution)/shard_map/ppermute | solution.py:536
  59.0 5.2 %collective-permute-start.11 = (f32[1,64,128]{2,1,0:T(8,128)S(1)}, f32[1,64,128]{2,1,0:T(8,128)S(1)}, u32[]{:S(2)}, u32[]{:S(2)}) collective-permute-start(f32[1,64,128]{2,1,0:T(8,128)S(1)} %get-tuple-element.81), channel_id=1, source_target_pairs={{0,4},{1,5},{2,6},{3,7},{4,0},{5,1},{6,2},{7,3},{8,12},{9,13},{10,... | collective-permute-start | bytes 98312 | tf_op jit(solution)/shard_map/ppermute | solution.py:536
  64.2 5.0 %collective-permute-start.21 = (f32[1,64,512]{2,1,0:T(8,128)S(1)}, f32[1,64,512]{2,1,0:T(8,128)S(1)}, u32[]{:S(2)}, u32[]{:S(2)}) collective-permute-start(f32[1,64,512]{2,1,0:T(8,128)S(1)} %share.1.refs_0_), channel_id=1, source_target_pairs={{0,16},{8,24},{16,0},{24,8},{1,17},{9,25},{17,1},{25,9},{2,18},{10... | collective-permute-start | bytes 393224 | tf_op jit(solution)/shard_map/ppermute | solution.py:536
  64.4 4.8 %collective-permute-start.20 = (f32[1,64,512]{2,1,0:T(8,128)S(1)}, f32[1,64,512]{2,1,0:T(8,128)S(1)}, u32[]{:S(2)}, u32[]{:S(2)}) collective-permute-start(f32[1,64,512]{2,1,0:T(8,128)S(1)} %share.1.refs_0_), channel_id=1, source_target_pairs={{0,8},{8,0},{16,24},{24,16},{1,9},{9,1},{17,25},{25,17},{2,10},{10... | collective-permute-start | bytes 393224 | tf_op jit(solution)/shard_map/ppermute | solution.py:536
  69.2 1.3 %collective-permute-start.22 = (f32[1,64,512]{2,1,0:T(8,128)S(1)}, f32[1,64,512]{2,1,0:T(8,128)S(1)}, u32[]{:S(2)}, u32[]{:S(2)}) collective-permute-start(f32[1,64,512]{2,1,0:T(8,128)S(1)} %collective-permute-done.21.refs_2_), channel_id=1, source_target_pairs={{0,8},{8,0},{16,24},{24,16},{1,9},{9,1},{17,25},{25,17},{2,10},{10... | collective-permute-start | bytes 393224 | tf_op jit(solution)/shard_map/ppermute | solution.py:536

commit v3 on v2

v3 whole, which is shorter than its diff:
```python
import functools

import jax
import jax.numpy as jnp
from jax import lax
from jax.experimental import pallas as pl
from jax.experimental.pallas import tpu as pltpu
from jax.sharding import PartitionSpec as P

CHUNKS = 8
LANES = 128
GROUP = 256
VMEM_LIMIT = 24 * 1024 * 1024
STREAMS = ((0, 2, "xyz", "yzx"), (2, 4, "xyz", "yzx"))

TWO_OVER_PI = 0.6366197723675814
PIO2_HIGH = 1.5703125
PIO2_MID = 0.0004837512969970703
PIO2_LOW = 7.549789948768648e-08


def sin_cos(angle):
    quadrant_real = jnp.floor(angle * TWO_OVER_PI + 0.5)
    rest = angle - quadrant_real * PIO2_HIGH
    rest = rest - quadrant_real * PIO2_MID
    rest = rest - quadrant_real * PIO2_LOW
    square = rest * rest
    sine = rest + rest * square * (
        -1.6666654611e-1 + square * (8.3321608736e-3 + square * -1.9515295891e-4)
    )
    cosine = (
        1.0
        - 0.5 * square
        + square
        * square
        * (4.166664568298827e-2 + square * (-1.388731625493765e-3 + square * 2.443315711809948e-5))
    )
    quadrant = quadrant_real.astype(jnp.int32)
    swapped = (quadrant & 1) == 1
    sin_base = jnp.where(swapped, cosine, sine)
    cos_base = jnp.where(swapped, sine, cosine)
    sin_value = jnp.where((quadrant & 2) == 2, -sin_base, sin_base)
    cos_value = jnp.where(((quadrant + 1) & 2) == 2, -cos_base, cos_base)
    return sin_value, cos_value


def gain_of(decay):
    twice = 2.0 * decay
    series = 1.0 / 3628800.0
    for factorial in (362880.0, 40320.0, 5040.0, 720.0, 120.0, 24.0, 6.0, 2.0, 1.0):
        series = 1.0 / factorial - twice * series
    return jnp.sqrt(jnp.where(twice < 0.5, twice * series, 1.0 - jnp.exp(-twice)))


def places():
    return lax.axis_index("context"), lax.axis_index("dp")


def shuffle(back=False):
    length = GROUP // CHUNKS
    scan = lax.broadcasted_iota(jnp.int32, (GROUP, GROUP), 1 if back else 0)
    time = lax.broadcasted_iota(jnp.int32, (GROUP, GROUP), 0 if back else 1)
    return jnp.where(time == (scan % CHUNKS) * length + scan // CHUNKS, 1.0, 0.0).astype(
        jnp.bfloat16
    )


def local_scan_kernel(
    step_hbm,
    decay_hbm,
    frequency_hbm,
    in_hbm,
    cot_hbm,
    in_proj_hbm,
    out_proj_hbm,
    fwd_re,
    fwd_im,
    fwd_are,
    fwd_aim,
    back_re,
    back_im,
    back_are,
    back_aim,
    chunk_ref,
    summary_ref,
    outside_ref,
    in_vmem,
    cot_vmem,
    in_proj_vmem,
    out_proj_vmem,
    decay_ref,
    step_ref,
    frequency_ref,
    in_time,
    cot_time,
    lam_re,
    lam_im,
    drive,
    adjoint,
    sems,
):
    rows = in_vmem.shape[0]
    groups = rows // GROUP
    length = GROUP // CHUNKS
    states = decay_ref.shape[1]
    copies = [
        pltpu.make_async_copy(source, target, sems.at[slot])
        for slot, (source, target) in enumerate(
            (
                (step_hbm, step_ref),
                (decay_hbm, decay_ref),
                (frequency_hbm, frequency_ref),
                (in_hbm, in_time),
                (in_proj_hbm, in_proj_vmem),
                (cot_hbm, cot_time),
                (out_proj_hbm, out_proj_vmem),
            )
        )
    ]
    for copy in copies:
        copy.start()
    for copy in copies[:3]:
        copy.wait()
    loads = copies[3:]
    decay = decay_ref[...]
    frequency = frequency_ref[...]
    gain = gain_of(decay)
    steps = [
        jnp.concatenate(
            [
                step_ref[:, first : first + length]
                for first in range(group * GROUP, (group + 1) * GROUP, length)
            ],
            axis=0,
        )
        for group in range(groups)
    ]
    for place in range(length):
        for group in range(groups):
            here = jnp.broadcast_to(steps[group][:, place : place + 1], (CHUNKS, states))
            damping = jnp.exp(-here * decay)
            sine, cosine = sin_cos(here * frequency)
            tile = pl.ds(group * GROUP + place * CHUNKS, CHUNKS)
            lam_re[tile, :] = damping * cosine
            lam_im[tile, :] = damping * sine
    to_scan = shuffle()
    pair_gain = jnp.concatenate([gain, gain], axis=1)
    for load, time_ref, scan_ref, proj_ref, target in (
        (loads[:2], in_time, in_vmem, in_proj_vmem, drive),
        (loads[2:], cot_time, cot_vmem, out_proj_vmem, adjoint),
    ):
        load[0].wait()
        for group in range(groups):
            part = pl.ds(group * GROUP, GROUP)
            scan_ref[part, :] = jnp.dot(
                to_scan, time_ref[part, :], preferred_element_type=jnp.float32
            ).astype(jnp.bfloat16)
        load[1].wait()
        driven = jnp.dot(scan_ref[...], proj_ref[...], preferred_element_type=jnp.float32)
        target[...] = driven * pair_gain if target is drive else driven
    re_cols, im_cols = pl.ds(0, states), pl.ds(states, states)

    def body(place, carry):
        results = []
        for group in range(groups):
            f_are, f_aim, f_re, f_im, b_are, b_aim, b_re, b_im = carry[8 * group : 8 * group + 8]
            first = group * GROUP + place * CHUNKS
            tile = pl.ds(pl.multiple_of(first, CHUNKS), CHUNKS)
            l_re, l_im = lam_re[tile, :], lam_im[tile, :]
            new_are = l_re * f_are - l_im * f_aim
            new_aim = l_re * f_aim + l_im * f_are
            new_re = l_re * f_re - l_im * f_im + drive[tile, re_cols]
            new_im = l_re * f_im + l_im * f_re + drive[tile, im_cols]
            fwd_are[tile, :] = new_are
            fwd_aim[tile, :] = new_aim
            fwd_re[tile, :] = new_re
            fwd_im[tile, :] = new_im
            first = group * GROUP + (length - 1 - place) * CHUNKS
            tile = pl.ds(pl.multiple_of(first, CHUNKS), CHUNKS)
            l_re, l_im = lam_re[tile, :], lam_im[tile, :]
            a_re = b_re + adjoint[tile, re_cols]
            a_im = b_im + adjoint[tile, im_cols]
            back_are[tile, :] = b_are
            back_aim[tile, :] = b_aim
            back_re[tile, :] = a_re
            back_im[tile, :] = a_im
            results += [
                new_are,
                new_aim,
                new_re,
                new_im,
                l_re * b_are + l_im * b_aim,
                l_re * b_aim - l_im * b_are,
                l_re * a_re + l_im * a_im,
                l_re * a_im - l_im * a_re,
            ]
        return tuple(results)

    zero = jnp.zeros((CHUNKS, states), jnp.float32)
    one = jnp.ones((CHUNKS, states), jnp.float32)
    totals = lax.fori_loop(
        0, length, body, (one, zero, zero, zero, one, zero, zero, zero) * groups, unroll=4
    )
    parts = [
        [totals[8 * group + slot] for slot in (0, 1, 2, 3, 6, 7)] for group in range(groups)
    ]
    for group in range(groups):
        for slot, part in enumerate(parts[group]):
            chunk_ref[slot, pl.ds(group * CHUNKS, CHUNKS), :] = part
    rows_of = [
        [part[chunk : chunk + 1, :] for part in parts[group]]
        for group in range(groups)
        for chunk in range(CHUNKS)
    ]
    t_are, t_aim, t_re, t_im = rows_of[0][:4]
    for l_re, l_im, d_re, d_im, _, _ in rows_of[1:]:
        t_are, t_aim = l_re * t_are - l_im * t_aim, l_re * t_aim + l_im * t_are
        t_re, t_im = l_re * t_re - l_im * t_im + d_re, l_re * t_im + l_im * t_re + d_im
    u_re, u_im = rows_of[-1][4:]
    for l_re, l_im, _, _, d_re, d_im in rows_of[-2::-1]:
        u_re, u_im = l_re * u_re + l_im * u_im + d_re, l_re * u_im - l_im * u_re + d_im
    summary_ref[...] = jnp.concatenate(
        [t_are, t_aim, t_re, t_im, u_re, u_im, t_are, t_aim], axis=0
    )
    one, zero = jnp.ones_like(t_are), jnp.zeros_like(t_are)
    outside_ref[...] = jnp.concatenate([one, zero, zero, zero] * 2, axis=0)


def held(shape, dtype=jnp.float32):
    return pltpu.VMEM(shape, dtype)


def call(kernel, name, out_shape, *args, inputs=None, outputs=None, scratch=(), flops=0):
    vmem = pl.BlockSpec(memory_space=pltpu.VMEM)
    return pl.pallas_call(
        kernel,
        out_shape=out_shape,
        in_specs=inputs or [vmem] * len(args),
        out_specs=outputs or jax.tree.map(lambda _: vmem, out_shape),
        scratch_shapes=scratch,
        compiler_params=pltpu.CompilerParams(vmem_limit_bytes=VMEM_LIMIT),
        cost_estimate=pl.CostEstimate(
            flops=flops, bytes_accessed=max(flops // 1000, 1024), transcendentals=0
        ),
        name=name,
    )(*args)


def local_scan(step_row, decay, frequency, flat_in, flat_cot, input_proj, output_proj):
    rows = flat_in.shape[0]
    states = decay.shape[1]
    args = [
        pltpu.with_memory_space_constraint(array, pltpu.HBM)
        for array in (step_row, decay, frequency, flat_in, flat_cot, input_proj, output_proj)
    ]
    return call(
        local_scan_kernel,
        "local_scan",
        [held((rows, states))] * 8
        + [held((6, rows // GROUP * CHUNKS, states)), held((8, states)), held((8, states))]
        + [held(array.shape, array.dtype) for array in args[3:]]
        + [held(decay.shape)],
        *args,
        inputs=[pl.BlockSpec(memory_space=pltpu.HBM)] * 7,
        scratch=[
            pltpu.VMEM(step_row.shape, jnp.float32),
            pltpu.VMEM(frequency.shape, jnp.float32),
            pltpu.VMEM(flat_in.shape, flat_in.dtype),
            pltpu.VMEM(flat_cot.shape, flat_cot.dtype),
            pltpu.VMEM((rows, states), jnp.float32),
            pltpu.VMEM((rows, states), jnp.float32),
            pltpu.VMEM((rows, 2 * states), jnp.float32),
            pltpu.VMEM((rows, 2 * states), jnp.float32),
            pltpu.SemaphoreType.DMA((7,)),
        ],
        flops=4 * rows * flat_in.shape[1] * 2 * states,
    )


def times(a, b):
    return a[0] * b[0] - a[1] * b[1], a[0] * b[1] + a[1] * b[0]


def times_conj(a, b):
    return a[0] * b[0] + a[1] * b[1], a[0] * b[1] - a[1] * b[0]


def plus(a, b):
    return a[0] + b[0], a[1] + b[1]


def pick(upper, a, b):
    return tuple(jnp.where(upper, x, y) for x, y in zip(a, b))


def pairs_of(array):
    return [(array[row : row + 1], array[row + 1 : row + 2]) for row in range(0, 8, 2)]


def widen(bit, outside, other):
    upper = ((lax.axis_index("context") >> bit) & 1) == 1
    below, below_sum, above, above_sum = outside
    product, forward, backward, _ = other
    return (
        pick(upper, times(below, product), below),
        pick(upper, plus(times(below, forward), below_sum), below_sum),
        pick(upper, above, times(above, product)),
        pick(upper, above_sum, plus(times_conj(above, backward), above_sum)),
    )


def combine_kernel(bit, total_ref, outside_ref, other_ref, total_out, outside_out):
    other = pairs_of(other_ref[...])
    mine = pairs_of(total_ref[...])
    outside = widen(bit, pairs_of(outside_ref[...]), other)
    outside_out[...] = jnp.concatenate([part for pair in outside for part in pair], axis=0)
    upper = ((lax.axis_index("context") >> bit) & 1) == 1
    low = [pick(upper, theirs, ours) for theirs, ours in zip(other, mine)]
    high = [pick(upper, ours, theirs) for theirs, ours in zip(other, mine)]
    product = times(low[0], high[0])
    forward = plus(times(high[0], low[1]), high[1])
    backward = plus(times_conj(low[0], high[2]), low[2])
    total_out[...] = jnp.concatenate([*product, *forward, *backward, *product], axis=0)


def states_kernel(
    bit,
    decay_ref,
    chunk_ref,
    fwd_re,
    fwd_im,
    fwd_are,
    fwd_aim,
    back_re,
    back_im,
    back_are,
    back_aim,
    outside_ref,
    other_ref,
    in_ref,
    cot_ref,
    state_ref,
    adjoint_ref,
    grad_ref,
):
    rows, states = fwd_re.shape
    groups = rows // GROUP
    dp_place = places()[1]
    gain = gain_of(decay_ref[...])
    outside = widen(bit, pairs_of(outside_ref[...]), pairs_of(other_ref[...]))
    (f_re, f_im), (b_re, b_im) = outside[1], outside[3]
    chunk_of = lambda slot, chunk: chunk_ref[slot, chunk : chunk + 1, :]
    f_starts, b_starts = [], []
    for chunk in range(groups * CHUNKS):
        f_starts.append((f_re, f_im))
        l_re, l_im = chunk_of(0, chunk), chunk_of(1, chunk)
        f_re, f_im = (
            l_re * f_re - l_im * f_im + chunk_of(2, chunk),
            l_re * f_im + l_im * f_re + chunk_of(3, chunk),
        )
    for chunk in reversed(range(groups * CHUNKS)):
        b_starts.insert(0, (b_re, b_im))
        l_re, l_im = chunk_of(0, chunk), chunk_of(1, chunk)
        b_re, b_im = (
            l_re * b_re + l_im * b_im + chunk_of(4, chunk),
            l_re * b_im - l_im * b_re + chunk_of(5, chunk),
        )
    for starts, re_ref, im_ref, are_ref, aim_ref, pairs_ref, scale in (
        (f_starts, fwd_re, fwd_im, fwd_are, fwd_aim, state_ref, None),
        (b_starts, back_re, back_im, back_are, back_aim, adjoint_ref, gain),
    ):
        for group in range(groups):
            mine = starts[group * CHUNKS : (group + 1) * CHUNKS]
            c_re = jnp.concatenate([start[0] for start in mine], axis=0)
            c_im = jnp.concatenate([start[1] for start in mine], axis=0)
            for first in range(group * GROUP, (group + 1) * GROUP, 2 * CHUNKS):
                part = pl.ds(first, 2 * CHUNKS)
                two = lambda value: jnp.concatenate([value, value], axis=0)
                a_re, a_im = are_ref[part, :], aim_ref[part, :]
                s_re = re_ref[part, :] + a_re * two(c_re) - a_im * two(c_im)
                s_im = im_ref[part, :] + a_re * two(c_im) + a_im * two(c_re)
                if scale is not None:
                    s_re, s_im = s_re * scale, s_im * scale
                pairs_ref[part, pl.ds(0, states)] = s_re.astype(jnp.bfloat16)
                pairs_ref[part, pl.ds(states, states)] = s_im.astype(jnp.bfloat16)
    grad_part(dp_place & 1 == 1, in_ref, cot_ref, state_ref, adjoint_ref, 0, grad_ref)


def grad_part(of_input, in_ref, cot_ref, state_ref, adjoint_ref, half, grad_ref):
    columns = pl.ds(half * grad_ref.shape[1], grad_ref.shape[1])
    over_rows = (((0,), (0,)), ((), ()))

    @pl.when(of_input)
    def _():
        grad_ref[...] = lax.dot_general(
            in_ref[...], adjoint_ref[:, columns], over_rows, preferred_element_type=jnp.float32
        )

    @pl.when(jnp.logical_not(of_input))
    def _():
        grad_ref[...] = lax.dot_general(
            cot_ref[...], state_ref[:, columns], over_rows, preferred_element_type=jnp.float32
        )


def grads_kernel(plan, in_ref, cot_ref, state_ref, adjoint_ref, *grad_refs):
    core = places()[1] & 1
    for (own, half), grad_ref in zip(plan, grad_refs):
        grad_part((core == 0) == own, in_ref, cot_ref, state_ref, adjoint_ref, half, grad_ref)


def grads(plan, flat_in, flat_cot, state_pairs, adjoint_pairs):
    rows, width = flat_in.shape
    states = state_pairs.shape[1] // 2
    return call(
        functools.partial(grads_kernel, plan),
        "grads",
        [held((width, states))] * len(plan),
        flat_in,
        flat_cot,
        state_pairs,
        adjoint_pairs,
        flops=2 * rows * width * states * len(plan),
    )


def global_states(bit, decay, chunk_totals, planes, outside, other, flat_in, flat_cot):
    rows, width = flat_in.shape
    states = decay.shape[1]
    return call(
        functools.partial(states_kernel, bit),
        "global_states",
        [
            held((rows, 2 * states), jnp.bfloat16),
            held((rows, 2 * states), jnp.bfloat16),
            held((width, states)),
        ],
        decay,
        chunk_totals,
        *planes,
        outside,
        other,
        flat_in,
        flat_cot,
        flops=2 * rows * width * 2 * states,
    )


def products_kernel(
    in_ref,
    cot_ref,
    state_ref,
    adjoint_ref,
    in_proj_ref,
    out_proj_ref,
    skip_ref,
    after_ref,
    out_hbm,
    back_hbm,
    token_ref,
    out_ref,
    back_ref,
    sems,
):
    over_states = (((1,), (1,)), ((), ()))
    token_ref[...] = jnp.zeros_like(token_ref)
    skip = skip_ref[...]
    to_time = shuffle(back=True)
    stores = []
    for slot, (pairs, proj, skipped, target, result) in enumerate(
        (
            (state_ref, out_proj_ref, in_ref, out_ref, out_hbm),
            (adjoint_ref, in_proj_ref, cot_ref, back_ref, back_hbm),
        )
    ):
        mixed = lax.dot_general(
            pairs[...], proj[...], over_states, preferred_element_type=jnp.float32
        )
        mixed = (mixed + skip * skipped[...].astype(jnp.float32)).astype(jnp.bfloat16)
        for first in range(0, mixed.shape[0], GROUP):
            target[pl.ds(first, GROUP), :] = jnp.dot(
                to_time, mixed[first : first + GROUP], preferred_element_type=jnp.float32
            ).astype(jnp.bfloat16)
        stores.append(pltpu.make_async_copy(target, result, sems.at[slot]))
        stores[-1].start()
    for store in stores:
        store.wait()


def products(
    flat_in, flat_cot, state_pairs, adjoint_pairs, input_proj, output_proj, skip_gain, after
):
    rows, width = flat_in.shape
    vmem = pl.BlockSpec(memory_space=pltpu.VMEM)
    hbm = pl.BlockSpec(memory_space=pltpu.HBM)
    return call(
        products_kernel,
        "products",
        [
            jax.ShapeDtypeStruct(flat_in.shape, jnp.bfloat16),
            jax.ShapeDtypeStruct(flat_in.shape, jnp.bfloat16),
            held((8, LANES)),
        ],
        flat_in,
        flat_cot,
        state_pairs,
        adjoint_pairs,
        input_proj,
        output_proj,
        skip_gain,
        after,
        inputs=[vmem] * 7 + [pl.BlockSpec(memory_space=pl.ANY)],
        outputs=[hbm, hbm, vmem],
        scratch=[
            pltpu.VMEM(flat_in.shape, jnp.bfloat16),
            pltpu.VMEM(flat_in.shape, jnp.bfloat16),
            pltpu.SemaphoreType.DMA((2,)),
        ],
        flops=4 * rows * width * state_pairs.shape[1],
    )


def own_bit(step):
    axis, bit = step
    return (lax.axis_index(axis) >> bit) & 1


def add_kernel(layouts, columns, settled, sent, scale, count, *refs):
    sources, out = refs[:count], refs[-1]
    is_zero = (lax.axis_index("dp") & 1) == 0
    indices = []
    for core in range(2):
        free = [s for s in layouts[-1][core] if s not in settled[core] and s != sent[core]]
        fixed = {step: own_bit(step) for step in settled[core]}
        if sent[core] is not None:
            fixed[sent[core]] = 1 - own_bit(sent[core])
        indices.append([])
        for block in range(2 ** len(free)):
            values = dict(fixed)
            for place, step in enumerate(free):
                values[step] = (block >> (len(free) - 1 - place)) & 1
            indices[core].append([])
            for layout in layouts:
                index = 0
                for step in layout[core]:
                    index = index * 2 + values[step]
                indices[core][-1].append(index)
    for block, both in enumerate(zip(*indices)):
        total = None
        for source, zero, one in zip(sources, *both):
            index = jnp.where(is_zero, zero, one)
            wide = source.shape[2] != columns[1] - columns[0]
            part = source[index, :, columns[0] : columns[1]] if wide else source[index]
            total = part if total is None else total + part
        out[block] = total if scale is None else total * scale


def gather_kernel(items, *refs):
    in_ref, out_ref = refs[-2:]
    dp_place = places()[1]
    for (columns, offset), share in zip(items, refs[:-2]):
        place = dp_place ^ offset
        for core, target in enumerate((in_ref, out_ref)):

            @pl.when(place & 1 == core)
            def _():
                target[place >> 1, :, columns[0] : columns[1]] = share[0]


def on_device(
    inputs, step_size, decay_rate, frequency, input_proj, output_proj, skip_gain, cotangent
):
    batch_count, row_count, model_width = inputs.shape
    state_count = decay_rate.shape[0]
    dp_count, context_count = lax.axis_size("dp"), lax.axis_size("context")
    dp_bits, context_bits = dp_count.bit_length() - 1, context_count.bit_length() - 1

    def swap(array, *steps):
        pairs = []
        for dp in range(dp_count):
            axis, bit = steps[dp & (len(steps) - 1)]
            for context in range(context_count):
                if axis == "dp":
                    partner = (dp ^ (1 << bit)) * context_count + context
                else:
                    partner = dp * context_count + (context ^ (1 << bit))
                pairs.append((dp * context_count + context, partner))
        return lax.ppermute(array, ("dp", "context"), pairs)

    *planes, chunk_totals, total, outside, flat_in, flat_cot, in_proj, out_proj, decay = local_scan(
        step_size,
        decay_rate.reshape(1, state_count),
        frequency.reshape(1, state_count),
        inputs.reshape(row_count, model_width),
        cotangent.reshape(row_count, model_width),
        input_proj,
        output_proj,
    )
    for bit in range(context_bits - 1):
        other = swap(total, ("context", bit))
        total, outside = call(
            functools.partial(combine_kernel, bit),
            "combine",
            [held(total.shape), held(outside.shape)],
            total,
            outside,
            other,
        )
    last = context_bits - 1
    state_pairs, adjoint_pairs, lent = global_states(
        last, decay, chunk_totals, planes, outside, swap(total, ("context", last)), flat_in, flat_cot
    )
    sides = (flat_in, flat_cot, state_pairs, adjoint_pairs)
    borrowed = [swap(lent, ("dp", 0))]
    kept, lent = grads(((True, 0), (False, 1)), *sides)
    borrowed.append(swap(lent, ("dp", 0)))
    kept = [kept, *grads(((True, 1),), *sides)]

    extra_bits = [("dp", bit) for bit in range(1, dp_bits)]
    piece = model_width // (context_count * dp_count // 2)
    layout = [("context", bit) for bit in reversed(range(context_bits))] + extra_bits[::-1]
    blocks = (2 ** len(layout), piece, state_count)
    grad_scale = float(batch_count * row_count * dp_count * context_count) ** (-0.5)
    z_bits = [("context", bit) for bit in range(1, context_bits)]
    y_bits = [("context", 0)]
    by_name = {"x": extra_bits, "y": y_bits, "z": z_bits, "Z": z_bits[::-1]}
    streams = []
    for first, past, *names in STREAMS:
        half = first * LANES // state_count
        columns = (first * LANES - half * state_count, past * LANES - half * state_count)
        streams.append(
            {
                "columns": columns,
                "at": first * LANES,
                "sources": [kept[half].reshape(blocks), borrowed[half].reshape(blocks)],
                "layouts": [(layout, layout)] * 2,
                "settled": ([], []),
                "orders": [[step for name in order for step in by_name[name]] for order in names],
            }
        )

    vmem, anywhere = pl.BlockSpec(memory_space=pltpu.VMEM), pl.BlockSpec(memory_space=pl.ANY)

    def add(stream, sent=(None, None), scale=None, later=()):
        free = len(layout) - len(stream["settled"][0]) - (sent[0] is not None)
        width = stream["columns"][1] - stream["columns"][0]
        return call(
            functools.partial(
                add_kernel,
                stream["layouts"],
                stream["columns"],
                stream["settled"],
                sent,
                scale,
                len(stream["sources"]),
            ),
            "halve" if scale is None else "share",
            held((2**free, piece, width)),
            *stream["sources"],
            *later,
            inputs=[vmem] * len(stream["sources"]) + [anywhere] * len(later),
        )

    token = ()
    for place in range(len(layout)):
        for stream in streams:
            steps = [order[place] for order in stream["orders"]]
            away = add(stream, steps, later=token if place == 1 else ())
            stream["settled"] = tuple(
                settled + [step] for settled, step in zip(stream["settled"], steps)
            )
            stream["sources"] = stream["sources"] + [swap(away, *steps)]
            left = tuple(
                [step for step in layout if step not in settled] for settled in stream["settled"]
            )
            stream["layouts"] = stream["layouts"] + [left]
        if place == 0:
            outputs, input_grad, *token = products(
                flat_in,
                flat_cot,
                state_pairs,
                adjoint_pairs,
                in_proj,
                out_proj,
                skip_gain.reshape(1, model_width),
                away,
            )
    items, shares = [], []
    for stream in streams:
        mine = [(0, add(stream, scale=grad_scale))]
        for bit in [bit for _, bit in extra_bits] + [0]:
            mine = mine + [
                (offset ^ (1 << bit), swap(share, ("dp", bit))) for offset, share in mine
            ]
        width = stream["columns"][1] - stream["columns"][0]
        for offset, share in mine:
            items.append(((stream["at"], stream["at"] + width), offset))
            shares.append(share)
    whole = jax.ShapeDtypeStruct((dp_count // 2, piece, 2 * state_count), jnp.float32)
    sums = call(functools.partial(gather_kernel, items), "gather", [whole, whole], *shares)
    sums = [part.reshape(model_width // context_count, 2 * state_count) for part in sums]
    return (outputs.reshape(inputs.shape), input_grad.reshape(inputs.shape), *sums)


def solution(mesh):
    in_specs = (
        P("dp", "context", None),
        P("dp", "context"),
        P(),
        P(),
        P(),
        P(),
        P(),
        P("dp", "context", None),
    )
    out_specs = (
        P("dp", "context", None),
        P("dp", "context", None),
        P("context", None),
        P("context", None),
    )
    return jax.shard_map(
        on_device, mesh=mesh, in_specs=in_specs, out_specs=out_specs, check_vma=False
    )
```

time: 71.6 us -> 63.4 us (0.89)
  waiting for transfers between devices: 30.9 us -> 20.4 us
  starting transfers between devices: 27.2 us -> 30.4 us
  Pallas kernels: 12.6 us -> 11.6 us
    ppermute x23 -> x19, waiting for transfers between devices: 30.9 us -> 20.4 us  [swap(): return lax.ppermute(array, ('dp', 'context'), pairs)]
    ppermute x23 -> x19, starting transfers between devices: 27.2 us -> 30.4 us  [swap(): return lax.ppermute(array, ('dp', 'context'), pairs)]
    pallas_call x15 -> x18, Pallas kernels: 12.6 us -> 11.6 us  [call(): pl.pallas_call(kernel, out_shape=out_shape, in_specs=inputs or [vmem] * l...]
  transfers between devices with their start and end apart: 23 -> 19, of which waited for: 17 -> 12; matrix products, arithmetic and copies ran while one was open for 0% -> 0% of each run, Pallas kernels for 4% -> 6%
where the time goes in v3:
time: 63.4 us; the launch traced here: 63.2 us
  starting transfers between devices  30.4 us (48%)
  waiting for transfers between devices  20.4 us (32%)
  Pallas kernels  11.6 us (18%)
  between operations  0.74 us (1%)
    ppermute x19, starting transfers between devices, swap(): return lax.ppermute(array, ('dp', 'context'), pairs)  30.4 us
    ppermute x19, waiting for transfers between devices, swap(): return lax.ppermute(array, ('dp', 'context'), pairs)  20.4 us
    pallas_call x18, Pallas kernels, call(): pl.pallas_call(kernel, out_shape=out_shape, in_specs=inputs or [vmem] * l...  11.6 us
  transfers between devices with their start and end apart: 19, of which 12 were waited for; matrix products, arithmetic and copies ran while one was open for 0% of the time, Pallas kernels for 6%

profile of v3, /device:TPU:0, one launch (start us, length us, event | category | flops | bytes accessed | tf_op | source)
XLA Modules:
  0.0 63.2 jit_solution(15173807346473139906)
XLA Ops:
  0.6 4.9 %local_scan.1 = (f32[512,256]{1,0:T(8,128)S(1)}, f32[512,256]{1,0:T(8,128)S(1)}, f32[512,256]{1,0:T(8,128)S(1)}, f32[512,256]{1,0:T(8,128)S(1)}, f32[512,256]{1,...) custom-call(f32[1,512]{1,0:T(1,128)} %step_hbm.1, ...), custom_call_target="tpu_custom_call" | custom-call | flops 1073741824 | bytes 1073741 | tf_op jit(solution)/shard_map/local_scan/pallas_call | solution.py:235
  5.5 3.0 %collective-permute-start = (f32[8,256]{1,0:T(8,128)S(1)}, f32[8,256]{1,0:T(8,128)S(1)}, u32[]{:S(2)}, u32[]{:S(2)}) collective-permute-start(f32[8,256]{1,0:T(8,128)S(1)} %get-tuple-element.46.total_ref), channel_id=1, source_target_pairs={{0,1},{1,0},{2,3},{3,2},{4,5},{5,4},{6,7},{7,6},{8,9},{9,8},{10,11... | collective-permute-start | bytes 24584 | tf_op jit(solution)/shard_map/ppermute | solution.py:588
  8.5 1.6 %collective-permute-done.other_ref = f32[8,256]{1,0:T(8,128)S(1)} collective-permute-done((f32[8,256]{1,0:T(8,128)S(1)}, f32[8,256]{1,0:T(8,128)S(1)}, u32[]{:S(2)}, u32[]{:S(2)}) %collective-permute-start) | collective-permute-done | bytes 8224 | tf_op jit(solution)/shard_map/ppermute | solution.py:588
  10.2 2.1 %collective-permute-start.1 = (f32[8,256]{1,0:T(8,128)S(1)}, f32[8,256]{1,0:T(8,128)S(1)}, u32[]{:S(2)}, u32[]{:S(2)}) collective-permute-start(f32[8,256]{1,0:T(8,128)S(1)} %get-tuple-element.48.total_ref), channel_id=1, source_target_pairs={{0,2},{1,3},{2,0},{3,1},{4,6},{5,7},{6,4},{7,5},{8,10},{9,11},{10,... | collective-permute-start | bytes 24584 | tf_op jit(solution)/shard_map/ppermute | solution.py:588
  12.3 1.6 %collective-permute-done.1.other_ref = f32[8,256]{1,0:T(8,128)S(1)} collective-permute-done((f32[8,256]{1,0:T(8,128)S(1)}, f32[8,256]{1,0:T(8,128)S(1)}, u32[]{:S(2)}, u32[]{:S(2)}) %collective-permute-start.1) | collective-permute-done | bytes 8224 | tf_op jit(solution)/shard_map/ppermute | solution.py:588
  14.0 3.1 %collective-permute-start.2 = (f32[8,256]{1,0:T(8,128)S(1)}, f32[8,256]{1,0:T(8,128)S(1)}, u32[]{:S(2)}, u32[]{:S(2)}) collective-permute-start(f32[8,256]{1,0:T(8,128)S(1)} %get-tuple-element.51), channel_id=1, source_target_pairs={{0,4},{1,5},{2,6},{3,7},{4,0},{5,1},{6,2},{7,3},{8,12},{9,13},{10,... | collective-permute-start | bytes 24584 | tf_op jit(solution)/shard_map/ppermute | solution.py:588
  17.1 1.6 %collective-permute-done.2.other_ref = f32[8,256]{1,0:T(8,128)S(1)} collective-permute-done((f32[8,256]{1,0:T(8,128)S(1)}, f32[8,256]{1,0:T(8,128)S(1)}, u32[]{:S(2)}, u32[]{:S(2)}) %collective-permute-start.2) | collective-permute-done | bytes 8224 | tf_op jit(solution)/shard_map/ppermute | solution.py:588
  21.9 1.6 %collective-permute-done.3 = f32[1024,256]{1,0:T(8,128)S(1)} collective-permute-done((f32[1024,256]{1,0:T(8,128)S(1)}, f32[1024,256]{1,0:T(8,128)S(1)}, u32[]{:S(2)}, u32[]{:S(2)}) %collective-permute-start.3) | collective-permute-done | bytes 1048608 | tf_op jit(solution)/shard_map/ppermute | solution.py:588
  23.6 1.9 %collective-permute-start.12 = (f32[8,64,256]{2,1,0:T(8,128)S(1)}, f32[8,64,256]{2,1,0:T(8,128)S(1)}, u32[]{:S(2)}, u32[]{:S(2)}) collective-permute-start(f32[8,64,256]{2,1,0:T(8,128)S(1)} %halve.8.after_ref), channel_id=1, source_target_pairs={{0,16},{1,17},{2,18},{3,19},{4,20},{5,21},{6,22},{7,23},{8,9},{9,8... | collective-permute-start | bytes 1572872 | tf_op jit(solution)/shard_map/ppermute | solution.py:588
  25.5 1.4 %collective-permute-start.5 = (f32[8,64,256]{2,1,0:T(8,128)S(1)}, f32[8,64,256]{2,1,0:T(8,128)S(1)}, u32[]{:S(2)}, u32[]{:S(2)}) collective-permute-start(f32[8,64,256]{2,1,0:T(8,128)S(1)} %halve.9), channel_id=1, source_target_pairs={{0,16},{1,17},{2,18},{3,19},{4,20},{5,21},{6,22},{7,23},{8,9},{9,8... | collective-permute-start | bytes 1572872 | tf_op jit(solution)/shard_map/ppermute | solution.py:588
  27.0 2.9 %products.1 = (bf16[512,1024]{1,0:T(8,128)(2,1)}, bf16[512,1024]{1,0:T(8,128)(2,1)}, f32[8,128]{1,0:T(8,128)S(1)}) custom-call(bf16[512,1024]{1,0:T(8,128)(2,1)S(1)} %get-tuple-element.34.in_ref, bf16[512,1024]{1,0:T(8,128)(2,1)S(1)} %get-tuple-element.35.cot_ref, bf16[512,512]{1,0:T(8,128)(2,1)S(1)} %get-tuple-element.52.state_ref, ...), custom_call_target="tpu_custom_call" | custom-call | flops 1073741824 | bytes 1073741 | tf_op jit(solution)/shard_map/products/pallas_call | solution.py:235
  29.9 2.9 %collective-permute-done.12.refs_2_ = f32[8,64,256]{2,1,0:T(8,128)S(1)} collective-permute-done((f32[8,64,256]{2,1,0:T(8,128)S(1)}, f32[8,64,256]{2,1,0:T(8,128)S(1)}, u32[]{:S(2)}, u32[]{:S(2)}) %collective-permute-start.12) | collective-permute-done | bytes 524320 | tf_op jit(solution)/shard_map/ppermute | solution.py:588
  32.9 1.9 %collective-permute-start.13 = (f32[4,64,256]{2,1,0:T(8,128)S(1)}, f32[4,64,256]{2,1,0:T(8,128)S(1)}, u32[]{:S(2)}, u32[]{:S(2)}) collective-permute-start(f32[4,64,256]{2,1,0:T(8,128)S(1)} %halve.13), channel_id=1, source_target_pairs={{0,1},{1,0},{2,3},{3,2},{4,5},{5,4},{6,7},{7,6},{8,10},{9,11},{10,... | collective-permute-start | bytes 786440 | tf_op jit(solution)/shard_map/ppermute | solution.py:588
  34.8 3.6 %collective-permute-done.5.refs_2_ = f32[8,64,256]{2,1,0:T(8,128)S(1)} collective-permute-done((f32[8,64,256]{2,1,0:T(8,128)S(1)}, f32[8,64,256]{2,1,0:T(8,128)S(1)}, u32[]{:S(2)}, u32[]{:S(2)}) %collective-permute-start.5) | collective-permute-done | bytes 524320 | tf_op jit(solution)/shard_map/ppermute | solution.py:588
  38.5 1.9 %collective-permute-start.6 = (f32[4,64,256]{2,1,0:T(8,128)S(1)}, f32[4,64,256]{2,1,0:T(8,128)S(1)}, u32[]{:S(2)}, u32[]{:S(2)}) collective-permute-start(f32[4,64,256]{2,1,0:T(8,128)S(1)} %halve.10), channel_id=1, source_target_pairs={{0,1},{1,0},{2,3},{3,2},{4,5},{5,4},{6,7},{7,6},{8,10},{9,11},{10,... | collective-permute-start | bytes 786440 | tf_op jit(solution)/shard_map/ppermute | solution.py:588
  40.6 1.9 %collective-permute-start.14 = (f32[2,64,256]{2,1,0:T(8,128)S(1)}, f32[2,64,256]{2,1,0:T(8,128)S(1)}, u32[]{:S(2)}, u32[]{:S(2)}) collective-permute-start(f32[2,64,256]{2,1,0:T(8,128)S(1)} %halve.14), channel_id=1, source_target_pairs={{0,2},{1,3},{2,0},{3,1},{4,6},{5,7},{6,4},{7,5},{8,12},{9,13},{10,... | collective-permute-start | bytes 393224 | tf_op jit(solution)/shard_map/ppermute | solution.py:588
  42.4 2.5 %collective-permute-done.6.refs_3_ = f32[4,64,256]{2,1,0:T(8,128)S(1)} collective-permute-done((f32[4,64,256]{2,1,0:T(8,128)S(1)}, f32[4,64,256]{2,1,0:T(8,128)S(1)}, u32[]{:S(2)}, u32[]{:S(2)}) %collective-permute-start.6) | collective-permute-done | bytes 262176 | tf_op jit(solution)/shard_map/ppermute | solution.py:588
  44.9 2.0 %collective-permute-start.7 = (f32[2,64,256]{2,1,0:T(8,128)S(1)}, f32[2,64,256]{2,1,0:T(8,128)S(1)}, u32[]{:S(2)}, u32[]{:S(2)}) collective-permute-start(f32[2,64,256]{2,1,0:T(8,128)S(1)} %halve.11), channel_id=1, source_target_pairs={{0,2},{1,3},{2,0},{3,1},{4,6},{5,7},{6,4},{7,5},{8,12},{9,13},{10,... | collective-permute-start | bytes 393224 | tf_op jit(solution)/shard_map/ppermute | solution.py:588
  47.3 2.6 %collective-permute-start.15 = (f32[1,64,256]{2,1,0:T(8,128)S(1)}, f32[1,64,256]{2,1,0:T(8,128)S(1)}, u32[]{:S(2)}, u32[]{:S(2)}) collective-permute-start(f32[1,64,256]{2,1,0:T(8,128)S(1)} %halve.15), channel_id=1, source_target_pairs={{0,4},{1,5},{2,6},{3,7},{4,0},{5,1},{6,2},{7,3},{8,24},{9,25},{10,... | collective-permute-start | bytes 196616 | tf_op jit(solution)/shard_map/ppermute | solution.py:588
  50.0 3.3 %collective-permute-start.8 = (f32[1,64,256]{2,1,0:T(8,128)S(1)}, f32[1,64,256]{2,1,0:T(8,128)S(1)}, u32[]{:S(2)}, u32[]{:S(2)}) collective-permute-start(f32[1,64,256]{2,1,0:T(8,128)S(1)} %halve.12), channel_id=1, source_target_pairs={{0,4},{1,5},{2,6},{3,7},{4,0},{5,1},{6,2},{7,3},{8,24},{9,25},{10,... | collective-permute-start | bytes 196616 | tf_op jit(solution)/shard_map/ppermute | solution.py:588
  53.3 1.4 %collective-permute-done.15.refs_5_ = f32[1,64,256]{2,1,0:T(8,128)S(1)} collective-permute-done((f32[1,64,256]{2,1,0:T(8,128)S(1)}, f32[1,64,256]{2,1,0:T(8,128)S(1)}, u32[]{:S(2)}, u32[]{:S(2)}) %collective-permute-start.15) | collective-permute-done | bytes 65568 | tf_op jit(solution)/shard_map/ppermute | solution.py:588
  54.7 1.7 %collective-permute-start.16 = (f32[1,64,256]{2,1,0:T(8,128)S(1)}, f32[1,64,256]{2,1,0:T(8,128)S(1)}, u32[]{:S(2)}, u32[]{:S(2)}) collective-permute-start(f32[1,64,256]{2,1,0:T(8,128)S(1)} %share.3.refs_4_), channel_id=1, source_target_pairs={{0,16},{1,17},{2,18},{3,19},{4,20},{5,21},{6,22},{7,23},{8,24},{9,... | collective-permute-start | bytes 196616 | tf_op jit(solution)/shard_map/ppermute | solution.py:588
  56.4 2.5 %collective-permute-start.9 = (f32[1,64,256]{2,1,0:T(8,128)S(1)}, f32[1,64,256]{2,1,0:T(8,128)S(1)}, u32[]{:S(2)}, u32[]{:S(2)}) collective-permute-start(f32[1,64,256]{2,1,0:T(8,128)S(1)} %share.2.refs_0_), channel_id=1, source_target_pairs={{0,16},{1,17},{2,18},{3,19},{4,20},{5,21},{6,22},{7,23},{8,24},{9,... | collective-permute-start | bytes 196616 | tf_op jit(solution)/shard_map/ppermute | solution.py:588
  59.4 1.7 %collective-permute-done.9.refs_1_ = f32[1,64,256]{2,1,0:T(8,128)S(1)} collective-permute-done((f32[1,64,256]{2,1,0:T(8,128)S(1)}, f32[1,64,256]{2,1,0:T(8,128)S(1)}, u32[]{:S(2)}, u32[]{:S(2)}) %collective-permute-start.9) | collective-permute-done | bytes 65568 | tf_op jit(solution)/shard_map/ppermute | solution.py:588
  (34 shorter events, 6.7 us)
Async XLA Ops:
  5.5 4.7 %collective-permute-start = (f32[8,256]{1,0:T(8,128)S(1)}, f32[8,256]{1,0:T(8,128)S(1)}, u32[]{:S(2)}, u32[]{:S(2)}) collective-permute-start(f32[8,256]{1,0:T(8,128)S(1)} %get-tuple-element.46.total_ref), channel_id=1, source_target_pairs={{0,1},{1,0},{2,3},{3,2},{4,5},{5,4},{6,7},{7,6},{8,9},{9,8},{10,11... | collective-permute-start | bytes 24584 | tf_op jit(solution)/shard_map/ppermute | solution.py:588
  10.2 3.8 %collective-permute-start.1 = (f32[8,256]{1,0:T(8,128)S(1)}, f32[8,256]{1,0:T(8,128)S(1)}, u32[]{:S(2)}, u32[]{:S(2)}) collective-permute-start(f32[8,256]{1,0:T(8,128)S(1)} %get-tuple-element.48.total_ref), channel_id=1, source_target_pairs={{0,2},{1,3},{2,0},{3,1},{4,6},{5,7},{6,4},{7,5},{8,10},{9,11},{10,... | collective-permute-start | bytes 24584 | tf_op jit(solution)/shard_map/ppermute | solution.py:588
  14.0 4.7 %collective-permute-start.2 = (f32[8,256]{1,0:T(8,128)S(1)}, f32[8,256]{1,0:T(8,128)S(1)}, u32[]{:S(2)}, u32[]{:S(2)}) collective-permute-start(f32[8,256]{1,0:T(8,128)S(1)} %get-tuple-element.51), channel_id=1, source_target_pairs={{0,4},{1,5},{2,6},{3,7},{4,0},{5,1},{6,2},{7,3},{8,12},{9,13},{10,... | collective-permute-start | bytes 24584 | tf_op jit(solution)/shard_map/ppermute | solution.py:588
  20.8 2.7 %collective-permute-start.3 = (f32[1024,256]{1,0:T(8,128)S(1)}, f32[1024,256]{1,0:T(8,128)S(1)}, u32[]{:S(2)}, u32[]{:S(2)}) collective-permute-start(f32[1024,256]{1,0:T(8,128)S(1)} %get-tuple-element.56), channel_id=1, source_target_pairs={{0,8},{1,9},{2,10},{3,11},{4,12},{5,13},{6,14},{7,15},{8,0},{9,1},... | collective-permute-start | bytes 3145736 | tf_op jit(solution)/shard_map/ppermute | solution.py:588
  20.9 4.6 %collective-permute-start.4 = (f32[1024,256]{1,0:T(8,128)S(1)}, f32[1024,256]{1,0:T(8,128)S(1)}, u32[]{:S(2)}, u32[]{:S(2)}) collective-permute-start(f32[1024,256]{1,0:T(8,128)S(1)} %get-tuple-element.60), channel_id=1, source_target_pairs={{0,8},{1,9},{2,10},{3,11},{4,12},{5,13},{6,14},{7,15},{8,0},{9,1},... | collective-permute-start | bytes 3145736 | tf_op jit(solution)/shard_map/ppermute | solution.py:588
  23.6 9.2 %collective-permute-start.12 = (f32[8,64,256]{2,1,0:T(8,128)S(1)}, f32[8,64,256]{2,1,0:T(8,128)S(1)}, u32[]{:S(2)}, u32[]{:S(2)}) collective-permute-start(f32[8,64,256]{2,1,0:T(8,128)S(1)} %halve.8.after_ref), channel_id=1, source_target_pairs={{0,16},{1,17},{2,18},{3,19},{4,20},{5,21},{6,22},{7,23},{8,9},{9,8... | collective-permute-start | bytes 1572872 | tf_op jit(solution)/shard_map/ppermute | solution.py:588
  25.5 1.5 %copy-start = (f32[1024]{0:T(1024)S(1)}, f32[1024]{0:T(1024)}, u32[]{:S(2)}) copy-start(f32[1024]{0:T(1024)} %param.14) | copy-start | bytes 12292
  25.5 12.9 %collective-permute-start.5 = (f32[8,64,256]{2,1,0:T(8,128)S(1)}, f32[8,64,256]{2,1,0:T(8,128)S(1)}, u32[]{:S(2)}, u32[]{:S(2)}) collective-permute-start(f32[8,64,256]{2,1,0:T(8,128)S(1)} %halve.9), channel_id=1, source_target_pairs={{0,16},{1,17},{2,18},{3,19},{4,20},{5,21},{6,22},{7,23},{8,9},{9,8... | collective-permute-start | bytes 1572872 | tf_op jit(solution)/shard_map/ppermute | solution.py:588
  32.9 7.7 %collective-permute-start.13 = (f32[4,64,256]{2,1,0:T(8,128)S(1)}, f32[4,64,256]{2,1,0:T(8,128)S(1)}, u32[]{:S(2)}, u32[]{:S(2)}) collective-permute-start(f32[4,64,256]{2,1,0:T(8,128)S(1)} %halve.13), channel_id=1, source_target_pairs={{0,1},{1,0},{2,3},{3,2},{4,5},{5,4},{6,7},{7,6},{8,10},{9,11},{10,... | collective-permute-start | bytes 786440 | tf_op jit(solution)/shard_map/ppermute | solution.py:588
  38.5 6.4 %collective-permute-start.6 = (f32[4,64,256]{2,1,0:T(8,128)S(1)}, f32[4,64,256]{2,1,0:T(8,128)S(1)}, u32[]{:S(2)}, u32[]{:S(2)}) collective-permute-start(f32[4,64,256]{2,1,0:T(8,128)S(1)} %halve.10), channel_id=1, source_target_pairs={{0,1},{1,0},{2,3},{3,2},{4,5},{5,4},{6,7},{7,6},{8,10},{9,11},{10,... | collective-permute-start | bytes 786440 | tf_op jit(solution)/shard_map/ppermute | solution.py:588
  40.6 6.7 %collective-permute-start.14 = (f32[2,64,256]{2,1,0:T(8,128)S(1)}, f32[2,64,256]{2,1,0:T(8,128)S(1)}, u32[]{:S(2)}, u32[]{:S(2)}) collective-permute-start(f32[2,64,256]{2,1,0:T(8,128)S(1)} %halve.14), channel_id=1, source_target_pairs={{0,2},{1,3},{2,0},{3,1},{4,6},{5,7},{6,4},{7,5},{8,12},{9,13},{10,... | collective-permute-start | bytes 393224 | tf_op jit(solution)/shard_map/ppermute | solution.py:588
  44.9 5.0 %collective-permute-start.7 = (f32[2,64,256]{2,1,0:T(8,128)S(1)}, f32[2,64,256]{2,1,0:T(8,128)S(1)}, u32[]{:S(2)}, u32[]{:S(2)}) collective-permute-start(f32[2,64,256]{2,1,0:T(8,128)S(1)} %halve.11), channel_id=1, source_target_pairs={{0,2},{1,3},{2,0},{3,1},{4,6},{5,7},{6,4},{7,5},{8,12},{9,13},{10,... | collective-permute-start | bytes 393224 | tf_op jit(solution)/shard_map/ppermute | solution.py:588
  47.3 7.3 %collective-permute-start.15 = (f32[1,64,256]{2,1,0:T(8,128)S(1)}, f32[1,64,256]{2,1,0:T(8,128)S(1)}, u32[]{:S(2)}, u32[]{:S(2)}) collective-permute-start(f32[1,64,256]{2,1,0:T(8,128)S(1)} %halve.15), channel_id=1, source_target_pairs={{0,4},{1,5},{2,6},{3,7},{4,0},{5,1},{6,2},{7,3},{8,24},{9,25},{10,... | collective-permute-start | bytes 196616 | tf_op jit(solution)/shard_map/ppermute | solution.py:588
  50.0 6.4 %collective-permute-start.8 = (f32[1,64,256]{2,1,0:T(8,128)S(1)}, f32[1,64,256]{2,1,0:T(8,128)S(1)}, u32[]{:S(2)}, u32[]{:S(2)}) collective-permute-start(f32[1,64,256]{2,1,0:T(8,128)S(1)} %halve.12), channel_id=1, source_target_pairs={{0,4},{1,5},{2,6},{3,7},{4,0},{5,1},{6,2},{7,3},{8,24},{9,25},{10,... | collective-permute-start | bytes 196616 | tf_op jit(solution)/shard_map/ppermute | solution.py:588
  54.7 4.7 %collective-permute-start.16 = (f32[1,64,256]{2,1,0:T(8,128)S(1)}, f32[1,64,256]{2,1,0:T(8,128)S(1)}, u32[]{:S(2)}, u32[]{:S(2)}) collective-permute-start(f32[1,64,256]{2,1,0:T(8,128)S(1)} %share.3.refs_4_), channel_id=1, source_target_pairs={{0,16},{1,17},{2,18},{3,19},{4,20},{5,21},{6,22},{7,23},{8,24},{9,... | collective-permute-start | bytes 196616 | tf_op jit(solution)/shard_map/ppermute | solution.py:588
  56.4 4.7 %collective-permute-start.9 = (f32[1,64,256]{2,1,0:T(8,128)S(1)}, f32[1,64,256]{2,1,0:T(8,128)S(1)}, u32[]{:S(2)}, u32[]{:S(2)}) collective-permute-start(f32[1,64,256]{2,1,0:T(8,128)S(1)} %share.2.refs_0_), channel_id=1, source_target_pairs={{0,16},{1,17},{2,18},{3,19},{4,20},{5,21},{6,22},{7,23},{8,24},{9,... | collective-permute-start | bytes 196616 | tf_op jit(solution)/shard_map/ppermute | solution.py:588
  58.9 2.3 %collective-permute-start.17 = (f32[1,64,256]{2,1,0:T(8,128)S(1)}, f32[1,64,256]{2,1,0:T(8,128)S(1)}, u32[]{:S(2)}, u32[]{:S(2)}) collective-permute-start(f32[1,64,256]{2,1,0:T(8,128)S(1)} %share.3.refs_4_), channel_id=1, source_target_pairs={{0,8},{1,9},{2,10},{3,11},{4,12},{5,13},{6,14},{7,15},{8,0},{9,1},... | collective-permute-start | bytes 196616 | tf_op jit(solution)/shard_map/ppermute | solution.py:588
  58.9 2.3 %collective-permute-start.10 = (f32[1,64,256]{2,1,0:T(8,128)S(1)}, f32[1,64,256]{2,1,0:T(8,128)S(1)}, u32[]{:S(2)}, u32[]{:S(2)}) collective-permute-start(f32[1,64,256]{2,1,0:T(8,128)S(1)} %share.2.refs_0_), channel_id=1, source_target_pairs={{0,8},{1,9},{2,10},{3,11},{4,12},{5,13},{6,14},{7,15},{8,0},{9,1},... | collective-permute-start | bytes 196616 | tf_op jit(solution)/shard_map/ppermute | solution.py:588
  59.4 1.7 %collective-permute-start.18 = (f32[1,64,256]{2,1,0:T(8,128)S(1)}, f32[1,64,256]{2,1,0:T(8,128)S(1)}, u32[]{:S(2)}, u32[]{:S(2)}) collective-permute-start(f32[1,64,256]{2,1,0:T(8,128)S(1)} %collective-permute-done.16.refs_5_), channel_id=1, source_target_pairs={{0,8},{1,9},{2,10},{3,11},{4,12},{5,13},{6,14},{7,15},{8,0},{9,1},... | collective-permute-start | bytes 196616 | tf_op jit(solution)/shard_map/ppermute | solution.py:588
  61.1 1.3 %collective-permute-start.11 = (f32[1,64,256]{2,1,0:T(8,128)S(1)}, f32[1,64,256]{2,1,0:T(8,128)S(1)}, u32[]{:S(2)}, u32[]{:S(2)}) collective-permute-start(f32[1,64,256]{2,1,0:T(8,128)S(1)} %collective-permute-done.9.refs_1_), channel_id=1, source_target_pairs={{0,8},{1,9},{2,10},{3,11},{4,12},{5,13},{6,14},{7,15},{8,0},{9,1},... | collective-permute-start | bytes 196616 | tf_op jit(solution)/shard_map/ppermute | solution.py:588

commit v4 on v3

v4 whole, which is shorter than its diff:
```python
import functools

import jax
import jax.numpy as jnp
from jax import lax
from jax.experimental import pallas as pl
from jax.experimental.pallas import tpu as pltpu
from jax.sharding import PartitionSpec as P

CHUNKS = 8
LANES = 128
GROUP = 256
LOAD_PIECES = 1
VMEM_LIMIT = 24 * 1024 * 1024
STREAMS = ((3, "xyz", "yzx"), (6, "xyz", "yzx"), (8, "xyz", "yzx"))

TWO_OVER_PI = 0.6366197723675814
PIO2_HIGH = 1.5703125
PIO2_MID = 0.0004837512969970703
PIO2_LOW = 7.549789948768648e-08


def sin_cos(angle):
    quadrant_real = jnp.floor(angle * TWO_OVER_PI + 0.5)
    rest = angle - quadrant_real * PIO2_HIGH
    rest = rest - quadrant_real * PIO2_MID
    rest = rest - quadrant_real * PIO2_LOW
    square = rest * rest
    sine = rest + rest * square * (
        -1.6666654611e-1 + square * (8.3321608736e-3 + square * -1.9515295891e-4)
    )
    cosine = (
        1.0
        - 0.5 * square
        + square
        * square
        * (4.166664568298827e-2 + square * (-1.388731625493765e-3 + square * 2.443315711809948e-5))
    )
    quadrant = quadrant_real.astype(jnp.int32)
    swapped = (quadrant & 1) == 1
    sin_base = jnp.where(swapped, cosine, sine)
    cos_base = jnp.where(swapped, sine, cosine)
    sin_value = jnp.where((quadrant & 2) == 2, -sin_base, sin_base)
    cos_value = jnp.where(((quadrant + 1) & 2) == 2, -cos_base, cos_base)
    return sin_value, cos_value


def gain_of(decay):
    twice = 2.0 * decay
    series = 1.0 / 3628800.0
    for factorial in (362880.0, 40320.0, 5040.0, 720.0, 120.0, 24.0, 6.0, 2.0, 1.0):
        series = 1.0 / factorial - twice * series
    return jnp.sqrt(jnp.where(twice < 0.5, twice * series, 1.0 - jnp.exp(-twice)))


def places():
    return lax.axis_index("context"), lax.axis_index("dp")


def shuffle(back=False):
    length = GROUP // CHUNKS
    scan = lax.broadcasted_iota(jnp.int32, (GROUP, GROUP), 1 if back else 0)
    time = lax.broadcasted_iota(jnp.int32, (GROUP, GROUP), 0 if back else 1)
    return jnp.where(time == (scan % CHUNKS) * length + scan // CHUNKS, 1.0, 0.0).astype(
        jnp.bfloat16
    )


def local_scan_kernel(
    step_hbm,
    decay_hbm,
    frequency_hbm,
    in_hbm,
    cot_hbm,
    in_proj_hbm,
    out_proj_hbm,
    lam_re,
    lam_im,
    drive,
    adjoint,
    chunk_ref,
    summary_ref,
    outside_ref,
    in_vmem,
    cot_vmem,
    in_proj_vmem,
    out_proj_vmem,
    decay_ref,
    step_ref,
    frequency_ref,
    in_time,
    cot_time,
    sems,
):
    rows = in_vmem.shape[0]
    groups = rows // GROUP
    length = GROUP // CHUNKS
    states = decay_ref.shape[1]
    small = [
        pltpu.make_async_copy(source, target, sems.at[slot])
        for slot, (source, target) in enumerate(
            ((step_hbm, step_ref), (decay_hbm, decay_ref), (frequency_hbm, frequency_ref))
        )
    ]
    loads = []
    for array, (source, target) in enumerate(
        (
            (in_hbm, in_time),
            (in_proj_hbm, in_proj_vmem),
            (cot_hbm, cot_time),
            (out_proj_hbm, out_proj_vmem),
        )
    ):
        count = source.shape[0] // LOAD_PIECES
        loads.append(
            [
                pltpu.make_async_copy(
                    source.at[pl.ds(piece * count, count)],
                    target.at[pl.ds(piece * count, count)],
                    sems.at[3 + array * LOAD_PIECES + piece],
                )
                for piece in range(LOAD_PIECES)
            ]
        )
    for copy in small + [copy for load in loads[:2] for copy in load]:
        copy.start()
    for copy in small:
        copy.wait()
    decay = decay_ref[...]
    frequency = frequency_ref[...]
    gain = gain_of(decay)
    steps = [
        jnp.concatenate(
            [
                step_ref[:, first : first + length]
                for first in range(group * GROUP, (group + 1) * GROUP, length)
            ],
            axis=0,
        )
        for group in range(groups)
    ]
    for place in range(length):
        for group in range(groups):
            here = jnp.broadcast_to(steps[group][:, place : place + 1], (CHUNKS, states))
            damping = jnp.exp(-here * decay)
            sine, cosine = sin_cos(here * frequency)
            tile = pl.ds(group * GROUP + place * CHUNKS, CHUNKS)
            lam_re[tile, :] = damping * cosine
            lam_im[tile, :] = damping * sine
    for copy in [copy for load in loads[2:] for copy in load]:
        copy.start()
    to_scan = shuffle()
    pair_gain = jnp.concatenate([gain, gain], axis=1)
    for load, time_ref, scan_ref, proj_ref, target in (
        (loads[:2], in_time, in_vmem, in_proj_vmem, drive),
        (loads[2:], cot_time, cot_vmem, out_proj_vmem, adjoint),
    ):
        for copy in load[0]:
            copy.wait()
        for group in range(groups):
            part = pl.ds(group * GROUP, GROUP)
            scan_ref[part, :] = jnp.dot(
                to_scan, time_ref[part, :], preferred_element_type=jnp.float32
            ).astype(jnp.bfloat16)
        for copy in load[1]:
            copy.wait()
        driven = jnp.dot(scan_ref[...], proj_ref[...], preferred_element_type=jnp.float32)
        target[...] = driven * pair_gain if target is drive else driven
    re_cols, im_cols = pl.ds(0, states), pl.ds(states, states)

    def body(place, carry):
        results = []
        for group in range(groups):
            a_re, a_im, f_re, f_im, b_re, b_im = carry[6 * group : 6 * group + 6]
            first = group * GROUP + place * CHUNKS
            tile = pl.ds(pl.multiple_of(first, CHUNKS), CHUNKS)
            lam = lam_re[tile, :], lam_im[tile, :]
            a_re, a_im = times(lam, (a_re, a_im))
            f_re, f_im = plus(times(lam, (f_re, f_im)), (drive[tile, re_cols], drive[tile, im_cols]))
            added = times_conj((a_re, a_im), (adjoint[tile, re_cols], adjoint[tile, im_cols]))
            results += [a_re, a_im, f_re, f_im, b_re + added[0], b_im + added[1]]
        return tuple(results)

    zero = jnp.zeros((CHUNKS, states), jnp.float32)
    one = jnp.ones((CHUNKS, states), jnp.float32)
    totals = lax.fori_loop(0, length, body, (one, zero, zero, zero, zero, zero) * groups, unroll=4)
    parts = [totals[6 * group : 6 * group + 6] for group in range(groups)]
    for group in range(groups):
        for slot, part in enumerate(parts[group]):
            chunk_ref[slot, pl.ds(group * CHUNKS, CHUNKS), :] = part
    rows_of = [
        [part[chunk : chunk + 1, :] for part in parts[group]]
        for group in range(groups)
        for chunk in range(CHUNKS)
    ]
    t_are, t_aim, t_re, t_im = rows_of[0][:4]
    for l_re, l_im, d_re, d_im, _, _ in rows_of[1:]:
        t_are, t_aim = l_re * t_are - l_im * t_aim, l_re * t_aim + l_im * t_are
        t_re, t_im = l_re * t_re - l_im * t_im + d_re, l_re * t_im + l_im * t_re + d_im
    u_re, u_im = rows_of[-1][4:]
    for l_re, l_im, _, _, d_re, d_im in rows_of[-2::-1]:
        u_re, u_im = l_re * u_re + l_im * u_im + d_re, l_re * u_im - l_im * u_re + d_im
    summary_ref[...] = jnp.concatenate(
        [t_are, t_aim, t_re, t_im, u_re, u_im, t_are, t_aim], axis=0
    )
    one, zero = jnp.ones_like(t_are), jnp.zeros_like(t_are)
    outside_ref[...] = jnp.concatenate([one, zero, zero, zero] * 2, axis=0)


def held(shape, dtype=jnp.float32):
    return pltpu.VMEM(shape, dtype)


def call(kernel, name, out_shape, *args, inputs=None, outputs=None, scratch=(), flops=0):
    vmem = pl.BlockSpec(memory_space=pltpu.VMEM)
    return pl.pallas_call(
        kernel,
        out_shape=out_shape,
        in_specs=inputs or [vmem] * len(args),
        out_specs=outputs or jax.tree.map(lambda _: vmem, out_shape),
        scratch_shapes=scratch,
        compiler_params=pltpu.CompilerParams(vmem_limit_bytes=VMEM_LIMIT),
        cost_estimate=pl.CostEstimate(
            flops=flops, bytes_accessed=max(flops // 1000, 1024), transcendentals=0
        ),
        name=name,
    )(*args)


def local_scan(step_row, decay, frequency, flat_in, flat_cot, input_proj, output_proj):
    rows = flat_in.shape[0]
    states = decay.shape[1]
    args = [
        pltpu.with_memory_space_constraint(array, pltpu.HBM)
        for array in (step_row, decay, frequency, flat_in, flat_cot, input_proj, output_proj)
    ]
    return call(
        local_scan_kernel,
        "local_scan",
        [held((rows, states))] * 2
        + [held((rows, 2 * states))] * 2
        + [held((6, rows // GROUP * CHUNKS, states)), held((8, states)), held((8, states))]
        + [held(array.shape, array.dtype) for array in args[3:]]
        + [held(decay.shape)],
        *args,
        inputs=[pl.BlockSpec(memory_space=pltpu.HBM)] * 7,
        scratch=[
            pltpu.VMEM(step_row.shape, jnp.float32),
            pltpu.VMEM(frequency.shape, jnp.float32),
            pltpu.VMEM(flat_in.shape, flat_in.dtype),
            pltpu.VMEM(flat_cot.shape, flat_cot.dtype),
            pltpu.SemaphoreType.DMA((3 + 4 * LOAD_PIECES,)),
        ],
        flops=4 * rows * flat_in.shape[1] * 2 * states,
    )


def planes_kernel(skipped, lam_re, lam_im, drive, adjoint, *rest):
    fwd_re, fwd_im, fwd_are, fwd_aim, back_re, back_im, back_are, back_aim = rest[skipped:]
    rows, states = lam_re.shape
    groups, length = rows // GROUP, GROUP // CHUNKS
    re_cols, im_cols = pl.ds(0, states), pl.ds(states, states)

    def body(place, carry):
        results = []
        for group in range(groups):
            f_are, f_aim, f_re, f_im, b_are, b_aim, b_re, b_im = carry[8 * group : 8 * group + 8]
            first = group * GROUP + place * CHUNKS
            tile = pl.ds(pl.multiple_of(first, CHUNKS), CHUNKS)
            l_re, l_im = lam_re[tile, :], lam_im[tile, :]
            new_are = l_re * f_are - l_im * f_aim
            new_aim = l_re * f_aim + l_im * f_are
            new_re = l_re * f_re - l_im * f_im + drive[tile, re_cols]
            new_im = l_re * f_im + l_im * f_re + drive[tile, im_cols]
            fwd_are[tile, :] = new_are
            fwd_aim[tile, :] = new_aim
            fwd_re[tile, :] = new_re
            fwd_im[tile, :] = new_im
            first = group * GROUP + (length - 1 - place) * CHUNKS
            tile = pl.ds(pl.multiple_of(first, CHUNKS), CHUNKS)
            l_re, l_im = lam_re[tile, :], lam_im[tile, :]
            a_re = b_re + adjoint[tile, re_cols]
            a_im = b_im + adjoint[tile, im_cols]
            back_are[tile, :] = b_are
            back_aim[tile, :] = b_aim
            back_re[tile, :] = a_re
            back_im[tile, :] = a_im
            results += [
                new_are,
                new_aim,
                new_re,
                new_im,
                l_re * b_are + l_im * b_aim,
                l_re * b_aim - l_im * b_are,
                l_re * a_re + l_im * a_im,
                l_re * a_im - l_im * a_re,
            ]
        return tuple(results)

    zero = jnp.zeros((CHUNKS, states), jnp.float32)
    one = jnp.ones((CHUNKS, states), jnp.float32)
    lax.fori_loop(
        0, length, body, (one, zero, zero, zero, one, zero, zero, zero) * groups, unroll=4
    )


def planes_of(lam_re, lam_im, drive, adjoint, *after):
    vmem = pl.BlockSpec(memory_space=pltpu.VMEM)
    return call(
        functools.partial(planes_kernel, len(after)),
        "planes",
        [held(lam_re.shape)] * 8,
        lam_re,
        lam_im,
        drive,
        adjoint,
        *after,
        inputs=[vmem] * 4 + [pl.BlockSpec(memory_space=pl.ANY)] * len(after),
    )


def times(a, b):
    return a[0] * b[0] - a[1] * b[1], a[0] * b[1] + a[1] * b[0]


def times_conj(a, b):
    return a[0] * b[0] + a[1] * b[1], a[0] * b[1] - a[1] * b[0]


def plus(a, b):
    return a[0] + b[0], a[1] + b[1]


def pick(upper, a, b):
    return tuple(jnp.where(upper, x, y) for x, y in zip(a, b))


def pairs_of(array):
    return [(array[row : row + 1], array[row + 1 : row + 2]) for row in range(0, 8, 2)]


def widen(bit, outside, other):
    upper = ((lax.axis_index("context") >> bit) & 1) == 1
    below, below_sum, above, above_sum = outside
    product, forward, backward, _ = other
    return (
        pick(upper, times(below, product), below),
        pick(upper, plus(times(below, forward), below_sum), below_sum),
        pick(upper, above, times(above, product)),
        pick(upper, above_sum, plus(times_conj(above, backward), above_sum)),
    )


def combine_kernel(bit, total_ref, outside_ref, other_ref, total_out, outside_out):
    other = pairs_of(other_ref[...])
    mine = pairs_of(total_ref[...])
    outside = widen(bit, pairs_of(outside_ref[...]), other)
    outside_out[...] = jnp.concatenate([part for pair in outside for part in pair], axis=0)
    upper = ((lax.axis_index("context") >> bit) & 1) == 1
    low = [pick(upper, theirs, ours) for theirs, ours in zip(other, mine)]
    high = [pick(upper, ours, theirs) for theirs, ours in zip(other, mine)]
    product = times(low[0], high[0])
    forward = plus(times(high[0], low[1]), high[1])
    backward = plus(times_conj(low[0], high[2]), low[2])
    total_out[...] = jnp.concatenate([*product, *forward, *backward, *product], axis=0)


def pairs_into(forward, chunk_ref, outside, gain, re_ref, im_ref, are_ref, aim_ref, pairs_ref):
    rows, states = re_ref.shape
    groups = rows // GROUP
    c_re, c_im = outside[1] if forward else outside[3]
    starts = {}
    chunks = range(groups * CHUNKS)
    for chunk in chunks if forward else reversed(chunks):
        starts[chunk] = (c_re, c_im)
        part = lambda slot: chunk_ref[slot, chunk : chunk + 1, :]
        factor, added = (part(0), part(1)), (part(2), part(3)) if forward else (part(4), part(5))
        c_re, c_im = plus((times if forward else times_conj)(factor, (c_re, c_im)), added)
    for group in range(groups):
        mine = [starts[group * CHUNKS + chunk] for chunk in range(CHUNKS)]
        c_re = jnp.concatenate([start[0] for start in mine] * 2, axis=0)
        c_im = jnp.concatenate([start[1] for start in mine] * 2, axis=0)
        for first in range(group * GROUP, (group + 1) * GROUP, 2 * CHUNKS):
            part = pl.ds(first, 2 * CHUNKS)
            a_re, a_im = are_ref[part, :], aim_ref[part, :]
            s_re = re_ref[part, :] + a_re * c_re - a_im * c_im
            s_im = im_ref[part, :] + a_re * c_im + a_im * c_re
            if not forward:
                s_re, s_im = s_re * gain, s_im * gain
            pairs_ref[part, pl.ds(0, states)] = s_re.astype(jnp.bfloat16)
            pairs_ref[part, pl.ds(states, states)] = s_im.astype(jnp.bfloat16)


def side_kernel(own, bit, parts, skipped, *refs):
    decay_ref, chunk_ref, *planes_refs = refs[:10]
    outside_ref, other_ref, in_ref, cot_ref = refs[10:14]
    pairs_ref, *outs, grad_ref = refs[14 + skipped :]
    core = places()[1] & 1
    of_input = core == (0 if own else 1)
    outside = widen(bit, pairs_of(outside_ref[...]), pairs_of(other_ref[...]))
    over_rows = (((0,), (0,)), ((), ()))
    for forward, rows_ref, planes in (
        (True, cot_ref, planes_refs[:4]),
        (False, in_ref, planes_refs[4:]),
    ):

        @pl.when(of_input != forward)
        def _():
            gain = gain_of(decay_ref[...])
            pairs_into(forward, chunk_ref, outside, gain, *planes, pairs_ref)
            grad_ref[...] = lax.dot_general(
                rows_ref[...], pairs_ref[...], over_rows, preferred_element_type=jnp.float32
            ).reshape(grad_ref.shape)

    for (layout, steps, far, first, past), out in zip(parts, outs):
        for block, both in enumerate(
            zip(*(block_indices(layout, [], step, far) for step in steps[::-1]))
        ):
            out[block] = grad_ref[jnp.where(core == 0, *both), first:past, :]


def side(own, bit, parts, piece, decay, chunk_totals, planes, outside, other, flat_in, flat_cot, after):
    rows, width = flat_in.shape
    states = decay.shape[1]
    args = [decay, chunk_totals, *planes, outside, other, flat_in, flat_cot, *after]
    blocks = (width // piece, piece, 2 * states)
    vmem = pl.BlockSpec(memory_space=pltpu.VMEM)
    shapes = [held((rows, 2 * states), jnp.bfloat16)]
    if own:
        shapes.append(held(blocks))
    for _, _, _, first, past in parts:
        shapes.append(held((blocks[0] // 2, past - first, 2 * states)))
    return call(
        functools.partial(side_kernel, own, bit, parts, len(after)),
        "kept" if own else "lent",
        shapes,
        *args,
        inputs=[vmem] * (len(args) - len(after)) + [pl.BlockSpec(memory_space=pl.ANY)] * len(after),
        scratch=() if own else (pltpu.VMEM(blocks, jnp.float32),),
        flops=2 * rows * width * 2 * states,
    )


def products_kernel(
    in_ref,
    cot_ref,
    lent_ref,
    kept_ref,
    in_proj_ref,
    out_proj_ref,
    skip_ref,
    after_ref,
    out_hbm,
    back_hbm,
    token_ref,
    out_ref,
    back_ref,
    sems,
):
    token_ref[...] = jnp.zeros_like(token_ref)
    over_states = (((1,), (1,)), ((), ()))
    skip = skip_ref[...]
    to_time = shuffle(back=True)
    core = places()[1] & 1
    stores = [
        pltpu.make_async_copy(out_ref, out_hbm, sems.at[0]),
        pltpu.make_async_copy(back_ref, back_hbm, sems.at[1]),
    ]
    for slot, (proj, skipped, target) in enumerate(
        ((out_proj_ref, in_ref, out_ref), (in_proj_ref, cot_ref, back_ref))
    ):
        for which, pairs in enumerate((lent_ref, kept_ref)):

            @pl.when((core == slot) == (which == 0))
            def _():
                mixed = lax.dot_general(
                    pairs[...], proj[...], over_states, preferred_element_type=jnp.float32
                )
                mixed = (mixed + skip * skipped[...].astype(jnp.float32)).astype(jnp.bfloat16)
                for first in range(0, mixed.shape[0], GROUP):
                    target[pl.ds(first, GROUP), :] = jnp.dot(
                        to_time, mixed[first : first + GROUP], preferred_element_type=jnp.float32
                    ).astype(jnp.bfloat16)

        stores[slot].start()
    for store in stores:
        store.wait()


def products(
    flat_in, flat_cot, lent_pairs, kept_pairs, input_proj, output_proj, skip_gain, after
):
    rows, width = flat_in.shape
    vmem = pl.BlockSpec(memory_space=pltpu.VMEM)
    hbm = pl.BlockSpec(memory_space=pltpu.HBM)
    return call(
        products_kernel,
        "products",
        [
            jax.ShapeDtypeStruct(flat_in.shape, jnp.bfloat16),
            jax.ShapeDtypeStruct(flat_in.shape, jnp.bfloat16),
            held((8, LANES)),
        ],
        flat_in,
        flat_cot,
        lent_pairs,
        kept_pairs,
        input_proj,
        output_proj,
        skip_gain,
        after,
        inputs=[vmem] * 7 + [pl.BlockSpec(memory_space=pl.ANY)],
        outputs=[hbm, hbm, vmem],
        scratch=[
            pltpu.VMEM(flat_in.shape, jnp.bfloat16),
            pltpu.VMEM(flat_in.shape, jnp.bfloat16),
            pltpu.SemaphoreType.DMA((2,)),
        ],
        flops=4 * rows * width * lent_pairs.shape[1],
    )


def own_bit(step):
    axis, bit = step
    return (lax.axis_index(axis) >> bit) & 1


def block_indices(layout, settled, sent, far, sources=None):
    values = {step: own_bit(step) for step in settled}
    if sent is not None:
        values[sent] = 1 - own_bit(sent) if far else own_bit(sent)
    free = [step for step in layout if step not in values]
    found = []
    for block in range(2 ** len(free)):
        for place, step in enumerate(free):
            values[step] = (block >> (len(free) - 1 - place)) & 1
        indices = []
        for source in sources or [layout]:
            index = 0
            for step in source:
                index = index * 2 + values[step]
            indices.append(index)
        found.append(indices if sources else indices[0])
    return found


def add_kernel(layout, layouts, rows, settled, sent, scale, count, *refs):
    sources, out = refs[:count], refs[-1]
    is_zero = (lax.axis_index("dp") & 1) == 0
    indices = [
        block_indices(layout, settled[core], sent[core], True, layouts[core]) for core in range(2)
    ]
    for block, both in enumerate(zip(*indices)):
        total = None
        for source, zero, one in zip(sources, *both):
            index = jnp.where(is_zero, zero, one)
            whole = source.shape[1] == rows[1] - rows[0]
            part = source[index] if whole else source[index, rows[0] : rows[1], :]
            total = part if total is None else total + part
        out[block] = total if scale is None else total * scale


def gather_kernel(items, *refs):
    in_ref, out_ref = refs[-2:]
    dp_place = places()[1]
    for (rows, offset), share in zip(items, refs[:-2]):
        place = dp_place ^ offset
        for core, target in enumerate((in_ref, out_ref)):

            @pl.when(place & 1 == core)
            def _():
                target[place >> 1, rows[0] : rows[1], :] = share[0]


def on_device(
    inputs, step_size, decay_rate, frequency, input_proj, output_proj, skip_gain, cotangent
):
    batch_count, row_count, model_width = inputs.shape
    state_count = decay_rate.shape[0]
    dp_count, context_count = lax.axis_size("dp"), lax.axis_size("context")
    dp_bits, context_bits = dp_count.bit_length() - 1, context_count.bit_length() - 1

    def swap(array, *steps):
        pairs = []
        for dp in range(dp_count):
            axis, bit = steps[dp & (len(steps) - 1)]
            for context in range(context_count):
                if axis == "dp":
                    partner = (dp ^ (1 << bit)) * context_count + context
                else:
                    partner = dp * context_count + (context ^ (1 << bit))
                pairs.append((dp * context_count + context, partner))
        return lax.ppermute(array, ("dp", "context"), pairs)

    *driven, chunk_totals, total, outside, flat_in, flat_cot, in_proj, out_proj, decay = local_scan(
        step_size,
        decay_rate.reshape(1, state_count),
        frequency.reshape(1, state_count),
        inputs.reshape(row_count, model_width),
        cotangent.reshape(row_count, model_width),
        input_proj,
        output_proj,
    )
    for bit in range(context_bits - 1):
        other = swap(total, ("context", bit))
        total, outside = call(
            functools.partial(combine_kernel, bit),
            "combine",
            [held(total.shape), held(outside.shape)],
            total,
            outside,
            other,
        )
    planes = planes_of(*driven, outside)
    last = context_bits - 1
    other = swap(total, ("context", last))

    extra_bits = [("dp", bit) for bit in range(1, dp_bits)]
    z_bits = [("context", bit) for bit in range(1, context_bits)]
    by_name = {"x": extra_bits, "y": [("context", 0)], "z": z_bits}
    layout = [("context", bit) for bit in reversed(range(context_bits))] + extra_bits[::-1]
    piece = model_width // 2 ** len(layout)
    grad_scale = float(batch_count * row_count * dp_count * context_count) ** (-0.5)
    less = lambda taken: [step for step in layout if step not in taken]
    streams, first, parts = [], 0, []
    for eighths, *names in STREAMS:
        past = max(8, piece * eighths // 64 * 8)
        if past > first:
            orders = [[step for name in order for step in by_name[name]] for order in names]
            streams.append({"rows": (first, past), "orders": orders, "settled": ([], [])})
            steps = [order[0] for order in orders]
            parts += [(layout, steps, far, first, past) for far in (True, False)]
            first = past

    common = (decay, chunk_totals, planes, outside, other, flat_in, flat_cot)
    lent_pairs, *lent = side(False, last, parts, piece, *common, ())
    borrowed = [swap(part, ("dp", 0)) for part in lent]
    kept_pairs, kept = side(True, last, [], piece, *common, lent[:1])

    vmem, anywhere = pl.BlockSpec(memory_space=pltpu.VMEM), pl.BlockSpec(memory_space=pl.ANY)

    def add(stream, sources, sent=(None, None), scale=None, later=()):
        layouts = [[left[core] for _, left in sources] for core in range(2)]
        free = len(layout) - len(stream["settled"][0]) - (sent[0] is not None)
        first, past = stream["rows"]
        return call(
            functools.partial(
                add_kernel,
                layout,
                layouts,
                stream["rows"],
                stream["settled"],
                sent,
                scale,
                len(sources),
            ),
            "halve" if scale is None else "share",
            held((2**free, past - first, 2 * state_count)),
            *(source for source, _ in sources),
            *later,
            inputs=[vmem] * len(sources) + [anywhere] * len(later),
        )

    before = []
    for place in range(len(layout)):
        for number, stream in enumerate(streams):
            steps = [order[place] for order in stream["orders"]]
            if place == 0:
                left = tuple(less([step]) for step in steps)
                far, near = borrowed[2 * number : 2 * number + 2]
                stream["sources"] = [(kept, (layout, layout)), (near, left)]
                away = add(stream, [stream["sources"][0], (far, left)], steps, later=before)
            else:
                away = add(stream, stream["sources"], steps, later=before)
            stream["settled"] = tuple(
                settled + [step] for settled, step in zip(stream["settled"], steps)
            )
            left = tuple(less(settled) for settled in stream["settled"])
            stream["sources"] = stream["sources"] + [(swap(away, *steps), left)]
        if place == 0:
            outputs, input_grad, token = products(
                flat_in,
                flat_cot,
                lent_pairs,
                kept_pairs,
                in_proj,
                out_proj,
                skip_gain.reshape(1, model_width),
                away,
            )
            before = [token]
    items, shares = [], []
    for stream in streams:
        mine = [(0, add(stream, stream["sources"], scale=grad_scale, later=before))]
        before = ()
        for bit in [bit for _, bit in extra_bits] + [0]:
            mine = mine + [
                (offset ^ (1 << bit), swap(share, ("dp", bit))) for offset, share in mine
            ]
        for offset, share in mine:
            items.append((stream["rows"], offset))
            shares.append(share)
    whole = jax.ShapeDtypeStruct((dp_count // 2, piece, 2 * state_count), jnp.float32)
    sums = call(functools.partial(gather_kernel, items), "gather", [whole, whole], *shares)
    sums = [part.reshape(model_width // context_count, 2 * state_count) for part in sums]
    return (outputs.reshape(inputs.shape), input_grad.reshape(inputs.shape), *sums)


def solution(mesh):
    in_specs = (
        P("dp", "context", None),
        P("dp", "context"),
        P(),
        P(),
        P(),
        P(),
        P(),
        P("dp", "context", None),
    )
    out_specs = (
        P("dp", "context", None),
        P("dp", "context", None),
        P("context", None),
        P("context", None),
    )
    return jax.shard_map(
        on_device, mesh=mesh, in_specs=in_specs, out_specs=out_specs, check_vma=False
    )
```

time: 63.4 us -> 60.7 us (0.957)
  waiting for transfers between devices: 20.4 us -> 11.2 us
  starting transfers between devices: 30.4 us -> 36.9 us
    ppermute x19 -> x30, waiting for transfers between devices: 20.4 us -> 11.2 us  [swap(): return lax.ppermute(array, ('dp', 'context'), pairs)]
    ppermute x19 -> x30, starting transfers between devices: 30.4 us -> 36.9 us  [swap(): return lax.ppermute(array, ('dp', 'context'), pairs)]
    pallas_call x18 -> x23, Pallas kernels: 11.6 us -> 11.7 us  [call(): pl.pallas_call(kernel, out_shape=out_shape, in_specs=inputs or [vmem] * l...]
  transfers between devices with their start and end apart: 19 -> 30, of which waited for: 12 -> 10; matrix products, arithmetic and copies ran while one was open for 0% -> 0% of each run, Pallas kernels for 6% -> 8%
where the time goes in v4:
time: 60.7 us; the launch traced here: 60.6 us
  starting transfers between devices  36.9 us (61%)
  Pallas kernels  11.7 us (19%)
  waiting for transfers between devices  11.2 us (18%)
  between operations  0.79 us (1%)
    ppermute x30, starting transfers between devices, swap(): return lax.ppermute(array, ('dp', 'context'), pairs)  36.9 us
    pallas_call x23, Pallas kernels, call(): pl.pallas_call(kernel, out_shape=out_shape, in_specs=inputs or [vmem] * l...  11.7 us
    ppermute x30, waiting for transfers between devices, swap(): return lax.ppermute(array, ('dp', 'context'), pairs)  11.2 us
  transfers between devices with their start and end apart: 30, of which 10 were waited for; matrix products, arithmetic and copies ran while one was open for 0% of the time, Pallas kernels for 8%

profile of v4, /device:TPU:0, one launch (start us, length us, event | category | flops | bytes accessed | tf_op | source)
XLA Modules:
  0.0 60.6 jit_solution(7893767229316967444)
XLA Ops:
  0.6 4.6 %local_scan.1 = (f32[512,256]{1,0:T(8,128)S(1)}, f32[512,256]{1,0:T(8,128)S(1)}, f32[512,512]{1,0:T(8,128)S(1)}, f32[512,512]{1,0:T(8,128)S(1)}, f32[6,16,256]{2...) custom-call(f32[1,512]{1,0:T(1,128)} %step_hbm.1, ...), custom_call_target="tpu_custom_call" | custom-call | flops 1073741824 | bytes 1073741 | tf_op jit(solution)/shard_map/local_scan/pallas_call | solution.py:216
  5.3 3.0 %collective-permute-start = (f32[8,256]{1,0:T(8,128)S(1)}, f32[8,256]{1,0:T(8,128)S(1)}, u32[]{:S(2)}, u32[]{:S(2)}) collective-permute-start(f32[8,256]{1,0:T(8,128)S(1)} %get-tuple-element.50.total_ref), channel_id=1, source_target_pairs={{0,1},{1,0},{2,3},{3,2},{4,5},{5,4},{6,7},{7,6},{8,9},{9,8},{10,11... | collective-permute-start | bytes 24584 | tf_op jit(solution)/shard_map/ppermute | solution.py:593
  8.3 1.6 %collective-permute-done.other_ref = f32[8,256]{1,0:T(8,128)S(1)} collective-permute-done((f32[8,256]{1,0:T(8,128)S(1)}, f32[8,256]{1,0:T(8,128)S(1)}, u32[]{:S(2)}, u32[]{:S(2)}) %collective-permute-start) | collective-permute-done | bytes 8224 | tf_op jit(solution)/shard_map/ppermute | solution.py:593
  10.0 2.1 %collective-permute-start.1 = (f32[8,256]{1,0:T(8,128)S(1)}, f32[8,256]{1,0:T(8,128)S(1)}, u32[]{:S(2)}, u32[]{:S(2)}) collective-permute-start(f32[8,256]{1,0:T(8,128)S(1)} %get-tuple-element.52.total_ref), channel_id=1, source_target_pairs={{0,2},{1,3},{2,0},{3,1},{4,6},{5,7},{6,4},{7,5},{8,10},{9,11},{10,... | collective-permute-start | bytes 24584 | tf_op jit(solution)/shard_map/ppermute | solution.py:593
  12.1 1.6 %collective-permute-done.1.other_ref = f32[8,256]{1,0:T(8,128)S(1)} collective-permute-done((f32[8,256]{1,0:T(8,128)S(1)}, f32[8,256]{1,0:T(8,128)S(1)}, u32[]{:S(2)}, u32[]{:S(2)}) %collective-permute-start.1) | collective-permute-done | bytes 8224 | tf_op jit(solution)/shard_map/ppermute | solution.py:593
  13.8 3.1 %collective-permute-start.2 = (f32[8,256]{1,0:T(8,128)S(1)}, f32[8,256]{1,0:T(8,128)S(1)}, u32[]{:S(2)}, u32[]{:S(2)}) collective-permute-start(f32[8,256]{1,0:T(8,128)S(1)} %get-tuple-element.63), channel_id=1, source_target_pairs={{0,4},{1,5},{2,6},{3,7},{4,0},{5,1},{6,2},{7,3},{8,12},{9,13},{10,... | collective-permute-start | bytes 24584 | tf_op jit(solution)/shard_map/ppermute | solution.py:593
  21.6 1.9 %collective-permute-start.15 = (f32[8,24,512]{2,1,0:T(8,128)S(1)}, f32[8,24,512]{2,1,0:T(8,128)S(1)}, u32[]{:S(2)}, u32[]{:S(2)}) collective-permute-start(f32[8,24,512]{2,1,0:T(8,128)S(1)} %halve.17), channel_id=1, source_target_pairs={{0,16},{1,17},{2,18},{3,19},{4,20},{5,21},{6,22},{7,23},{8,9},{9,8... | collective-permute-start | bytes 1179656 | tf_op jit(solution)/shard_map/ppermute | solution.py:593
  23.5 1.3 %collective-permute-start.6 = (f32[8,24,512]{2,1,0:T(8,128)S(1)}, f32[8,24,512]{2,1,0:T(8,128)S(1)}, u32[]{:S(2)}, u32[]{:S(2)}) collective-permute-start(f32[8,24,512]{2,1,0:T(8,128)S(1)} %halve.13), channel_id=1, source_target_pairs={{0,16},{1,17},{2,18},{3,19},{4,20},{5,21},{6,22},{7,23},{8,9},{9,8... | collective-permute-start | bytes 1179656 | tf_op jit(solution)/shard_map/ppermute | solution.py:593
  26.0 3.1 %products.1 = (bf16[512,1024]{1,0:T(8,128)(2,1)}, bf16[512,1024]{1,0:T(8,128)(2,1)}, f32[8,128]{1,0:T(8,128)S(1)}) custom-call(bf16[512,1024]{1,0:T(8,128)(2,1)S(1)} %get-tuple-element.42.refs_12_.in_ref, bf16[512,1024]{1,0:T(8,128)(2,1)S(1)} %get-tuple-element.43.refs_13_.cot_ref, bf16[512,512]{1,0:T(8,128)(2,1)S(1)} %get-tuple-element.64.lent_ref, ...), custom_call_target="tpu_custom_call" | custom-call | flops 1073741824 | bytes 1073741 | tf_op jit(solution)/shard_map/products/pallas_call | solution.py:216
  29.4 1.9 %collective-permute-start.16 = (f32[4,24,512]{2,1,0:T(8,128)S(1)}, f32[4,24,512]{2,1,0:T(8,128)S(1)}, u32[]{:S(2)}, u32[]{:S(2)}) collective-permute-start(f32[4,24,512]{2,1,0:T(8,128)S(1)} %halve.18), channel_id=1, source_target_pairs={{0,1},{1,0},{2,3},{3,2},{4,5},{5,4},{6,7},{7,6},{8,10},{9,11},{10,... | collective-permute-start | bytes 589832 | tf_op jit(solution)/shard_map/ppermute | solution.py:593
  31.4 2.3 %collective-permute-done.6.refs_2_ = f32[8,24,512]{2,1,0:T(8,128)S(1)} collective-permute-done((f32[8,24,512]{2,1,0:T(8,128)S(1)}, f32[8,24,512]{2,1,0:T(8,128)S(1)}, u32[]{:S(2)}, u32[]{:S(2)}) %collective-permute-start.6) | collective-permute-done | bytes 393248 | tf_op jit(solution)/shard_map/ppermute | solution.py:593
  33.6 1.9 %collective-permute-start.7 = (f32[4,24,512]{2,1,0:T(8,128)S(1)}, f32[4,24,512]{2,1,0:T(8,128)S(1)}, u32[]{:S(2)}, u32[]{:S(2)}) collective-permute-start(f32[4,24,512]{2,1,0:T(8,128)S(1)} %halve.14), channel_id=1, source_target_pairs={{0,1},{1,0},{2,3},{3,2},{4,5},{5,4},{6,7},{7,6},{8,10},{9,11},{10,... | collective-permute-start | bytes 589832 | tf_op jit(solution)/shard_map/ppermute | solution.py:593
  36.5 1.9 %collective-permute-start.24 = (f32[4,16,512]{2,1,0:T(8,128)S(1)}, f32[4,16,512]{2,1,0:T(8,128)S(1)}, u32[]{:S(2)}, u32[]{:S(2)}) collective-permute-start(f32[4,16,512]{2,1,0:T(8,128)S(1)} %halve.21), channel_id=1, source_target_pairs={{0,1},{1,0},{2,3},{3,2},{4,5},{5,4},{6,7},{7,6},{8,10},{9,11},{10,... | collective-permute-start | bytes 393224 | tf_op jit(solution)/shard_map/ppermute | solution.py:593
  38.4 1.6 %collective-permute-start.17 = (f32[2,24,512]{2,1,0:T(8,128)S(1)}, f32[2,24,512]{2,1,0:T(8,128)S(1)}, u32[]{:S(2)}, u32[]{:S(2)}) collective-permute-start(f32[2,24,512]{2,1,0:T(8,128)S(1)} %halve.19), channel_id=1, source_target_pairs={{0,2},{1,3},{2,0},{3,1},{4,6},{5,7},{6,4},{7,5},{8,12},{9,13},{10,... | collective-permute-start | bytes 294920 | tf_op jit(solution)/shard_map/ppermute | solution.py:593
  40.1 1.6 %collective-permute-start.8 = (f32[2,24,512]{2,1,0:T(8,128)S(1)}, f32[2,24,512]{2,1,0:T(8,128)S(1)}, u32[]{:S(2)}, u32[]{:S(2)}) collective-permute-start(f32[2,24,512]{2,1,0:T(8,128)S(1)} %halve.15), channel_id=1, source_target_pairs={{0,2},{1,3},{2,0},{3,1},{4,6},{5,7},{6,4},{7,5},{8,12},{9,13},{10,... | collective-permute-start | bytes 294920 | tf_op jit(solution)/shard_map/ppermute | solution.py:593
  41.7 1.8 %collective-permute-start.25 = (f32[2,16,512]{2,1,0:T(8,128)S(1)}, f32[2,16,512]{2,1,0:T(8,128)S(1)}, u32[]{:S(2)}, u32[]{:S(2)}) collective-permute-start(f32[2,16,512]{2,1,0:T(8,128)S(1)} %halve.22), channel_id=1, source_target_pairs={{0,2},{1,3},{2,0},{3,1},{4,6},{5,7},{6,4},{7,5},{8,12},{9,13},{10,... | collective-permute-start | bytes 196616 | tf_op jit(solution)/shard_map/ppermute | solution.py:593
  43.5 3.6 %collective-permute-start.18 = (f32[1,24,512]{2,1,0:T(8,128)S(1)}, f32[1,24,512]{2,1,0:T(8,128)S(1)}, u32[]{:S(2)}, u32[]{:S(2)}) collective-permute-start(f32[1,24,512]{2,1,0:T(8,128)S(1)} %halve.20), channel_id=1, source_target_pairs={{0,4},{1,5},{2,6},{3,7},{4,0},{5,1},{6,2},{7,3},{8,24},{9,25},{10,... | collective-permute-start | bytes 147464 | tf_op jit(solution)/shard_map/ppermute | solution.py:593
  47.1 1.8 %collective-permute-start.9 = (f32[1,24,512]{2,1,0:T(8,128)S(1)}, f32[1,24,512]{2,1,0:T(8,128)S(1)}, u32[]{:S(2)}, u32[]{:S(2)}) collective-permute-start(f32[1,24,512]{2,1,0:T(8,128)S(1)} %halve.16), channel_id=1, source_target_pairs={{0,4},{1,5},{2,6},{3,7},{4,0},{5,1},{6,2},{7,3},{8,24},{9,25},{10,... | collective-permute-start | bytes 147464 | tf_op jit(solution)/shard_map/ppermute | solution.py:593
  48.9 1.4 %collective-permute-start.26 = (f32[1,16,512]{2,1,0:T(8,128)S(1)}, f32[1,16,512]{2,1,0:T(8,128)S(1)}, u32[]{:S(2)}, u32[]{:S(2)}) collective-permute-start(f32[1,16,512]{2,1,0:T(8,128)S(1)} %halve.23), channel_id=1, source_target_pairs={{0,4},{1,5},{2,6},{3,7},{4,0},{5,1},{6,2},{7,3},{8,24},{9,25},{10,... | collective-permute-start | bytes 98312 | tf_op jit(solution)/shard_map/ppermute | solution.py:593
  50.3 1.6 %collective-permute-start.19 = (f32[1,24,512]{2,1,0:T(8,128)S(1)}, f32[1,24,512]{2,1,0:T(8,128)S(1)}, u32[]{:S(2)}, u32[]{:S(2)}) collective-permute-start(f32[1,24,512]{2,1,0:T(8,128)S(1)} %share.4.refs_4_), channel_id=1, source_target_pairs={{0,16},{1,17},{2,18},{3,19},{4,20},{5,21},{6,22},{7,23},{8,24},{9,... | collective-permute-start | bytes 147464 | tf_op jit(solution)/shard_map/ppermute | solution.py:593
  52.2 1.5 %collective-permute-start.10 = (f32[1,24,512]{2,1,0:T(8,128)S(1)}, f32[1,24,512]{2,1,0:T(8,128)S(1)}, u32[]{:S(2)}, u32[]{:S(2)}) collective-permute-start(f32[1,24,512]{2,1,0:T(8,128)S(1)} %share.3.refs_0_), channel_id=1, source_target_pairs={{0,16},{1,17},{2,18},{3,19},{4,20},{5,21},{6,22},{7,23},{8,24},{9,... | collective-permute-start | bytes 147464 | tf_op jit(solution)/shard_map/ppermute | solution.py:593
  54.4 1.6 %collective-permute-start.27 = (f32[1,16,512]{2,1,0:T(8,128)S(1)}, f32[1,16,512]{2,1,0:T(8,128)S(1)}, u32[]{:S(2)}, u32[]{:S(2)}) collective-permute-start(f32[1,16,512]{2,1,0:T(8,128)S(1)} %share.5.refs_8_), channel_id=1, source_target_pairs={{0,16},{1,17},{2,18},{3,19},{4,20},{5,21},{6,22},{7,23},{8,24},{9,... | collective-permute-start | bytes 98312 | tf_op jit(solution)/shard_map/ppermute | solution.py:593
  57.0 1.4 %collective-permute-done.27.refs_9_ = f32[1,16,512]{2,1,0:T(8,128)S(1)} collective-permute-done((f32[1,16,512]{2,1,0:T(8,128)S(1)}, f32[1,16,512]{2,1,0:T(8,128)S(1)}, u32[]{:S(2)}, u32[]{:S(2)}) %collective-permute-start.27) | collective-permute-done | bytes 32800 | tf_op jit(solution)/shard_map/ppermute | solution.py:593
  58.4 1.2 %collective-permute-done.29.refs_11_ = f32[1,16,512]{2,1,0:T(8,128)S(1)} collective-permute-done((f32[1,16,512]{2,1,0:T(8,128)S(1)}, f32[1,16,512]{2,1,0:T(8,128)S(1)}, u32[]{:S(2)}, u32[]{:S(2)}) %collective-permute-start.29) | collective-permute-done | bytes 32800 | tf_op jit(solution)/shard_map/ppermute | solution.py:593
  (61 shorter events, 10.3 us)
Async XLA Ops:
  5.3 4.7 %collective-permute-start = (f32[8,256]{1,0:T(8,128)S(1)}, f32[8,256]{1,0:T(8,128)S(1)}, u32[]{:S(2)}, u32[]{:S(2)}) collective-permute-start(f32[8,256]{1,0:T(8,128)S(1)} %get-tuple-element.50.total_ref), channel_id=1, source_target_pairs={{0,1},{1,0},{2,3},{3,2},{4,5},{5,4},{6,7},{7,6},{8,9},{9,8},{10,11... | collective-permute-start | bytes 24584 | tf_op jit(solution)/shard_map/ppermute | solution.py:593
  10.0 3.8 %collective-permute-start.1 = (f32[8,256]{1,0:T(8,128)S(1)}, f32[8,256]{1,0:T(8,128)S(1)}, u32[]{:S(2)}, u32[]{:S(2)}) collective-permute-start(f32[8,256]{1,0:T(8,128)S(1)} %get-tuple-element.52.total_ref), channel_id=1, source_target_pairs={{0,2},{1,3},{2,0},{3,1},{4,6},{5,7},{6,4},{7,5},{8,10},{9,11},{10,... | collective-permute-start | bytes 24584 | tf_op jit(solution)/shard_map/ppermute | solution.py:593
  13.8 4.7 %collective-permute-start.2 = (f32[8,256]{1,0:T(8,128)S(1)}, f32[8,256]{1,0:T(8,128)S(1)}, u32[]{:S(2)}, u32[]{:S(2)}) collective-permute-start(f32[8,256]{1,0:T(8,128)S(1)} %get-tuple-element.63), channel_id=1, source_target_pairs={{0,4},{1,5},{2,6},{3,7},{4,0},{5,1},{6,2},{7,3},{8,12},{9,13},{10,... | collective-permute-start | bytes 24584 | tf_op jit(solution)/shard_map/ppermute | solution.py:593
  19.6 3.9 %collective-permute-start.5 = (f32[8,24,512]{2,1,0:T(8,128)S(1)}, f32[8,24,512]{2,1,0:T(8,128)S(1)}, u32[]{:S(2)}, u32[]{:S(2)}) collective-permute-start(f32[8,24,512]{2,1,0:T(8,128)S(1)} %get-tuple-element.65.refs_14_), channel_id=1, source_target_pairs={{0,8},{1,9},{2,10},{3,11},{4,12},{5,13},{6,14},{7,15},{8,0},{9,1},... | collective-permute-start | bytes 1179656 | tf_op jit(solution)/shard_map/ppermute | solution.py:593
  20.1 5.3 %collective-permute-start.13 = (f32[8,24,512]{2,1,0:T(8,128)S(1)}, f32[8,24,512]{2,1,0:T(8,128)S(1)}, u32[]{:S(2)}, u32[]{:S(2)}) collective-permute-start(f32[8,24,512]{2,1,0:T(8,128)S(1)} %get-tuple-element.75), channel_id=1, source_target_pairs={{0,8},{1,9},{2,10},{3,11},{4,12},{5,13},{6,14},{7,15},{8,0},{9,1},... | collective-permute-start | bytes 1179656 | tf_op jit(solution)/shard_map/ppermute | solution.py:593
  20.2 4.7 %collective-permute-start.3 = (f32[8,16,512]{2,1,0:T(8,128)S(1)}, f32[8,16,512]{2,1,0:T(8,128)S(1)}, u32[]{:S(2)}, u32[]{:S(2)}) collective-permute-start(f32[8,16,512]{2,1,0:T(8,128)S(1)} %get-tuple-element.70), channel_id=1, source_target_pairs={{0,8},{1,9},{2,10},{3,11},{4,12},{5,13},{6,14},{7,15},{8,0},{9,1},... | collective-permute-start | bytes 786440 | tf_op jit(solution)/shard_map/ppermute | solution.py:593
  21.6 7.8 %collective-permute-start.15 = (f32[8,24,512]{2,1,0:T(8,128)S(1)}, f32[8,24,512]{2,1,0:T(8,128)S(1)}, u32[]{:S(2)}, u32[]{:S(2)}) collective-permute-start(f32[8,24,512]{2,1,0:T(8,128)S(1)} %halve.17), channel_id=1, source_target_pairs={{0,16},{1,17},{2,18},{3,19},{4,20},{5,21},{6,22},{7,23},{8,9},{9,8... | collective-permute-start | bytes 1179656 | tf_op jit(solution)/shard_map/ppermute | solution.py:593
  23.4 7.9 %collective-permute-start.4 = (f32[8,24,512]{2,1,0:T(8,128)S(1)}, f32[8,24,512]{2,1,0:T(8,128)S(1)}, u32[]{:S(2)}, u32[]{:S(2)}) collective-permute-start(f32[8,24,512]{2,1,0:T(8,128)S(1)} %get-tuple-element.73), channel_id=1, source_target_pairs={{0,8},{1,9},{2,10},{3,11},{4,12},{5,13},{6,14},{7,15},{8,0},{9,1},... | collective-permute-start | bytes 1179656 | tf_op jit(solution)/shard_map/ppermute | solution.py:593
  23.5 10.1 %collective-permute-start.6 = (f32[8,24,512]{2,1,0:T(8,128)S(1)}, f32[8,24,512]{2,1,0:T(8,128)S(1)}, u32[]{:S(2)}, u32[]{:S(2)}) collective-permute-start(f32[8,24,512]{2,1,0:T(8,128)S(1)} %halve.13), channel_id=1, source_target_pairs={{0,16},{1,17},{2,18},{3,19},{4,20},{5,21},{6,22},{7,23},{8,9},{9,8... | collective-permute-start | bytes 1179656 | tf_op jit(solution)/shard_map/ppermute | solution.py:593
  24.8 10.7 %collective-permute-start.22 = (f32[8,16,512]{2,1,0:T(8,128)S(1)}, f32[8,16,512]{2,1,0:T(8,128)S(1)}, u32[]{:S(2)}, u32[]{:S(2)}) collective-permute-start(f32[8,16,512]{2,1,0:T(8,128)S(1)} %get-tuple-element.77), channel_id=1, source_target_pairs={{0,8},{1,9},{2,10},{3,11},{4,12},{5,13},{6,14},{7,15},{8,0},{9,1},... | collective-permute-start | bytes 786440 | tf_op jit(solution)/shard_map/ppermute | solution.py:593
  25.4 11.1 %collective-permute-start.23 = (f32[8,16,512]{2,1,0:T(8,128)S(1)}, f32[8,16,512]{2,1,0:T(8,128)S(1)}, u32[]{:S(2)}, u32[]{:S(2)}) collective-permute-start(f32[8,16,512]{2,1,0:T(8,128)S(1)} %halve.12.after_ref), channel_id=1, source_target_pairs={{0,16},{1,17},{2,18},{3,19},{4,20},{5,21},{6,22},{7,23},{8,9},{9,8... | collective-permute-start | bytes 786440 | tf_op jit(solution)/shard_map/ppermute | solution.py:593
  29.4 8.9 %collective-permute-start.16 = (f32[4,24,512]{2,1,0:T(8,128)S(1)}, f32[4,24,512]{2,1,0:T(8,128)S(1)}, u32[]{:S(2)}, u32[]{:S(2)}) collective-permute-start(f32[4,24,512]{2,1,0:T(8,128)S(1)} %halve.18), channel_id=1, source_target_pairs={{0,1},{1,0},{2,3},{3,2},{4,5},{5,4},{6,7},{7,6},{8,10},{9,11},{10,... | collective-permute-start | bytes 589832 | tf_op jit(solution)/shard_map/ppermute | solution.py:593
  33.6 6.4 %collective-permute-start.7 = (f32[4,24,512]{2,1,0:T(8,128)S(1)}, f32[4,24,512]{2,1,0:T(8,128)S(1)}, u32[]{:S(2)}, u32[]{:S(2)}) collective-permute-start(f32[4,24,512]{2,1,0:T(8,128)S(1)} %halve.14), channel_id=1, source_target_pairs={{0,1},{1,0},{2,3},{3,2},{4,5},{5,4},{6,7},{7,6},{8,10},{9,11},{10,... | collective-permute-start | bytes 589832 | tf_op jit(solution)/shard_map/ppermute | solution.py:593
  36.5 5.3 %collective-permute-start.24 = (f32[4,16,512]{2,1,0:T(8,128)S(1)}, f32[4,16,512]{2,1,0:T(8,128)S(1)}, u32[]{:S(2)}, u32[]{:S(2)}) collective-permute-start(f32[4,16,512]{2,1,0:T(8,128)S(1)} %halve.21), channel_id=1, source_target_pairs={{0,1},{1,0},{2,3},{3,2},{4,5},{5,4},{6,7},{7,6},{8,10},{9,11},{10,... | collective-permute-start | bytes 393224 | tf_op jit(solution)/shard_map/ppermute | solution.py:593
  38.4 5.1 %collective-permute-start.17 = (f32[2,24,512]{2,1,0:T(8,128)S(1)}, f32[2,24,512]{2,1,0:T(8,128)S(1)}, u32[]{:S(2)}, u32[]{:S(2)}) collective-permute-start(f32[2,24,512]{2,1,0:T(8,128)S(1)} %halve.19), channel_id=1, source_target_pairs={{0,2},{1,3},{2,0},{3,1},{4,6},{5,7},{6,4},{7,5},{8,12},{9,13},{10,... | collective-permute-start | bytes 294920 | tf_op jit(solution)/shard_map/ppermute | solution.py:593
  40.1 7.0 %collective-permute-start.8 = (f32[2,24,512]{2,1,0:T(8,128)S(1)}, f32[2,24,512]{2,1,0:T(8,128)S(1)}, u32[]{:S(2)}, u32[]{:S(2)}) collective-permute-start(f32[2,24,512]{2,1,0:T(8,128)S(1)} %halve.15), channel_id=1, source_target_pairs={{0,2},{1,3},{2,0},{3,1},{4,6},{5,7},{6,4},{7,5},{8,12},{9,13},{10,... | collective-permute-start | bytes 294920 | tf_op jit(solution)/shard_map/ppermute | solution.py:593
  41.7 7.2 %collective-permute-start.25 = (f32[2,16,512]{2,1,0:T(8,128)S(1)}, f32[2,16,512]{2,1,0:T(8,128)S(1)}, u32[]{:S(2)}, u32[]{:S(2)}) collective-permute-start(f32[2,16,512]{2,1,0:T(8,128)S(1)} %halve.22), channel_id=1, source_target_pairs={{0,2},{1,3},{2,0},{3,1},{4,6},{5,7},{6,4},{7,5},{8,12},{9,13},{10,... | collective-permute-start | bytes 196616 | tf_op jit(solution)/shard_map/ppermute | solution.py:593
  43.5 6.8 %collective-permute-start.18 = (f32[1,24,512]{2,1,0:T(8,128)S(1)}, f32[1,24,512]{2,1,0:T(8,128)S(1)}, u32[]{:S(2)}, u32[]{:S(2)}) collective-permute-start(f32[1,24,512]{2,1,0:T(8,128)S(1)} %halve.20), channel_id=1, source_target_pairs={{0,4},{1,5},{2,6},{3,7},{4,0},{5,1},{6,2},{7,3},{8,24},{9,25},{10,... | collective-permute-start | bytes 147464 | tf_op jit(solution)/shard_map/ppermute | solution.py:593
  47.1 5.1 %collective-permute-start.9 = (f32[1,24,512]{2,1,0:T(8,128)S(1)}, f32[1,24,512]{2,1,0:T(8,128)S(1)}, u32[]{:S(2)}, u32[]{:S(2)}) collective-permute-start(f32[1,24,512]{2,1,0:T(8,128)S(1)} %halve.16), channel_id=1, source_target_pairs={{0,4},{1,5},{2,6},{3,7},{4,0},{5,1},{6,2},{7,3},{8,24},{9,25},{10,... | collective-permute-start | bytes 147464 | tf_op jit(solution)/shard_map/ppermute | solution.py:593
  48.9 5.4 %collective-permute-start.26 = (f32[1,16,512]{2,1,0:T(8,128)S(1)}, f32[1,16,512]{2,1,0:T(8,128)S(1)}, u32[]{:S(2)}, u32[]{:S(2)}) collective-permute-start(f32[1,16,512]{2,1,0:T(8,128)S(1)} %halve.23), channel_id=1, source_target_pairs={{0,4},{1,5},{2,6},{3,7},{4,0},{5,1},{6,2},{7,3},{8,24},{9,25},{10,... | collective-permute-start | bytes 98312 | tf_op jit(solution)/shard_map/ppermute | solution.py:593
  50.3 6.2 %collective-permute-start.19 = (f32[1,24,512]{2,1,0:T(8,128)S(1)}, f32[1,24,512]{2,1,0:T(8,128)S(1)}, u32[]{:S(2)}, u32[]{:S(2)}) collective-permute-start(f32[1,24,512]{2,1,0:T(8,128)S(1)} %share.4.refs_4_), channel_id=1, source_target_pairs={{0,16},{1,17},{2,18},{3,19},{4,20},{5,21},{6,22},{7,23},{8,24},{9,... | collective-permute-start | bytes 147464 | tf_op jit(solution)/shard_map/ppermute | solution.py:593
  52.2 4.5 %collective-permute-start.10 = (f32[1,24,512]{2,1,0:T(8,128)S(1)}, f32[1,24,512]{2,1,0:T(8,128)S(1)}, u32[]{:S(2)}, u32[]{:S(2)}) collective-permute-start(f32[1,24,512]{2,1,0:T(8,128)S(1)} %share.3.refs_0_), channel_id=1, source_target_pairs={{0,16},{1,17},{2,18},{3,19},{4,20},{5,21},{6,22},{7,23},{8,24},{9,... | collective-permute-start | bytes 147464 | tf_op jit(solution)/shard_map/ppermute | solution.py:593
  54.4 4.0 %collective-permute-start.27 = (f32[1,16,512]{2,1,0:T(8,128)S(1)}, f32[1,16,512]{2,1,0:T(8,128)S(1)}, u32[]{:S(2)}, u32[]{:S(2)}) collective-permute-start(f32[1,16,512]{2,1,0:T(8,128)S(1)} %share.5.refs_8_), channel_id=1, source_target_pairs={{0,16},{1,17},{2,18},{3,19},{4,20},{5,21},{6,22},{7,23},{8,24},{9,... | collective-permute-start | bytes 98312 | tf_op jit(solution)/shard_map/ppermute | solution.py:593
  56.0 3.6 %collective-permute-start.20 = (f32[1,24,512]{2,1,0:T(8,128)S(1)}, f32[1,24,512]{2,1,0:T(8,128)S(1)}, u32[]{:S(2)}, u32[]{:S(2)}) collective-permute-start(f32[1,24,512]{2,1,0:T(8,128)S(1)} %share.4.refs_4_), channel_id=1, source_target_pairs={{0,8},{1,9},{2,10},{3,11},{4,12},{5,13},{6,14},{7,15},{8,0},{9,1},... | collective-permute-start | bytes 147464 | tf_op jit(solution)/shard_map/ppermute | solution.py:593
  (7 other events, 17.1 us)

commit v5 on v4

--- a/solution.py
+++ b/solution.py
@@ -12,7 +12,7 @@
 GROUP = 256
 LOAD_PIECES = 1
 VMEM_LIMIT = 24 * 1024 * 1024
-STREAMS = ((3, "xyz", "yzx"), (6, "xyz", "yzx"), (8, "xyz", "yzx"))
+STREAMS = ((5, "xyz", "yzx"), (8, "aybX", "yabX"))
 
 TWO_OVER_PI = 0.6366197723675814
 PIO2_HIGH = 1.5703125
@@ -569,7 +569,10 @@
 
             @pl.when(place & 1 == core)
             def _():
-                target[place >> 1, rows[0] : rows[1], :] = share[0]
+                if share.shape[0] == target.shape[0]:
+                    target[:, rows[0] : rows[1], :] = share[...]
+                else:
+                    target[place >> 1, rows[0] : rows[1], :] = share[0]
 
 
 def on_device(
@@ -617,7 +620,13 @@
 
     extra_bits = [("dp", bit) for bit in range(1, dp_bits)]
     z_bits = [("context", bit) for bit in range(1, context_bits)]
-    by_name = {"x": extra_bits, "y": [("context", 0)], "z": z_bits}
+    by_name = {
+        "x": extra_bits,
+        "y": [("context", 0)],
+        "z": z_bits,
+        "a": z_bits[:1],
+        "b": z_bits[1:],
+    }
     layout = [("context", bit) for bit in reversed(range(context_bits))] + extra_bits[::-1]
     piece = model_width // 2 ** len(layout)
     grad_scale = float(batch_count * row_count * dp_count * context_count) ** (-0.5)
@@ -626,8 +635,11 @@
     for eighths, *names in STREAMS:
         past = max(8, piece * eighths // 64 * 8)
         if past > first:
-            orders = [[step for name in order for step in by_name[name]] for order in names]
-            streams.append({"rows": (first, past), "orders": orders, "settled": ([], [])})
+            orders = [[step for name in order for step in by_name[name.lower()]] for order in names]
+            halvings = len(layout) - (len(extra_bits) if "X" in names[0] else 0)
+            streams.append(
+                {"rows": (first, past), "orders": orders, "settled": ([], []), "halvings": halvings}
+            )
             steps = [order[0] for order in orders]
             parts += [(layout, steps, far, first, past) for far in (True, False)]
             first = past
@@ -665,6 +677,11 @@
     for place in range(len(layout)):
         for number, stream in enumerate(streams):
             steps = [order[place] for order in stream["orders"]]
+            if place >= stream["halvings"]:
+                left = tuple(less(settled) for settled in stream["settled"])
+                away = add(stream, stream["sources"], later=before)
+                stream["sources"] = [(away, left), (swap(away, *steps), left)]
+                continue
             if place == 0:
                 left = tuple(less([step]) for step in steps)
                 far, near = borrowed[2 * number : 2 * number + 2]
@@ -693,7 +710,7 @@
     for stream in streams:
         mine = [(0, add(stream, stream["sources"], scale=grad_scale, later=before))]
         before = ()
-        for bit in [bit for _, bit in extra_bits] + [0]:
+        for bit in [bit for _, bit in extra_bits if stream["halvings"] == len(layout)] + [0]:
             mine = mine + [
                 (offset ^ (1 << bit), swap(share, ("dp", bit))) for offset, share in mine
             ]

time: 60.7 us -> 58.2 us (0.959)
  starting transfers between devices: 36.9 us -> 27.5 us
  waiting for transfers between devices: 11.2 us -> 18.2 us
    ppermute x30 -> x19, starting transfers between devices: 36.9 us -> 27.5 us  [swap(): return lax.ppermute(array, ('dp', 'context'), pairs)]
    ppermute x30 -> x19, waiting for transfers between devices: 11.2 us -> 18.2 us  [swap(): return lax.ppermute(array, ('dp', 'context'), pairs)]
    pallas_call x23 -> x18, Pallas kernels: 11.7 us -> 11.6 us  [call(): pl.pallas_call(kernel, out_shape=out_shape, in_specs=inputs or [vmem] * l...]
  transfers between devices with their start and end apart: 30 -> 19, of which waited for: 10 -> 14; matrix products, arithmetic and copies ran while one was open for 0% -> 0% of each run, Pallas kernels for 8% -> 9%
where the time goes in v5:
time: 58.2 us; the launch traced here: 58 us
  starting transfers between devices  27.5 us (47%)
  waiting for transfers between devices  18.2 us (31%)
  Pallas kernels  11.6 us (20%)
  between operations  0.75 us (1%)
    ppermute x19, starting transfers between devices, swap(): return lax.ppermute(array, ('dp', 'context'), pairs)  27.5 us
    ppermute x19, waiting for transfers between devices, swap(): return lax.ppermute(array, ('dp', 'context'), pairs)  18.2 us
    pallas_call x18, Pallas kernels, call(): pl.pallas_call(kernel, out_shape=out_shape, in_specs=inputs or [vmem] * l...  11.6 us
  transfers between devices with their start and end apart: 19, of which 14 were waited for; matrix products, arithmetic and copies ran while one was open for 0% of the time, Pallas kernels for 9%

profile of v5, /device:TPU:0, one launch (start us, length us, event | category | flops | bytes accessed | tf_op | source)
XLA Modules:
  0.0 58.0 jit_solution(14193086262535810046)
XLA Ops:
  0.6 4.6 %local_scan.1 = (f32[512,256]{1,0:T(8,128)S(1)}, f32[512,256]{1,0:T(8,128)S(1)}, f32[512,512]{1,0:T(8,128)S(1)}, f32[512,512]{1,0:T(8,128)S(1)}, f32[6,16,256]{2...) custom-call(f32[1,512]{1,0:T(1,128)} %step_hbm.1, ...), custom_call_target="tpu_custom_call" | custom-call | flops 1073741824 | bytes 1073741 | tf_op jit(solution)/shard_map/local_scan/pallas_call | solution.py:216
  5.3 3.0 %collective-permute-start = (f32[8,256]{1,0:T(8,128)S(1)}, f32[8,256]{1,0:T(8,128)S(1)}, u32[]{:S(2)}, u32[]{:S(2)}) collective-permute-start(f32[8,256]{1,0:T(8,128)S(1)} %get-tuple-element.48.total_ref), channel_id=1, source_target_pairs={{0,1},{1,0},{2,3},{3,2},{4,5},{5,4},{6,7},{7,6},{8,9},{9,8},{10,11... | collective-permute-start | bytes 24584 | tf_op jit(solution)/shard_map/ppermute | solution.py:596
  8.3 1.6 %collective-permute-done.other_ref = f32[8,256]{1,0:T(8,128)S(1)} collective-permute-done((f32[8,256]{1,0:T(8,128)S(1)}, f32[8,256]{1,0:T(8,128)S(1)}, u32[]{:S(2)}, u32[]{:S(2)}) %collective-permute-start) | collective-permute-done | bytes 8224 | tf_op jit(solution)/shard_map/ppermute | solution.py:596
  10.0 2.1 %collective-permute-start.1 = (f32[8,256]{1,0:T(8,128)S(1)}, f32[8,256]{1,0:T(8,128)S(1)}, u32[]{:S(2)}, u32[]{:S(2)}) collective-permute-start(f32[8,256]{1,0:T(8,128)S(1)} %get-tuple-element.50.total_ref), channel_id=1, source_target_pairs={{0,2},{1,3},{2,0},{3,1},{4,6},{5,7},{6,4},{7,5},{8,10},{9,11},{10,... | collective-permute-start | bytes 24584 | tf_op jit(solution)/shard_map/ppermute | solution.py:596
  12.1 1.6 %collective-permute-done.1.other_ref = f32[8,256]{1,0:T(8,128)S(1)} collective-permute-done((f32[8,256]{1,0:T(8,128)S(1)}, f32[8,256]{1,0:T(8,128)S(1)}, u32[]{:S(2)}, u32[]{:S(2)}) %collective-permute-start.1) | collective-permute-done | bytes 8224 | tf_op jit(solution)/shard_map/ppermute | solution.py:596
  13.8 3.1 %collective-permute-start.2 = (f32[8,256]{1,0:T(8,128)S(1)}, f32[8,256]{1,0:T(8,128)S(1)}, u32[]{:S(2)}, u32[]{:S(2)}) collective-permute-start(f32[8,256]{1,0:T(8,128)S(1)} %get-tuple-element.61), channel_id=1, source_target_pairs={{0,4},{1,5},{2,6},{3,7},{4,0},{5,1},{6,2},{7,3},{8,12},{9,13},{10,... | collective-permute-start | bytes 24584 | tf_op jit(solution)/shard_map/ppermute | solution.py:596
  17.5 1.0 %collective-permute-done.2.refs_11_ = f32[8,256]{1,0:T(8,128)S(1)} collective-permute-done((f32[8,256]{1,0:T(8,128)S(1)}, f32[8,256]{1,0:T(8,128)S(1)}, u32[]{:S(2)}, u32[]{:S(2)}) %collective-permute-start.2) | collective-permute-done | bytes 8224 | tf_op jit(solution)/shard_map/ppermute | solution.py:596
  18.5 1.0 %lent.1 = (bf16[512,512]{1,0:T(8,128)(2,1)S(1)}, f32[8,40,512]{2,1,0:T(8,128)S(1)}, f32[8,40,512]{2,1,0:T(8,128)S(1)}, f32[8,24,512]{2,1,0:T(8,128)S(1)}, f32[8,24,512]{2,1,0:T(8,128)S(1)}) custom-call(f32[1,256]{1,0:T(1,128)S(1)} %get-tuple-element.42.refs_0_, f32[6,16,256]{2,1,0:T(8,128)S(1)} %get-tuple-element.43.refs_1_, ...), custom_call_target="tpu_custom_call" | custom-call | flops 536870912 | bytes 536870 | tf_op jit(solution)/shard_map/lent/pallas_call | solution.py:216
  21.8 1.9 %collective-permute-start.6 = (f32[8,40,512]{2,1,0:T(8,128)S(1)}, f32[8,40,512]{2,1,0:T(8,128)S(1)}, u32[]{:S(2)}, u32[]{:S(2)}) collective-permute-start(f32[8,40,512]{2,1,0:T(8,128)S(1)} %halve.9), channel_id=1, source_target_pairs={{0,16},{1,17},{2,18},{3,19},{4,20},{5,21},{6,22},{7,23},{8,9},{9,8... | collective-permute-start | bytes 1966088 | tf_op jit(solution)/shard_map/ppermute | solution.py:596
  24.2 1.2 %collective-permute-done.3.refs_1_ = f32[8,24,512]{2,1,0:T(8,128)S(1)} collective-permute-done((f32[8,24,512]{2,1,0:T(8,128)S(1)}, f32[8,24,512]{2,1,0:T(8,128)S(1)}, u32[]{:S(2)}, u32[]{:S(2)}) %collective-permute-start.3) | collective-permute-done | bytes 393248 | tf_op jit(solution)/shard_map/ppermute | solution.py:596
  25.4 1.6 %collective-permute-start.14 = (f32[8,24,512]{2,1,0:T(8,128)S(1)}, f32[8,24,512]{2,1,0:T(8,128)S(1)}, u32[]{:S(2)}, u32[]{:S(2)}) collective-permute-start(f32[8,24,512]{2,1,0:T(8,128)S(1)} %halve.8.after_ref), channel_id=1, source_target_pairs={{0,2},{1,3},{2,0},{3,1},{4,6},{5,7},{6,4},{7,5},{8,9},{9,8},{10,11... | collective-permute-start | bytes 1179656 | tf_op jit(solution)/shard_map/ppermute | solution.py:596
  27.1 3.1 %products.1 = (bf16[512,1024]{1,0:T(8,128)(2,1)}, bf16[512,1024]{1,0:T(8,128)(2,1)}, f32[8,128]{1,0:T(8,128)S(1)}) custom-call(bf16[512,1024]{1,0:T(8,128)(2,1)S(1)} %get-tuple-element.40.refs_12_.in_ref, bf16[512,1024]{1,0:T(8,128)(2,1)S(1)} %get-tuple-element.41.refs_13_.cot_ref, bf16[512,512]{1,0:T(8,128)(2,1)S(1)} %get-tuple-element.62.lent_ref, ...), custom_call_target="tpu_custom_call" | custom-call | flops 1073741824 | bytes 1073741 | tf_op jit(solution)/shard_map/products/pallas_call | solution.py:216
  30.2 2.2 %collective-permute-done.6.refs_2_ = f32[8,40,512]{2,1,0:T(8,128)S(1)} collective-permute-done((f32[8,40,512]{2,1,0:T(8,128)S(1)}, f32[8,40,512]{2,1,0:T(8,128)S(1)}, u32[]{:S(2)}, u32[]{:S(2)}) %collective-permute-start.6) | collective-permute-done | bytes 655392 | tf_op jit(solution)/shard_map/ppermute | solution.py:596
  32.5 1.9 %collective-permute-start.7 = (f32[4,40,512]{2,1,0:T(8,128)S(1)}, f32[4,40,512]{2,1,0:T(8,128)S(1)}, u32[]{:S(2)}, u32[]{:S(2)}) collective-permute-start(f32[4,40,512]{2,1,0:T(8,128)S(1)} %halve.10), channel_id=1, source_target_pairs={{0,1},{1,0},{2,3},{3,2},{4,5},{5,4},{6,7},{7,6},{8,10},{9,11},{10,... | collective-permute-start | bytes 983048 | tf_op jit(solution)/shard_map/ppermute | solution.py:596
  34.9 4.7 %collective-permute-done.7.refs_3_ = f32[4,40,512]{2,1,0:T(8,128)S(1)} collective-permute-done((f32[4,40,512]{2,1,0:T(8,128)S(1)}, f32[4,40,512]{2,1,0:T(8,128)S(1)}, u32[]{:S(2)}, u32[]{:S(2)}) %collective-permute-start.7) | collective-permute-done | bytes 327712 | tf_op jit(solution)/shard_map/ppermute | solution.py:596
  39.7 2.0 %collective-permute-start.8 = (f32[2,40,512]{2,1,0:T(8,128)S(1)}, f32[2,40,512]{2,1,0:T(8,128)S(1)}, u32[]{:S(2)}, u32[]{:S(2)}) collective-permute-start(f32[2,40,512]{2,1,0:T(8,128)S(1)} %halve.11), channel_id=1, source_target_pairs={{0,2},{1,3},{2,0},{3,1},{4,6},{5,7},{6,4},{7,5},{8,12},{9,13},{10,... | collective-permute-start | bytes 491528 | tf_op jit(solution)/shard_map/ppermute | solution.py:596
  41.7 3.0 %collective-permute-start.16 = (f32[2,24,512]{2,1,0:T(8,128)S(1)}, f32[2,24,512]{2,1,0:T(8,128)S(1)}, u32[]{:S(2)}, u32[]{:S(2)}) collective-permute-start(f32[2,24,512]{2,1,0:T(8,128)S(1)} %halve.14), channel_id=1, source_target_pairs={{0,4},{1,5},{2,6},{3,7},{4,0},{5,1},{6,2},{7,3},{8,12},{9,13},{10,... | collective-permute-start | bytes 294920 | tf_op jit(solution)/shard_map/ppermute | solution.py:596
  44.7 1.0 %collective-permute-done.8.refs_4_ = f32[2,40,512]{2,1,0:T(8,128)S(1)} collective-permute-done((f32[2,40,512]{2,1,0:T(8,128)S(1)}, f32[2,40,512]{2,1,0:T(8,128)S(1)}, u32[]{:S(2)}, u32[]{:S(2)}) %collective-permute-start.8) | collective-permute-done | bytes 163872 | tf_op jit(solution)/shard_map/ppermute | solution.py:596
  45.8 3.1 %collective-permute-start.9 = (f32[1,40,512]{2,1,0:T(8,128)S(1)}, f32[1,40,512]{2,1,0:T(8,128)S(1)}, u32[]{:S(2)}, u32[]{:S(2)}) collective-permute-start(f32[1,40,512]{2,1,0:T(8,128)S(1)} %halve.12), channel_id=1, source_target_pairs={{0,4},{1,5},{2,6},{3,7},{4,0},{5,1},{6,2},{7,3},{8,24},{9,25},{10,... | collective-permute-start | bytes 245768 | tf_op jit(solution)/shard_map/ppermute | solution.py:596
  49.7 1.6 %collective-permute-start.17 = (f32[2,24,512]{2,1,0:T(8,128)S(1)}, f32[2,24,512]{2,1,0:T(8,128)S(1)}, u32[]{:S(2)}, u32[]{:S(2)}) collective-permute-start(f32[2,24,512]{2,1,0:T(8,128)S(1)} %halve.15.refs_0_), channel_id=1, source_target_pairs={{0,16},{1,17},{2,18},{3,19},{4,20},{5,21},{6,22},{7,23},{8,24},{9,... | collective-permute-start | bytes 294920 | tf_op jit(solution)/shard_map/ppermute | solution.py:596
  51.4 2.0 %collective-permute-start.10 = (f32[1,40,512]{2,1,0:T(8,128)S(1)}, f32[1,40,512]{2,1,0:T(8,128)S(1)}, u32[]{:S(2)}, u32[]{:S(2)}) collective-permute-start(f32[1,40,512]{2,1,0:T(8,128)S(1)} %share.2.refs_0_), channel_id=1, source_target_pairs={{0,16},{1,17},{2,18},{3,19},{4,20},{5,21},{6,22},{7,23},{8,24},{9,... | collective-permute-start | bytes 245768 | tf_op jit(solution)/shard_map/ppermute | solution.py:596
  53.3 1.0 %collective-permute-done.17.refs_1_ = f32[2,24,512]{2,1,0:T(8,128)S(1)} collective-permute-done((f32[2,24,512]{2,1,0:T(8,128)S(1)}, f32[2,24,512]{2,1,0:T(8,128)S(1)}, u32[]{:S(2)}, u32[]{:S(2)}) %collective-permute-start.17) | collective-permute-done | bytes 98336 | tf_op jit(solution)/shard_map/ppermute | solution.py:596
  55.0 0.9 %collective-permute-done.10.refs_1_ = f32[1,40,512]{2,1,0:T(8,128)S(1)} collective-permute-done((f32[1,40,512]{2,1,0:T(8,128)S(1)}, f32[1,40,512]{2,1,0:T(8,128)S(1)}, u32[]{:S(2)}, u32[]{:S(2)}) %collective-permute-start.10) | collective-permute-done | bytes 81952 | tf_op jit(solution)/shard_map/ppermute | solution.py:596
  55.9 1.3 %collective-permute-done.12.refs_3_ = f32[1,40,512]{2,1,0:T(8,128)S(1)} collective-permute-done((f32[1,40,512]{2,1,0:T(8,128)S(1)}, f32[1,40,512]{2,1,0:T(8,128)S(1)}, u32[]{:S(2)}, u32[]{:S(2)}) %collective-permute-start.12) | collective-permute-done | bytes 81952 | tf_op jit(solution)/shard_map/ppermute | solution.py:596
  (34 shorter events, 6.6 us)
Async XLA Ops:
  5.3 4.7 %collective-permute-start = (f32[8,256]{1,0:T(8,128)S(1)}, f32[8,256]{1,0:T(8,128)S(1)}, u32[]{:S(2)}, u32[]{:S(2)}) collective-permute-start(f32[8,256]{1,0:T(8,128)S(1)} %get-tuple-element.48.total_ref), channel_id=1, source_target_pairs={{0,1},{1,0},{2,3},{3,2},{4,5},{5,4},{6,7},{7,6},{8,9},{9,8},{10,11... | collective-permute-start | bytes 24584 | tf_op jit(solution)/shard_map/ppermute | solution.py:596
  10.0 3.8 %collective-permute-start.1 = (f32[8,256]{1,0:T(8,128)S(1)}, f32[8,256]{1,0:T(8,128)S(1)}, u32[]{:S(2)}, u32[]{:S(2)}) collective-permute-start(f32[8,256]{1,0:T(8,128)S(1)} %get-tuple-element.50.total_ref), channel_id=1, source_target_pairs={{0,2},{1,3},{2,0},{3,1},{4,6},{5,7},{6,4},{7,5},{8,10},{9,11},{10,... | collective-permute-start | bytes 24584 | tf_op jit(solution)/shard_map/ppermute | solution.py:596
  13.8 4.7 %collective-permute-start.2 = (f32[8,256]{1,0:T(8,128)S(1)}, f32[8,256]{1,0:T(8,128)S(1)}, u32[]{:S(2)}, u32[]{:S(2)}) collective-permute-start(f32[8,256]{1,0:T(8,128)S(1)} %get-tuple-element.61), channel_id=1, source_target_pairs={{0,4},{1,5},{2,6},{3,7},{4,0},{5,1},{6,2},{7,3},{8,12},{9,13},{10,... | collective-permute-start | bytes 24584 | tf_op jit(solution)/shard_map/ppermute | solution.py:596
  19.5 2.2 %collective-permute-start.5 = (f32[8,40,512]{2,1,0:T(8,128)S(1)}, f32[8,40,512]{2,1,0:T(8,128)S(1)}, u32[]{:S(2)}, u32[]{:S(2)}) collective-permute-start(f32[8,40,512]{2,1,0:T(8,128)S(1)} %get-tuple-element.63.refs_14_), channel_id=1, source_target_pairs={{0,8},{1,9},{2,10},{3,11},{4,12},{5,13},{6,14},{7,15},{8,0},{9,1},... | collective-permute-start | bytes 1966088 | tf_op jit(solution)/shard_map/ppermute | solution.py:596
  19.6 10.6 %collective-permute-start.4 = (f32[8,40,512]{2,1,0:T(8,128)S(1)}, f32[8,40,512]{2,1,0:T(8,128)S(1)}, u32[]{:S(2)}, u32[]{:S(2)}) collective-permute-start(f32[8,40,512]{2,1,0:T(8,128)S(1)} %get-tuple-element.71), channel_id=1, source_target_pairs={{0,8},{1,9},{2,10},{3,11},{4,12},{5,13},{6,14},{7,15},{8,0},{9,1},... | collective-permute-start | bytes 1966088 | tf_op jit(solution)/shard_map/ppermute | solution.py:596
  21.7 5.3 %copy-start = (f32[1024]{0:T(1024)S(1)}, f32[1024]{0:T(1024)}, u32[]{:S(2)}) copy-start(f32[1024]{0:T(1024)} %param.14) | copy-start | bytes 12292
  21.8 10.7 %collective-permute-start.6 = (f32[8,40,512]{2,1,0:T(8,128)S(1)}, f32[8,40,512]{2,1,0:T(8,128)S(1)}, u32[]{:S(2)}, u32[]{:S(2)}) collective-permute-start(f32[8,40,512]{2,1,0:T(8,128)S(1)} %halve.9), channel_id=1, source_target_pairs={{0,16},{1,17},{2,18},{3,19},{4,20},{5,21},{6,22},{7,23},{8,9},{9,8... | collective-permute-start | bytes 1966088 | tf_op jit(solution)/shard_map/ppermute | solution.py:596
  23.6 1.7 %collective-permute-start.3 = (f32[8,24,512]{2,1,0:T(8,128)S(1)}, f32[8,24,512]{2,1,0:T(8,128)S(1)}, u32[]{:S(2)}, u32[]{:S(2)}) collective-permute-start(f32[8,24,512]{2,1,0:T(8,128)S(1)} %get-tuple-element.68), channel_id=1, source_target_pairs={{0,8},{1,9},{2,10},{3,11},{4,12},{5,13},{6,14},{7,15},{8,0},{9,1},... | collective-permute-start | bytes 1179656 | tf_op jit(solution)/shard_map/ppermute | solution.py:596
  23.6 10.7 %collective-permute-start.13 = (f32[8,24,512]{2,1,0:T(8,128)S(1)}, f32[8,24,512]{2,1,0:T(8,128)S(1)}, u32[]{:S(2)}, u32[]{:S(2)}) collective-permute-start(f32[8,24,512]{2,1,0:T(8,128)S(1)} %get-tuple-element.73), channel_id=1, source_target_pairs={{0,8},{1,9},{2,10},{3,11},{4,12},{5,13},{6,14},{7,15},{8,0},{9,1},... | collective-permute-start | bytes 1179656 | tf_op jit(solution)/shard_map/ppermute | solution.py:596
  25.4 9.0 %collective-permute-start.14 = (f32[8,24,512]{2,1,0:T(8,128)S(1)}, f32[8,24,512]{2,1,0:T(8,128)S(1)}, u32[]{:S(2)}, u32[]{:S(2)}) collective-permute-start(f32[8,24,512]{2,1,0:T(8,128)S(1)} %halve.8.after_ref), channel_id=1, source_target_pairs={{0,2},{1,3},{2,0},{3,1},{4,6},{5,7},{6,4},{7,5},{8,9},{9,8},{10,11... | collective-permute-start | bytes 1179656 | tf_op jit(solution)/shard_map/ppermute | solution.py:596
  32.5 7.1 %collective-permute-start.7 = (f32[4,40,512]{2,1,0:T(8,128)S(1)}, f32[4,40,512]{2,1,0:T(8,128)S(1)}, u32[]{:S(2)}, u32[]{:S(2)}) collective-permute-start(f32[4,40,512]{2,1,0:T(8,128)S(1)} %halve.10), channel_id=1, source_target_pairs={{0,1},{1,0},{2,3},{3,2},{4,5},{5,4},{6,7},{7,6},{8,10},{9,11},{10,... | collective-permute-start | bytes 983048 | tf_op jit(solution)/shard_map/ppermute | solution.py:596
  34.4 7.3 %collective-permute-start.15 = (f32[4,24,512]{2,1,0:T(8,128)S(1)}, f32[4,24,512]{2,1,0:T(8,128)S(1)}, u32[]{:S(2)}, u32[]{:S(2)}) collective-permute-start(f32[4,24,512]{2,1,0:T(8,128)S(1)} %halve.13), channel_id=1, source_target_pairs={{0,1},{1,0},{2,3},{3,2},{4,5},{5,4},{6,7},{7,6},{8,10},{9,11},{10,... | collective-permute-start | bytes 589832 | tf_op jit(solution)/shard_map/ppermute | solution.py:596
  39.7 6.1 %collective-permute-start.8 = (f32[2,40,512]{2,1,0:T(8,128)S(1)}, f32[2,40,512]{2,1,0:T(8,128)S(1)}, u32[]{:S(2)}, u32[]{:S(2)}) collective-permute-start(f32[2,40,512]{2,1,0:T(8,128)S(1)} %halve.11), channel_id=1, source_target_pairs={{0,2},{1,3},{2,0},{3,1},{4,6},{5,7},{6,4},{7,5},{8,12},{9,13},{10,... | collective-permute-start | bytes 491528 | tf_op jit(solution)/shard_map/ppermute | solution.py:596
  41.7 7.9 %collective-permute-start.16 = (f32[2,24,512]{2,1,0:T(8,128)S(1)}, f32[2,24,512]{2,1,0:T(8,128)S(1)}, u32[]{:S(2)}, u32[]{:S(2)}) collective-permute-start(f32[2,24,512]{2,1,0:T(8,128)S(1)} %halve.14), channel_id=1, source_target_pairs={{0,4},{1,5},{2,6},{3,7},{4,0},{5,1},{6,2},{7,3},{8,12},{9,13},{10,... | collective-permute-start | bytes 294920 | tf_op jit(solution)/shard_map/ppermute | solution.py:596
  45.8 5.5 %collective-permute-start.9 = (f32[1,40,512]{2,1,0:T(8,128)S(1)}, f32[1,40,512]{2,1,0:T(8,128)S(1)}, u32[]{:S(2)}, u32[]{:S(2)}) collective-permute-start(f32[1,40,512]{2,1,0:T(8,128)S(1)} %halve.12), channel_id=1, source_target_pairs={{0,4},{1,5},{2,6},{3,7},{4,0},{5,1},{6,2},{7,3},{8,24},{9,25},{10,... | collective-permute-start | bytes 245768 | tf_op jit(solution)/shard_map/ppermute | solution.py:596
  49.7 4.7 %collective-permute-start.17 = (f32[2,24,512]{2,1,0:T(8,128)S(1)}, f32[2,24,512]{2,1,0:T(8,128)S(1)}, u32[]{:S(2)}, u32[]{:S(2)}) collective-permute-start(f32[2,24,512]{2,1,0:T(8,128)S(1)} %halve.15.refs_0_), channel_id=1, source_target_pairs={{0,16},{1,17},{2,18},{3,19},{4,20},{5,21},{6,22},{7,23},{8,24},{9,... | collective-permute-start | bytes 294920 | tf_op jit(solution)/shard_map/ppermute | solution.py:596
  51.4 4.5 %collective-permute-start.10 = (f32[1,40,512]{2,1,0:T(8,128)S(1)}, f32[1,40,512]{2,1,0:T(8,128)S(1)}, u32[]{:S(2)}, u32[]{:S(2)}) collective-permute-start(f32[1,40,512]{2,1,0:T(8,128)S(1)} %share.2.refs_0_), channel_id=1, source_target_pairs={{0,16},{1,17},{2,18},{3,19},{4,20},{5,21},{6,22},{7,23},{8,24},{9,... | collective-permute-start | bytes 245768 | tf_op jit(solution)/shard_map/ppermute | solution.py:596
  54.4 1.5 %collective-permute-start.18 = (f32[2,24,512]{2,1,0:T(8,128)S(1)}, f32[2,24,512]{2,1,0:T(8,128)S(1)}, u32[]{:S(2)}, u32[]{:S(2)}) collective-permute-start(f32[2,24,512]{2,1,0:T(8,128)S(1)} %share.3.refs_4_), channel_id=1, source_target_pairs={{0,8},{1,9},{2,10},{3,11},{4,12},{5,13},{6,14},{7,15},{8,0},{9,1},... | collective-permute-start | bytes 294920 | tf_op jit(solution)/shard_map/ppermute | solution.py:596
  54.5 1.4 %collective-permute-start.11 = (f32[1,40,512]{2,1,0:T(8,128)S(1)}, f32[1,40,512]{2,1,0:T(8,128)S(1)}, u32[]{:S(2)}, u32[]{:S(2)}) collective-permute-start(f32[1,40,512]{2,1,0:T(8,128)S(1)} %share.2.refs_0_), channel_id=1, source_target_pairs={{0,8},{1,9},{2,10},{3,11},{4,12},{5,13},{6,14},{7,15},{8,0},{9,1},... | collective-permute-start | bytes 245768 | tf_op jit(solution)/shard_map/ppermute | solution.py:596
  55.9 1.3 %collective-permute-start.12 = (f32[1,40,512]{2,1,0:T(8,128)S(1)}, f32[1,40,512]{2,1,0:T(8,128)S(1)}, u32[]{:S(2)}, u32[]{:S(2)}) collective-permute-start(f32[1,40,512]{2,1,0:T(8,128)S(1)} %collective-permute-done.10.refs_1_), channel_id=1, source_target_pairs={{0,8},{1,9},{2,10},{3,11},{4,12},{5,13},{6,14},{7,15},{8,0},{9,1},... | collective-permute-start | bytes 245768 | tf_op jit(solution)/shard_map/ppermute | solution.py:596

commit v6 on v5

--- a/solution.py
+++ b/solution.py
@@ -428,8 +428,9 @@
     shapes = [held((rows, 2 * states), jnp.bfloat16)]
     if own:
         shapes.append(held(blocks))
-    for _, _, _, first, past in parts:
-        shapes.append(held((blocks[0] // 2, past - first, 2 * states)))
+    for _, steps, _, first, past in parts:
+        count = blocks[0] if steps[0] is None else blocks[0] // 2
+        shapes.append(held((count, past - first, 2 * states)))
     return call(
         functools.partial(side_kernel, own, bit, parts, len(after)),
         "kept" if own else "lent",
@@ -641,7 +642,8 @@
                 {"rows": (first, past), "orders": orders, "settled": ([], []), "halvings": halvings}
             )
             steps = [order[0] for order in orders]
-            parts += [(layout, steps, far, first, past) for far in (True, False)]
+            pieces = [(steps, True), (steps, False)] if first == 0 else [((None, None), False)]
+            parts += [(layout, which, far, first, past) for which, far in pieces]
             first = past
 
     common = (decay, chunk_totals, planes, outside, other, flat_in, flat_cot)
@@ -684,7 +686,10 @@
                 continue
             if place == 0:
                 left = tuple(less([step]) for step in steps)
-                far, near = borrowed[2 * number : 2 * number + 2]
+                if number == 0:
+                    far, near = borrowed[:2]
+                else:
+                    far, near, left = borrowed[number + 1], borrowed[number + 1], (layout, layout)
                 stream["sources"] = [(kept, (layout, layout)), (near, left)]
                 away = add(stream, [stream["sources"][0], (far, left)], steps, later=before)
             else:

time: 58.2 us -> 58.2 us (level)
  starting transfers between devices: 27.5 us -> 26.8 us
  waiting for transfers between devices: 18.2 us -> 18.8 us
    ppermute x19 -> x18, waiting for transfers between devices: 18.2 us -> 18.8 us  [swap(): return lax.ppermute(array, ('dp', 'context'), pairs)]
    ppermute x19 -> x18, starting transfers between devices: 27.5 us -> 26.8 us  [swap(): return lax.ppermute(array, ('dp', 'context'), pairs)]
  transfers between devices with their start and end apart: 19 -> 18, of which waited for: 14 -> 13; matrix products, arithmetic and copies ran while one was open for 0% -> 0% of each run, Pallas kernels for 9% -> 9%
where the time goes in v6:
time: 58.2 us; the launch traced here: 58 us
  starting transfers between devices  26.8 us (46%)
  waiting for transfers between devices  18.8 us (32%)
  Pallas kernels  11.6 us (20%)
  between operations  0.75 us (1%)
    ppermute x18, starting transfers between devices, swap(): return lax.ppermute(array, ('dp', 'context'), pairs)  26.8 us
    ppermute x18, waiting for transfers between devices, swap(): return lax.ppermute(array, ('dp', 'context'), pairs)  18.8 us
    pallas_call x18, Pallas kernels, call(): pl.pallas_call(kernel, out_shape=out_shape, in_specs=inputs or [vmem] * l...  11.6 us
  transfers between devices with their start and end apart: 18, of which 13 were waited for; matrix products, arithmetic and copies ran while one was open for 0% of the time, Pallas kernels for 9%

profile of v6, /device:TPU:0, one launch (start us, length us, event | category | flops | bytes accessed | tf_op | source)
XLA Modules:
  0.0 58.0 jit_solution(2893432019983635542)
XLA Ops:
  0.6 4.6 %local_scan.1 = (f32[512,256]{1,0:T(8,128)S(1)}, f32[512,256]{1,0:T(8,128)S(1)}, f32[512,512]{1,0:T(8,128)S(1)}, f32[512,512]{1,0:T(8,128)S(1)}, f32[6,16,256]{2...) custom-call(f32[1,512]{1,0:T(1,128)} %step_hbm.1, ...), custom_call_target="tpu_custom_call" | custom-call | flops 1073741824 | bytes 1073741 | tf_op jit(solution)/shard_map/local_scan/pallas_call | solution.py:216
  5.3 3.0 %collective-permute-start = (f32[8,256]{1,0:T(8,128)S(1)}, f32[8,256]{1,0:T(8,128)S(1)}, u32[]{:S(2)}, u32[]{:S(2)}) collective-permute-start(f32[8,256]{1,0:T(8,128)S(1)} %get-tuple-element.47.total_ref), channel_id=1, source_target_pairs={{0,1},{1,0},{2,3},{3,2},{4,5},{5,4},{6,7},{7,6},{8,9},{9,8},{10,11... | collective-permute-start | bytes 24584 | tf_op jit(solution)/shard_map/ppermute | solution.py:597
  8.3 1.6 %collective-permute-done.other_ref = f32[8,256]{1,0:T(8,128)S(1)} collective-permute-done((f32[8,256]{1,0:T(8,128)S(1)}, f32[8,256]{1,0:T(8,128)S(1)}, u32[]{:S(2)}, u32[]{:S(2)}) %collective-permute-start) | collective-permute-done | bytes 8224 | tf_op jit(solution)/shard_map/ppermute | solution.py:597
  10.0 2.1 %collective-permute-start.1 = (f32[8,256]{1,0:T(8,128)S(1)}, f32[8,256]{1,0:T(8,128)S(1)}, u32[]{:S(2)}, u32[]{:S(2)}) collective-permute-start(f32[8,256]{1,0:T(8,128)S(1)} %get-tuple-element.49.total_ref), channel_id=1, source_target_pairs={{0,2},{1,3},{2,0},{3,1},{4,6},{5,7},{6,4},{7,5},{8,10},{9,11},{10,... | collective-permute-start | bytes 24584 | tf_op jit(solution)/shard_map/ppermute | solution.py:597
  12.1 1.6 %collective-permute-done.1.other_ref = f32[8,256]{1,0:T(8,128)S(1)} collective-permute-done((f32[8,256]{1,0:T(8,128)S(1)}, f32[8,256]{1,0:T(8,128)S(1)}, u32[]{:S(2)}, u32[]{:S(2)}) %collective-permute-start.1) | collective-permute-done | bytes 8224 | tf_op jit(solution)/shard_map/ppermute | solution.py:597
  13.8 3.1 %collective-permute-start.2 = (f32[8,256]{1,0:T(8,128)S(1)}, f32[8,256]{1,0:T(8,128)S(1)}, u32[]{:S(2)}, u32[]{:S(2)}) collective-permute-start(f32[8,256]{1,0:T(8,128)S(1)} %get-tuple-element.60), channel_id=1, source_target_pairs={{0,4},{1,5},{2,6},{3,7},{4,0},{5,1},{6,2},{7,3},{8,12},{9,13},{10,... | collective-permute-start | bytes 24584 | tf_op jit(solution)/shard_map/ppermute | solution.py:597
  17.5 1.0 %collective-permute-done.2.refs_11_ = f32[8,256]{1,0:T(8,128)S(1)} collective-permute-done((f32[8,256]{1,0:T(8,128)S(1)}, f32[8,256]{1,0:T(8,128)S(1)}, u32[]{:S(2)}, u32[]{:S(2)}) %collective-permute-start.2) | collective-permute-done | bytes 8224 | tf_op jit(solution)/shard_map/ppermute | solution.py:597
  18.5 1.0 %lent.1 = (bf16[512,512]{1,0:T(8,128)(2,1)S(1)}, f32[8,40,512]{2,1,0:T(8,128)S(1)}, f32[8,40,512]{2,1,0:T(8,128)S(1)}, f32[16,24,512]{2,1,0:T(8,128)S(1)}) custom-call(f32[1,256]{1,0:T(1,128)S(1)} %get-tuple-element.41.refs_0_, f32[6,16,256]{2,1,0:T(8,128)S(1)} %get-tuple-element.42.refs_1_, f32[512,256]{1,0:T(8,128)S(1)} %get-tuple-element.52.refs_2_, ...), custom_call_target="tpu_custom_call" | custom-call | flops 536870912 | bytes 536870 | tf_op jit(solution)/shard_map/lent/pallas_call | solution.py:216
  20.2 0.9 %kept.1 = (bf16[512,512]{1,0:T(8,128)(2,1)S(1)}, f32[16,64,512]{2,1,0:T(8,128)S(1)}) custom-call(f32[1,256]{1,0:T(1,128)S(1)} %get-tuple-element.41.refs_0_, f32[6,16,256]{2,1,0:T(8,128)S(1)} %get-tuple-element.42.refs_1_, f32[512,256]{1,0:T(8,128)S(1)} %get-tuple-element.52.refs_2_, f32[512,256]{1,0:T(8,128)S(1)} %get-tuple-element.53.refs_3_, ...), custom_call_target="tpu_custom_call" | custom-call | flops 536870912 | bytes 536870 | tf_op jit(solution)/shard_map/kept/pallas_call | solution.py:216
  21.7 1.9 %collective-permute-start.6 = (f32[8,40,512]{2,1,0:T(8,128)S(1)}, f32[8,40,512]{2,1,0:T(8,128)S(1)}, u32[]{:S(2)}, u32[]{:S(2)}) collective-permute-start(f32[8,40,512]{2,1,0:T(8,128)S(1)} %halve.9), channel_id=1, source_target_pairs={{0,16},{1,17},{2,18},{3,19},{4,20},{5,21},{6,22},{7,23},{8,9},{9,8... | collective-permute-start | bytes 1966088 | tf_op jit(solution)/shard_map/ppermute | solution.py:597
  23.7 1.6 %collective-permute-start.13 = (f32[8,24,512]{2,1,0:T(8,128)S(1)}, f32[8,24,512]{2,1,0:T(8,128)S(1)}, u32[]{:S(2)}, u32[]{:S(2)}) collective-permute-start(f32[8,24,512]{2,1,0:T(8,128)S(1)} %halve.8.after_ref), channel_id=1, source_target_pairs={{0,2},{1,3},{2,0},{3,1},{4,6},{5,7},{6,4},{7,5},{8,9},{9,8},{10,11... | collective-permute-start | bytes 1179656 | tf_op jit(solution)/shard_map/ppermute | solution.py:597
  25.3 3.1 %products.1 = (bf16[512,1024]{1,0:T(8,128)(2,1)}, bf16[512,1024]{1,0:T(8,128)(2,1)}, f32[8,128]{1,0:T(8,128)S(1)}) custom-call(bf16[512,1024]{1,0:T(8,128)(2,1)S(1)} %get-tuple-element.39.refs_12_.in_ref, bf16[512,1024]{1,0:T(8,128)(2,1)S(1)} %get-tuple-element.40.refs_13_.cot_ref, bf16[512,512]{1,0:T(8,128)(2,1)S(1)} %get-tuple-element.61.lent_ref, ...), custom_call_target="tpu_custom_call" | custom-call | flops 1073741824 | bytes 1073741 | tf_op jit(solution)/shard_map/products/pallas_call | solution.py:216
  28.5 3.9 %collective-permute-done.6.refs_2_ = f32[8,40,512]{2,1,0:T(8,128)S(1)} collective-permute-done((f32[8,40,512]{2,1,0:T(8,128)S(1)}, f32[8,40,512]{2,1,0:T(8,128)S(1)}, u32[]{:S(2)}, u32[]{:S(2)}) %collective-permute-start.6) | collective-permute-done | bytes 655392 | tf_op jit(solution)/shard_map/ppermute | solution.py:597
  32.5 1.9 %collective-permute-start.7 = (f32[4,40,512]{2,1,0:T(8,128)S(1)}, f32[4,40,512]{2,1,0:T(8,128)S(1)}, u32[]{:S(2)}, u32[]{:S(2)}) collective-permute-start(f32[4,40,512]{2,1,0:T(8,128)S(1)} %halve.10), channel_id=1, source_target_pairs={{0,1},{1,0},{2,3},{3,2},{4,5},{5,4},{6,7},{7,6},{8,10},{9,11},{10,... | collective-permute-start | bytes 983048 | tf_op jit(solution)/shard_map/ppermute | solution.py:597
  34.7 4.9 %collective-permute-done.7.refs_3_ = f32[4,40,512]{2,1,0:T(8,128)S(1)} collective-permute-done((f32[4,40,512]{2,1,0:T(8,128)S(1)}, f32[4,40,512]{2,1,0:T(8,128)S(1)}, u32[]{:S(2)}, u32[]{:S(2)}) %collective-permute-start.7) | collective-permute-done | bytes 327712 | tf_op jit(solution)/shard_map/ppermute | solution.py:597
  39.7 2.0 %collective-permute-start.8 = (f32[2,40,512]{2,1,0:T(8,128)S(1)}, f32[2,40,512]{2,1,0:T(8,128)S(1)}, u32[]{:S(2)}, u32[]{:S(2)}) collective-permute-start(f32[2,40,512]{2,1,0:T(8,128)S(1)} %halve.11), channel_id=1, source_target_pairs={{0,2},{1,3},{2,0},{3,1},{4,6},{5,7},{6,4},{7,5},{8,12},{9,13},{10,... | collective-permute-start | bytes 491528 | tf_op jit(solution)/shard_map/ppermute | solution.py:597
  41.7 3.0 %collective-permute-start.15 = (f32[2,24,512]{2,1,0:T(8,128)S(1)}, f32[2,24,512]{2,1,0:T(8,128)S(1)}, u32[]{:S(2)}, u32[]{:S(2)}) collective-permute-start(f32[2,24,512]{2,1,0:T(8,128)S(1)} %halve.14), channel_id=1, source_target_pairs={{0,4},{1,5},{2,6},{3,7},{4,0},{5,1},{6,2},{7,3},{8,12},{9,13},{10,... | collective-permute-start | bytes 294920 | tf_op jit(solution)/shard_map/ppermute | solution.py:597
  44.7 1.0 %collective-permute-done.8.refs_4_ = f32[2,40,512]{2,1,0:T(8,128)S(1)} collective-permute-done((f32[2,40,512]{2,1,0:T(8,128)S(1)}, f32[2,40,512]{2,1,0:T(8,128)S(1)}, u32[]{:S(2)}, u32[]{:S(2)}) %collective-permute-start.8) | collective-permute-done | bytes 163872 | tf_op jit(solution)/shard_map/ppermute | solution.py:597
  45.8 3.1 %collective-permute-start.9 = (f32[1,40,512]{2,1,0:T(8,128)S(1)}, f32[1,40,512]{2,1,0:T(8,128)S(1)}, u32[]{:S(2)}, u32[]{:S(2)}) collective-permute-start(f32[1,40,512]{2,1,0:T(8,128)S(1)} %halve.12), channel_id=1, source_target_pairs={{0,4},{1,5},{2,6},{3,7},{4,0},{5,1},{6,2},{7,3},{8,24},{9,25},{10,... | collective-permute-start | bytes 245768 | tf_op jit(solution)/shard_map/ppermute | solution.py:597
  49.7 1.6 %collective-permute-start.16 = (f32[2,24,512]{2,1,0:T(8,128)S(1)}, f32[2,24,512]{2,1,0:T(8,128)S(1)}, u32[]{:S(2)}, u32[]{:S(2)}) collective-permute-start(f32[2,24,512]{2,1,0:T(8,128)S(1)} %halve.15.refs_0_), channel_id=1, source_target_pairs={{0,16},{1,17},{2,18},{3,19},{4,20},{5,21},{6,22},{7,23},{8,24},{9,... | collective-permute-start | bytes 294920 | tf_op jit(solution)/shard_map/ppermute | solution.py:597
  51.4 2.0 %collective-permute-start.10 = (f32[1,40,512]{2,1,0:T(8,128)S(1)}, f32[1,40,512]{2,1,0:T(8,128)S(1)}, u32[]{:S(2)}, u32[]{:S(2)}) collective-permute-start(f32[1,40,512]{2,1,0:T(8,128)S(1)} %share.2.refs_0_), channel_id=1, source_target_pairs={{0,16},{1,17},{2,18},{3,19},{4,20},{5,21},{6,22},{7,23},{8,24},{9,... | collective-permute-start | bytes 245768 | tf_op jit(solution)/shard_map/ppermute | solution.py:597
  53.3 1.0 %collective-permute-done.16.refs_1_ = f32[2,24,512]{2,1,0:T(8,128)S(1)} collective-permute-done((f32[2,24,512]{2,1,0:T(8,128)S(1)}, f32[2,24,512]{2,1,0:T(8,128)S(1)}, u32[]{:S(2)}, u32[]{:S(2)}) %collective-permute-start.16) | collective-permute-done | bytes 98336 | tf_op jit(solution)/shard_map/ppermute | solution.py:597
  55.0 0.9 %collective-permute-done.10.refs_1_ = f32[1,40,512]{2,1,0:T(8,128)S(1)} collective-permute-done((f32[1,40,512]{2,1,0:T(8,128)S(1)}, f32[1,40,512]{2,1,0:T(8,128)S(1)}, u32[]{:S(2)}, u32[]{:S(2)}) %collective-permute-start.10) | collective-permute-done | bytes 81952 | tf_op jit(solution)/shard_map/ppermute | solution.py:597
  55.9 1.3 %collective-permute-done.12.refs_3_ = f32[1,40,512]{2,1,0:T(8,128)S(1)} collective-permute-done((f32[1,40,512]{2,1,0:T(8,128)S(1)}, f32[1,40,512]{2,1,0:T(8,128)S(1)}, u32[]{:S(2)}, u32[]{:S(2)}) %collective-permute-start.12) | collective-permute-done | bytes 81952 | tf_op jit(solution)/shard_map/ppermute | solution.py:597
  (32 shorter events, 4.9 us)
Async XLA Ops:
  5.3 4.7 %collective-permute-start = (f32[8,256]{1,0:T(8,128)S(1)}, f32[8,256]{1,0:T(8,128)S(1)}, u32[]{:S(2)}, u32[]{:S(2)}) collective-permute-start(f32[8,256]{1,0:T(8,128)S(1)} %get-tuple-element.47.total_ref), channel_id=1, source_target_pairs={{0,1},{1,0},{2,3},{3,2},{4,5},{5,4},{6,7},{7,6},{8,9},{9,8},{10,11... | collective-permute-start | bytes 24584 | tf_op jit(solution)/shard_map/ppermute | solution.py:597
  10.0 3.8 %collective-permute-start.1 = (f32[8,256]{1,0:T(8,128)S(1)}, f32[8,256]{1,0:T(8,128)S(1)}, u32[]{:S(2)}, u32[]{:S(2)}) collective-permute-start(f32[8,256]{1,0:T(8,128)S(1)} %get-tuple-element.49.total_ref), channel_id=1, source_target_pairs={{0,2},{1,3},{2,0},{3,1},{4,6},{5,7},{6,4},{7,5},{8,10},{9,11},{10,... | collective-permute-start | bytes 24584 | tf_op jit(solution)/shard_map/ppermute | solution.py:597
  13.8 4.7 %collective-permute-start.2 = (f32[8,256]{1,0:T(8,128)S(1)}, f32[8,256]{1,0:T(8,128)S(1)}, u32[]{:S(2)}, u32[]{:S(2)}) collective-permute-start(f32[8,256]{1,0:T(8,128)S(1)} %get-tuple-element.60), channel_id=1, source_target_pairs={{0,4},{1,5},{2,6},{3,7},{4,0},{5,1},{6,2},{7,3},{8,12},{9,13},{10,... | collective-permute-start | bytes 24584 | tf_op jit(solution)/shard_map/ppermute | solution.py:597
  19.5 2.2 %collective-permute-start.5 = (f32[8,40,512]{2,1,0:T(8,128)S(1)}, f32[8,40,512]{2,1,0:T(8,128)S(1)}, u32[]{:S(2)}, u32[]{:S(2)}) collective-permute-start(f32[8,40,512]{2,1,0:T(8,128)S(1)} %get-tuple-element.62.refs_14_), channel_id=1, source_target_pairs={{0,8},{1,9},{2,10},{3,11},{4,12},{5,13},{6,14},{7,15},{8,0},{9,1},... | collective-permute-start | bytes 1966088 | tf_op jit(solution)/shard_map/ppermute | solution.py:597
  19.6 4.1 %collective-permute-start.3 = (f32[16,24,512]{2,1,0:T(8,128)S(1)}, f32[16,24,512]{2,1,0:T(8,128)S(1)}, u32[]{:S(2)}, u32[]{:S(2)}) collective-permute-start(f32[16,24,512]{2,1,0:T(8,128)S(1)} %get-tuple-element.67), channel_id=1, source_target_pairs={{0,8},{1,9},{2,10},{3,11},{4,12},{5,13},{6,14},{7,15},{8,0},{9,1},... | collective-permute-start | bytes 2359304 | tf_op jit(solution)/shard_map/ppermute | solution.py:597
  20.1 8.4 %collective-permute-start.4 = (f32[8,40,512]{2,1,0:T(8,128)S(1)}, f32[8,40,512]{2,1,0:T(8,128)S(1)}, u32[]{:S(2)}, u32[]{:S(2)}) collective-permute-start(f32[8,40,512]{2,1,0:T(8,128)S(1)} %get-tuple-element.70), channel_id=1, source_target_pairs={{0,8},{1,9},{2,10},{3,11},{4,12},{5,13},{6,14},{7,15},{8,0},{9,1},... | collective-permute-start | bytes 1966088 | tf_op jit(solution)/shard_map/ppermute | solution.py:597
  21.7 3.6 %copy-start = (f32[1024]{0:T(1024)S(1)}, f32[1024]{0:T(1024)}, u32[]{:S(2)}) copy-start(f32[1024]{0:T(1024)} %param.14) | copy-start | bytes 12292
  21.7 10.7 %collective-permute-start.6 = (f32[8,40,512]{2,1,0:T(8,128)S(1)}, f32[8,40,512]{2,1,0:T(8,128)S(1)}, u32[]{:S(2)}, u32[]{:S(2)}) collective-permute-start(f32[8,40,512]{2,1,0:T(8,128)S(1)} %halve.9), channel_id=1, source_target_pairs={{0,16},{1,17},{2,18},{3,19},{4,20},{5,21},{6,22},{7,23},{8,9},{9,8... | collective-permute-start | bytes 1966088 | tf_op jit(solution)/shard_map/ppermute | solution.py:597
  23.7 10.7 %collective-permute-start.13 = (f32[8,24,512]{2,1,0:T(8,128)S(1)}, f32[8,24,512]{2,1,0:T(8,128)S(1)}, u32[]{:S(2)}, u32[]{:S(2)}) collective-permute-start(f32[8,24,512]{2,1,0:T(8,128)S(1)} %halve.8.after_ref), channel_id=1, source_target_pairs={{0,2},{1,3},{2,0},{3,1},{4,6},{5,7},{6,4},{7,5},{8,9},{9,8},{10,11... | collective-permute-start | bytes 1179656 | tf_op jit(solution)/shard_map/ppermute | solution.py:597
  32.5 7.1 %collective-permute-start.7 = (f32[4,40,512]{2,1,0:T(8,128)S(1)}, f32[4,40,512]{2,1,0:T(8,128)S(1)}, u32[]{:S(2)}, u32[]{:S(2)}) collective-permute-start(f32[4,40,512]{2,1,0:T(8,128)S(1)} %halve.10), channel_id=1, source_target_pairs={{0,1},{1,0},{2,3},{3,2},{4,5},{5,4},{6,7},{7,6},{8,10},{9,11},{10,... | collective-permute-start | bytes 983048 | tf_op jit(solution)/shard_map/ppermute | solution.py:597
  34.4 7.3 %collective-permute-start.14 = (f32[4,24,512]{2,1,0:T(8,128)S(1)}, f32[4,24,512]{2,1,0:T(8,128)S(1)}, u32[]{:S(2)}, u32[]{:S(2)}) collective-permute-start(f32[4,24,512]{2,1,0:T(8,128)S(1)} %halve.13), channel_id=1, source_target_pairs={{0,1},{1,0},{2,3},{3,2},{4,5},{5,4},{6,7},{7,6},{8,10},{9,11},{10,... | collective-permute-start | bytes 589832 | tf_op jit(solution)/shard_map/ppermute | solution.py:597
  39.7 6.1 %collective-permute-start.8 = (f32[2,40,512]{2,1,0:T(8,128)S(1)}, f32[2,40,512]{2,1,0:T(8,128)S(1)}, u32[]{:S(2)}, u32[]{:S(2)}) collective-permute-start(f32[2,40,512]{2,1,0:T(8,128)S(1)} %halve.11), channel_id=1, source_target_pairs={{0,2},{1,3},{2,0},{3,1},{4,6},{5,7},{6,4},{7,5},{8,12},{9,13},{10,... | collective-permute-start | bytes 491528 | tf_op jit(solution)/shard_map/ppermute | solution.py:597
  41.7 7.9 %collective-permute-start.15 = (f32[2,24,512]{2,1,0:T(8,128)S(1)}, f32[2,24,512]{2,1,0:T(8,128)S(1)}, u32[]{:S(2)}, u32[]{:S(2)}) collective-permute-start(f32[2,24,512]{2,1,0:T(8,128)S(1)} %halve.14), channel_id=1, source_target_pairs={{0,4},{1,5},{2,6},{3,7},{4,0},{5,1},{6,2},{7,3},{8,12},{9,13},{10,... | collective-permute-start | bytes 294920 | tf_op jit(solution)/shard_map/ppermute | solution.py:597
  45.8 5.6 %collective-permute-start.9 = (f32[1,40,512]{2,1,0:T(8,128)S(1)}, f32[1,40,512]{2,1,0:T(8,128)S(1)}, u32[]{:S(2)}, u32[]{:S(2)}) collective-permute-start(f32[1,40,512]{2,1,0:T(8,128)S(1)} %halve.12), channel_id=1, source_target_pairs={{0,4},{1,5},{2,6},{3,7},{4,0},{5,1},{6,2},{7,3},{8,24},{9,25},{10,... | collective-permute-start | bytes 245768 | tf_op jit(solution)/shard_map/ppermute | solution.py:597
  49.7 4.7 %collective-permute-start.16 = (f32[2,24,512]{2,1,0:T(8,128)S(1)}, f32[2,24,512]{2,1,0:T(8,128)S(1)}, u32[]{:S(2)}, u32[]{:S(2)}) collective-permute-start(f32[2,24,512]{2,1,0:T(8,128)S(1)} %halve.15.refs_0_), channel_id=1, source_target_pairs={{0,16},{1,17},{2,18},{3,19},{4,20},{5,21},{6,22},{7,23},{8,24},{9,... | collective-permute-start | bytes 294920 | tf_op jit(solution)/shard_map/ppermute | solution.py:597
  51.4 4.5 %collective-permute-start.10 = (f32[1,40,512]{2,1,0:T(8,128)S(1)}, f32[1,40,512]{2,1,0:T(8,128)S(1)}, u32[]{:S(2)}, u32[]{:S(2)}) collective-permute-start(f32[1,40,512]{2,1,0:T(8,128)S(1)} %share.2.refs_0_), channel_id=1, source_target_pairs={{0,16},{1,17},{2,18},{3,19},{4,20},{5,21},{6,22},{7,23},{8,24},{9,... | collective-permute-start | bytes 245768 | tf_op jit(solution)/shard_map/ppermute | solution.py:597
  54.4 1.5 %collective-permute-start.17 = (f32[2,24,512]{2,1,0:T(8,128)S(1)}, f32[2,24,512]{2,1,0:T(8,128)S(1)}, u32[]{:S(2)}, u32[]{:S(2)}) collective-permute-start(f32[2,24,512]{2,1,0:T(8,128)S(1)} %share.3.refs_4_), channel_id=1, source_target_pairs={{0,8},{1,9},{2,10},{3,11},{4,12},{5,13},{6,14},{7,15},{8,0},{9,1},... | collective-permute-start | bytes 294920 | tf_op jit(solution)/shard_map/ppermute | solution.py:597
  54.5 1.4 %collective-permute-start.11 = (f32[1,40,512]{2,1,0:T(8,128)S(1)}, f32[1,40,512]{2,1,0:T(8,128)S(1)}, u32[]{:S(2)}, u32[]{:S(2)}) collective-permute-start(f32[1,40,512]{2,1,0:T(8,128)S(1)} %share.2.refs_0_), channel_id=1, source_target_pairs={{0,8},{1,9},{2,10},{3,11},{4,12},{5,13},{6,14},{7,15},{8,0},{9,1},... | collective-permute-start | bytes 245768 | tf_op jit(solution)/shard_map/ppermute | solution.py:597
  55.9 1.3 %collective-permute-start.12 = (f32[1,40,512]{2,1,0:T(8,128)S(1)}, f32[1,40,512]{2,1,0:T(8,128)S(1)}, u32[]{:S(2)}, u32[]{:S(2)}) collective-permute-start(f32[1,40,512]{2,1,0:T(8,128)S(1)} %collective-permute-done.10.refs_1_), channel_id=1, source_target_pairs={{0,8},{1,9},{2,10},{3,11},{4,12},{5,13},{6,14},{7,15},{8,0},{9,1},... | collective-permute-start | bytes 245768 | tf_op jit(solution)/shard_map/ppermute | solution.py:597
